TPU v7x, 128 devices: a whole 4x4x4 slice. The times are simulated.
128 devices in a mesh: cube: 128 (over y, z, x, core).
Axes of the slice: x: 4, y: 4, z: 4, core: 2. Of those that a mesh axis runs over, the one named last changes fastest.
Arguments:
- front_leaf: bfloat16 [2048, 16384], P(None, 'cube'), may hold values from -6 to 6
- front_lower: bfloat16 [4096, 16384], P(None, 'cube'), may hold values from -6 to 6
- front_upper: bfloat16 [8192, 16384], P(None, 'cube'), may hold values from -6 to 6
- front_root: bfloat16 [16384, 16384], P(None, 'cube'), may hold values from -6 to 6
- inv_leaf: bfloat16 [16384, 128], P('cube'), as said below
- inv_lower: bfloat16 [16384, 128], P('cube'), as said below
- inv_upper: bfloat16 [16384, 128], P('cube'), as said below
- inv_root: bfloat16 [16384, 128], P('cube'), as said below
- pivots_leaf: int32 [8, 2], replicated, may hold values from 0 to 15, as said below
- pivots_lower: int32 [4, 2], replicated, may hold values from 0 to 31, as said below
- pivots_upper: int32 [2, 2], replicated, may hold values from 0 to 63, as said below
- pivots_root: int32 [1, 2], replicated, may hold values from 0 to 127, as said below
- child_sides: int32 [3, 128], replicated, may hold values from 0 to 1
Outputs:
- factored_leaf: float32 [2048, 16384], P(None, 'cube')
- factored_lower: float32 [4096, 16384], P(None, 'cube')
- factored_upper: float32 [8192, 16384], P(None, 'cube')
- factored_root: float32 [16384, 16384], P(None, 'cube')
Inputs may be any that keep to these rules, and one draw needn't show every extreme that they name: `pivots_leaf`: each row holds 2 different block positions of its front. `pivots_lower`: each row holds 2 different block positions of its front. `pivots_upper`: each row holds 2 different block positions of its front. `pivots_root`: the row holds 2 different block positions of the root front. `inv_leaf`: each 128 x 128 block has positive diagonal entries from 1/64 to 1/16 and small entries of either sign elsewhere. `inv_lower`: as for inv_leaf. `inv_upper`: as for inv_leaf. `inv_root`: as for inv_leaf.
All inputs are finite; a program needn't handle non-finite values.
Results may differ from a plain program's by a relative error of at most 0.025.
Values may be sent and summed in bfloat16 or wider, within the bound.
No kernel may reach another device: no remote copies, remote signals or barrier semaphores. Data moves between devices by JAX's collectives and lax.ppermute only.
A program may use at most 128 MiB of HBM per device.

v0:
```python
import jax
import jax.numpy as jnp
from jax import lax
from jax.sharding import PartitionSpec as P


def partner(array, axis, bit):
    return lax.ppermute(array, axis, [(i, i ^ 1 << bit) for i in range(lax.axis_size(axis))])


def scale_panel(column, inverse):
    return jnp.dot(column, inverse.astype(jnp.float32), precision=lax.Precision.HIGHEST).astype(
        jnp.bfloat16
    )


def empty_panel(column, inverse):
    return jnp.zeros(column.shape, jnp.bfloat16)


def spread_panel(factor, local_blk, pivot_blk, cube_bits, block_cols):
    pieces = factor.reshape(-1, block_cols, block_cols)
    relative = jnp.bitwise_xor(local_blk, pivot_blk)
    for bit_num in range(cube_bits - 1, -1, -1):
        half_size = pieces.shape[0] // 2
        own_bit = jnp.bitwise_and(jnp.right_shift(local_blk, bit_num), 1) == 1
        retained = jnp.where(own_bit, pieces[half_size:], pieces[:half_size])
        outgoing = jnp.where(own_bit, pieces[:half_size], pieces[half_size:])
        received = partner(outgoing, "cube", bit_num)
        holding = jnp.bitwise_and(relative, (1 << bit_num + 1) - 1) == 0
        pieces = jnp.where(holding, retained, received)
    for bit_num in range(cube_bits):
        received = partner(pieces, "cube", bit_num)
        own_bit = jnp.bitwise_and(jnp.right_shift(local_blk, bit_num), 1) == 1
        pieces = jnp.where(
            own_bit, jnp.concatenate([received, pieces], 0), jnp.concatenate([pieces, received], 0)
        )
    return pieces.reshape(-1, block_cols)


def lift_rows(column, pivot_table, side_table, front_num, groups, block_cols):
    pivot_row = lax.dynamic_index_in_dim(pivot_table, front_num, 0, keepdims=False)
    blocks = jnp.arange(groups, dtype=jnp.int32)
    done_blocks = jnp.any(blocks[:, None] == pivot_row[None, :], axis=1)
    side_row = lax.dynamic_slice_in_dim(side_table, front_num * groups, groups, 0)
    positions = blocks + groups * side_row
    targets = jnp.arange(2 * groups, dtype=jnp.int32)
    select = (
        (positions[:, None] == targets[None, :]) & jnp.logical_not(done_blocks)[:, None]
    ).astype(jnp.float32)
    lifted = jnp.einsum(
        "rp,rab->pab",
        select,
        column.reshape(groups, block_cols, block_cols),
        precision=lax.Precision.HIGHEST,
    )
    return lifted.reshape(2 * groups * block_cols, block_cols)


def band_rows(matrix, block_num, block_cols):
    return lax.dynamic_slice_in_dim(matrix, block_num * block_cols, block_cols, 0)


def shards(
    front_leaf,
    front_lower,
    front_upper,
    front_root,
    inv_leaf,
    inv_lower,
    inv_upper,
    inv_root,
    pivots_leaf,
    pivots_lower,
    pivots_upper,
    pivots_root,
    child_sides,
):
    fronts = (front_leaf, front_lower, front_upper, front_root)
    inverses = (inv_leaf, inv_lower, inv_upper, inv_root)
    tables = (pivots_leaf, pivots_lower, pivots_upper, pivots_root)
    device_idx = lax.axis_index("cube")
    block_cols = front_leaf.shape[1]
    carried = None
    results = []
    for tier_num in range(4):
        front_width = fronts[tier_num].shape[0]
        groups = front_width // block_cols
        cube_bits = groups.bit_length() - 1
        owner_front = device_idx // groups
        local_blk = device_idx % groups
        column = fronts[tier_num].astype(jnp.float32)
        if carried is not None:
            column = lax.optimization_barrier((column + carried).astype(jnp.bfloat16)).astype(
                jnp.float32
            )
        pivot_row = lax.dynamic_index_in_dim(tables[tier_num], owner_front, 0, keepdims=False)
        block_ids = jnp.arange(front_width, dtype=jnp.int32) // block_cols
        inverse = inverses[tier_num]
        done_rows = jnp.zeros((front_width,), jnp.bool_)
        done_column = jnp.zeros((), jnp.bool_)
        for panel_num in range(tables[tier_num].shape[1]):
            pivot_blk = pivot_row[panel_num]
            is_pivot = local_blk == pivot_blk
            factor = lax.cond(is_pivot, scale_panel, empty_panel, column, inverse)
            shared = spread_panel(factor, local_blk, pivot_blk, cube_bits, block_cols).astype(
                jnp.float32
            )
            done_rows = done_rows | (block_ids == pivot_blk)
            pivot_band = band_rows(column, pivot_blk, block_cols)
            masked = jnp.where(done_rows[:, None], 0.0, shared)
            update = jnp.dot(masked, pivot_band, precision=lax.Precision.HIGHEST)
            column = jnp.where(is_pivot, shared, jnp.where(done_column, column, column - update))
            done_column = done_column | is_pivot
        results.append(column)
        if tier_num < 3:
            partner_col = partner(column, "cube", cube_bits)
            side_table = child_sides[tier_num]
            parent_bit = jnp.bitwise_and(jnp.right_shift(device_idx, cube_bits), 1)
            partner_idx = jnp.bitwise_xor(device_idx, groups)
            partner_front = jnp.bitwise_xor(owner_front, 1)
            own_map = lift_rows(
                column, tables[tier_num], side_table, owner_front, groups, block_cols
            )
            partner_map = lift_rows(
                partner_col, tables[tier_num], side_table, partner_front, groups, block_cols
            )
            partner_pivots = lax.dynamic_index_in_dim(
                tables[tier_num], partner_front, 0, keepdims=False
            )
            partner_done = jnp.any(partner_pivots == local_blk)
            own_lands = (side_table[device_idx] == parent_bit) & jnp.logical_not(done_column)
            partner_lands = (side_table[partner_idx] == parent_bit) & jnp.logical_not(partner_done)
            carried = jnp.where(own_lands, own_map, 0.0) + jnp.where(
                partner_lands, partner_map, 0.0
            )
    return (results[0], results[1], results[2], results[3])


def solution(mesh):
    placed = (
        P(None, "cube"),
        P(None, "cube"),
        P(None, "cube"),
        P(None, "cube"),
        P("cube", None),
        P("cube", None),
        P("cube", None),
        P("cube", None),
        P(),
        P(),
        P(),
        P(),
        P(),
    )
    return jax.shard_map(
        shards,
        mesh=mesh,
        in_specs=placed,
        out_specs=(P(None, "cube"), P(None, "cube"), P(None, "cube"), P(None, "cube")),
        check_vma=False,
    )
```

profile of v0, /device:TPU:1, one launch (start us, length us, event | category | flops | bytes accessed | tf_op | source)
XLA Modules:
  0.0 1126.6 jit_solution(5226854567688315213)
XLA Ops:
  91.9 15.0 %collective-permute-done.16 = f32[2048,128]{1,0:T(8,128)S(1)} collective-permute-done((f32[2048,128]{1,0:T(8,128)S(1)}, f32[2048,128]{1,0:T(8,128)S(1)}, u32[]{:S(2)}, u32[]{:S(2)}) %collective-permute-start.16) | collective-permute-done | bytes 1048608 | tf_op jit(solution)/shard_map/ppermute | solution.py:8
  259.9 34.8 %collective-permute-done.37 = f32[4096,128]{1,0:T(8,128)S(1)} collective-permute-done((f32[4096,128]{1,0:T(8,128)}, f32[4096,128]{1,0:T(8,128)S(1)}, u32[]{:S(2)}, u32[]{:S(2)}) %collective-permute-start.37) | collective-permute-done | bytes 2097184 | tf_op jit(solution)/shard_map/ppermute | solution.py:8
  305.4 20.5 %collective-permute-done.38 = bf16[32,128,128]{2,1,0:T(8,128)(2,1)} collective-permute-done((bf16[32,128,128]{2,1,0:T(8,128)(2,1)}, bf16[32,128,128]{2,1,0:T(8,128)(2,1)}, u32[]{:S(2)}, u32[]{:S(2)}) %collective-permute-start.38) | collective-permute-done | bytes 1048608 | tf_op jit(solution)/shard_map/ppermute | solution.py:8
  328.6 10.5 collective-permute-done.39
  385.3 12.3 %collective-permute-done.48 = bf16[16,128,128]{2,1,0:T(8,128)(2,1)S(1)} collective-permute-done((bf16[16,128,128]{2,1,0:T(8,128)(2,1)S(1)}, bf16[16,128,128]{2,1,0:T(8,128)(2,1)S(1)}, u32[]{:S(2)}, u32[]{:S(2)}) %collective-permute-start.48) | collective-permute-done | bytes 524320 | tf_op jit(solution)/shard_map/ppermute | solution.py:8
  401.9 18.5 %collective-permute-done.49 = bf16[32,128,128]{2,1,0:T(8,128)(2,1)} collective-permute-done((bf16[32,128,128]{2,1,0:T(8,128)(2,1)S(1)}, bf16[32,128,128]{2,1,0:T(8,128)(2,1)}, u32[]{:S(2)}, u32[]{:S(2)}) %collective-permute-start.49) | collective-permute-done | bytes 1048608 | tf_op jit(solution)/shard_map/ppermute | solution.py:8
  433.2 19.0 %collective-permute-done.50 = bf16[32,128,128]{2,1,0:T(8,128)(2,1)} collective-permute-done((bf16[32,128,128]{2,1,0:T(8,128)(2,1)S(1)}, bf16[32,128,128]{2,1,0:T(8,128)(2,1)}, u32[]{:S(2)}, u32[]{:S(2)}) %collective-permute-start.50) | collective-permute-done | bytes 1048608 | tf_op jit(solution)/shard_map/ppermute | solution.py:8
  478.7 10.6 collective-permute-start.55
  520.2 16.7 %collective-permute-done.61 = bf16[32,128,128]{2,1,0:T(8,128)(2,1)S(1)} collective-permute-done((bf16[32,128,128]{2,1,0:T(8,128)(2,1)S(1)}, bf16[32,128,128]{2,1,0:T(8,128)(2,1)S(1)}, u32[]{:S(2)}, u32[]{:S(2)}) %collective-permute-start.61) | collective-permute-done | bytes 1048608 | tf_op jit(solution)/shard_map/ppermute | solution.py:8
  537.3 11.9 %fusion.5 = f32[8192,128]{1,0:T(8,128)} fusion(f32[8192,128]{1,0:T(8,128)} %fusion.4, bf16[8192,128]{1,0:T(8,128)(2,1)S(1)} %bitcast.138, pred[8192]{0:T(1024)(128)(4,1)S(1)} %fusion.67, pred[]{:T(512)S(6)} %eq.652, pred[]{:T(512)S(6)} %eq.639, s32[]{:T(128)S(6)} %select_n.1472), kind=kOutput, calls=%fused_computation.19 | convolution fusion | flops 1616904192 | bytes 12656646 | tf_op jit(solution)/shard_map/dot_general | solution.py:112
  567.6 74.4 %collective-permute-done.62 = f32[8192,128]{1,0:T(8,128)} collective-permute-done((f32[8192,128]{1,0:T(8,128)}, f32[8192,128]{1,0:T(8,128)}, u32[]{:S(2)}, u32[]{:S(2)}) %collective-permute-start.62) | collective-permute-done | bytes 4194336 | tf_op jit(solution)/shard_map/ppermute | solution.py:8
  666.6 40.7 %collective-permute-done.63 = bf16[64,128,128]{2,1,0:T(8,128)(2,1)} collective-permute-done((bf16[64,128,128]{2,1,0:T(8,128)(2,1)}, bf16[64,128,128]{2,1,0:T(8,128)(2,1)}, u32[]{:S(2)}, u32[]{:S(2)}) %collective-permute-start.63) | collective-permute-done | bytes 2097184 | tf_op jit(solution)/shard_map/ppermute | solution.py:8
  712.2 18.8 %collective-permute-done.64 = bf16[32,128,128]{2,1,0:T(8,128)(2,1)S(1)} collective-permute-done((bf16[32,128,128]{2,1,0:T(8,128)(2,1)S(1)}, bf16[32,128,128]{2,1,0:T(8,128)(2,1)S(1)}, u32[]{:S(2)}, u32[]{:S(2)}) %collective-permute-start.64) | collective-permute-done | bytes 1048608 | tf_op jit(solution)/shard_map/ppermute | solution.py:8
  759.5 11.0 collective-permute-start.69
  790.5 12.5 %collective-permute-done.74 = bf16[16,128,128]{2,1,0:T(8,128)(2,1)S(1)} collective-permute-done((bf16[16,128,128]{2,1,0:T(8,128)(2,1)S(1)}, bf16[16,128,128]{2,1,0:T(8,128)(2,1)S(1)}, u32[]{:S(2)}, u32[]{:S(2)}) %collective-permute-start.74) | collective-permute-done | bytes 524320 | tf_op jit(solution)/shard_map/ppermute | solution.py:8
  804.4 20.5 %collective-permute-done.75 = bf16[32,128,128]{2,1,0:T(8,128)(2,1)S(1)} collective-permute-done((bf16[32,128,128]{2,1,0:T(8,128)(2,1)S(1)}, bf16[32,128,128]{2,1,0:T(8,128)(2,1)S(1)}, u32[]{:S(2)}, u32[]{:S(2)}) %collective-permute-start.75) | collective-permute-done | bytes 1048608 | tf_op jit(solution)/shard_map/ppermute | solution.py:8
  828.7 43.0 %collective-permute-done.76 = bf16[64,128,128]{2,1,0:T(8,128)(2,1)} collective-permute-done((bf16[64,128,128]{2,1,0:T(8,128)(2,1)S(1)}, bf16[64,128,128]{2,1,0:T(8,128)(2,1)}, u32[]{:S(2)}, u32[]{:S(2)}) %collective-permute-start.76) | collective-permute-done | bytes 2097184 | tf_op jit(solution)/shard_map/ppermute | solution.py:8
  875.2 15.6 %fusion.1 = f32[16384,128]{1,0:T(8,128)} fusion(bf16[16384,128]{1,0:T(8,128)(2,1)S(1)} %bitcast.127, pred[16384]{0:T(1024)(128)(4,1)S(1)} %fusion.46, pred[]{:T(512)S(6)} %eq.695, bf16[16384,128]{1,0:T(8,128)(2,1)S(1)} %copy-done.1, s32[]{:T(128)S(6)} %select_n.1544), kind=kOutput, calls=%fused_computation.11 | convolution fusion | flops 3233808384 | bytes 21020676 | tf_op jit(solution)/shard_map/dot_general | solution.py:112
  895.6 44.3 %collective-permute-done.77 = bf16[64,128,128]{2,1,0:T(8,128)(2,1)} collective-permute-done((bf16[64,128,128]{2,1,0:T(8,128)(2,1)}, bf16[64,128,128]{2,1,0:T(8,128)(2,1)}, u32[]{:S(2)}, u32[]{:S(2)}) %collective-permute-start.77) | collective-permute-done | bytes 2097184 | tf_op jit(solution)/shard_map/ppermute | solution.py:8
  944.8 19.7 %collective-permute-done.78 = bf16[32,128,128]{2,1,0:T(8,128)(2,1)S(1)} collective-permute-done((bf16[32,128,128]{2,1,0:T(8,128)(2,1)S(1)}, bf16[32,128,128]{2,1,0:T(8,128)(2,1)S(1)}, u32[]{:S(2)}, u32[]{:S(2)}) %collective-permute-start.78) | collective-permute-done | bytes 1048608 | tf_op jit(solution)/shard_map/ppermute | solution.py:8
  1022.3 11.2 collective-permute-done.88
  1034.1 21.5 %collective-permute-done.89 = bf16[32,128,128]{2,1,0:T(8,128)(2,1)S(1)} collective-permute-done((bf16[32,128,128]{2,1,0:T(8,128)(2,1)S(1)}, bf16[32,128,128]{2,1,0:T(8,128)(2,1)S(1)}, u32[]{:S(2)}, u32[]{:S(2)}) %collective-permute-start.89) | collective-permute-done | bytes 1048608 | tf_op jit(solution)/shard_map/ppermute | solution.py:8
  1060.5 41.8 %collective-permute-done.90 = bf16[64,128,128]{2,1,0:T(8,128)(2,1)} collective-permute-done((bf16[64,128,128]{2,1,0:T(8,128)(2,1)S(1)}, bf16[64,128,128]{2,1,0:T(8,128)(2,1)}, u32[]{:S(2)}, u32[]{:S(2)}) %collective-permute-start.90) | collective-permute-done | bytes 2097184 | tf_op jit(solution)/shard_map/ppermute | solution.py:8
  1104.8 21.5 %fusion.2 = f32[16384,128]{1,0:T(8,128)} fusion(f32[16384,128]{1,0:T(8,128)} %fusion.1, bf16[16384,128]{1,0:T(8,128)(2,1)S(1)} %bitcast.133, pred[16384]{0:T(1024)(128)(4,1)S(1)} %fusion.51, pred[]{:T(512)S(6)} %eq.695, pred[]{:T(512)S(6)} %eq.680, s32[]{:T(128)S(6)} %select_n.1575), kind=kOutput, calls=%fused_computation.12 | convolution fusion | flops 3233808384 | bytes 25247750 | tf_op jit(solution)/shard_map/dot_general | solution.py:112
  (418 shorter events, 539.7 us)
Async XLA Ops:
  80.9 26.0 %collective-permute-start.16 = (f32[2048,128]{1,0:T(8,128)S(1)}, f32[2048,128]{1,0:T(8,128)S(1)}, u32[]{:S(2)}, u32[]{:S(2)}) collective-permute-start(f32[2048,128]{1,0:T(8,128)S(1)} %fusion.22), channel_id=1, source_target_pairs={{0,16},{1,17},{2,18},{3,19},{4,20},{5,21},{6,22},{7,23},{8,24},{9,... | collective-permute-start | bytes 3145736 | tf_op jit(solution)/shard_map/ppermute | solution.py:8
  112.1 11.3 %collective-permute-start.17 = (bf16[16,128,128]{2,1,0:T(8,128)(2,1)S(1)}, bf16[16,128,128]{2,1,0:T(8,128)(2,1)S(1)}, u32[]{:S(2)}, u32[]{:S(2)}) collective-permute-start(bf16[16,128,128]{2,1,0:T(8,128)(2,1)S(1)} %broadcast_select_fusion.11), channel_id=1, source_target_pairs={{0,16},{1,17},{2,18},{3,19},{4,20},{5,21},{6,22},{7,23},{8,24},{9,... | collective-permute-start | bytes 1572872 | tf_op jit(solution)/shard_map/ppermute | solution.py:8
  231.9 14.3 %collective-permute-start.36 = (bf16[16,128,128]{2,1,0:T(8,128)(2,1)S(1)}, bf16[16,128,128]{2,1,0:T(8,128)(2,1)S(1)}, u32[]{:S(2)}, u32[]{:S(2)}) collective-permute-start(bf16[16,128,128]{2,1,0:T(8,128)(2,1)S(1)} %maximum_select_fusion.15), channel_id=1, source_target_pairs={{0,16},{1,17},{2,18},{3,19},{4,20},{5,21},{6,22},{7,23},{8,24},{9,... | collective-permute-start | bytes 1572872 | tf_op jit(solution)/shard_map/ppermute | solution.py:8
  249.8 44.9 %collective-permute-start.37 = (f32[4096,128]{1,0:T(8,128)}, f32[4096,128]{1,0:T(8,128)S(1)}, u32[]{:S(2)}, u32[]{:S(2)}) collective-permute-start(f32[4096,128]{1,0:T(8,128)} %fusion.8), channel_id=1, source_target_pairs={{0,32},{1,33},{2,34},{3,35},{4,36},{5,37},{6,38},{7,39},{8,40},{9,... | collective-permute-start | bytes 6291464 | tf_op jit(solution)/shard_map/ppermute | solution.py:8
  304.7 21.2 %collective-permute-start.38 = (bf16[32,128,128]{2,1,0:T(8,128)(2,1)}, bf16[32,128,128]{2,1,0:T(8,128)(2,1)}, u32[]{:S(2)}, u32[]{:S(2)}) collective-permute-start(bf16[32,128,128]{2,1,0:T(8,128)(2,1)} %broadcast_select_fusion.5), channel_id=1, source_target_pairs={{0,32},{1,33},{2,34},{3,35},{4,36},{5,37},{6,38},{7,39},{8,40},{9,... | collective-permute-start | bytes 3145736 | tf_op jit(solution)/shard_map/ppermute | solution.py:8
  356.2 11.3 %collective-permute-start.43 = (bf16[1,128,128]{2,1,0:T(8,128)(2,1)S(1)}, bf16[1,128,128]{2,1,0:T(8,128)(2,1)S(1)}, u32[]{:S(2)}, u32[]{:S(2)}) collective-permute-start(bf16[1,128,128]{2,1,0:T(8,128)(2,1)S(1)} %broadcast_select_fusion.39), channel_id=1, source_target_pairs={{0,1},{1,0},{2,3},{3,2},{4,5},{5,4},{6,7},{7,6},{8,9},{9,8},{10,11... | collective-permute-start | bytes 98312 | tf_op jit(solution)/shard_map/ppermute | solution.py:8
  385.1 12.5 %collective-permute-start.48 = (bf16[16,128,128]{2,1,0:T(8,128)(2,1)S(1)}, bf16[16,128,128]{2,1,0:T(8,128)(2,1)S(1)}, u32[]{:S(2)}, u32[]{:S(2)}) collective-permute-start(bf16[16,128,128]{2,1,0:T(8,128)(2,1)S(1)} %maximum_select_fusion.16), channel_id=1, source_target_pairs={{0,16},{1,17},{2,18},{3,19},{4,20},{5,21},{6,22},{7,23},{8,24},{9,... | collective-permute-start | bytes 1572872 | tf_op jit(solution)/shard_map/ppermute | solution.py:8
  397.8 22.6 %collective-permute-start.49 = (bf16[32,128,128]{2,1,0:T(8,128)(2,1)S(1)}, bf16[32,128,128]{2,1,0:T(8,128)(2,1)}, u32[]{:S(2)}, u32[]{:S(2)}) collective-permute-start(bf16[32,128,128]{2,1,0:T(8,128)(2,1)S(1)} %maximum_select_fusion.8), channel_id=1, source_target_pairs={{0,32},{1,33},{2,34},{3,35},{4,36},{5,37},{6,38},{7,39},{8,40},{9,... | collective-permute-start | bytes 3145736 | tf_op jit(solution)/shard_map/ppermute | solution.py:8
  431.1 21.1 %collective-permute-start.50 = (bf16[32,128,128]{2,1,0:T(8,128)(2,1)S(1)}, bf16[32,128,128]{2,1,0:T(8,128)(2,1)}, u32[]{:S(2)}, u32[]{:S(2)}) collective-permute-start(bf16[32,128,128]{2,1,0:T(8,128)(2,1)S(1)} %broadcast_select_fusion.4), channel_id=1, source_target_pairs={{0,32},{1,33},{2,34},{3,35},{4,36},{5,37},{6,38},{7,39},{8,40},{9,... | collective-permute-start | bytes 3145736 | tf_op jit(solution)/shard_map/ppermute | solution.py:8
  478.7 11.5 %collective-permute-start.55 = (bf16[1,128,128]{2,1,0:T(8,128)(2,1)S(1)}, bf16[1,128,128]{2,1,0:T(8,128)(2,1)S(1)}, u32[]{:S(2)}, u32[]{:S(2)}) collective-permute-start(bf16[1,128,128]{2,1,0:T(8,128)(2,1)S(1)} %broadcast_select_fusion.38), channel_id=1, source_target_pairs={{0,1},{1,0},{2,3},{3,2},{4,5},{5,4},{6,7},{7,6},{8,9},{9,8},{10,11... | collective-permute-start | bytes 98312 | tf_op jit(solution)/shard_map/ppermute | solution.py:8
  505.5 11.0 collective-permute-start.60
  516.7 20.2 %collective-permute-start.61 = (bf16[32,128,128]{2,1,0:T(8,128)(2,1)S(1)}, bf16[32,128,128]{2,1,0:T(8,128)(2,1)S(1)}, u32[]{:S(2)}, u32[]{:S(2)}) collective-permute-start(bf16[32,128,128]{2,1,0:T(8,128)(2,1)S(1)} %maximum_select_fusion.9), channel_id=1, source_target_pairs={{0,32},{1,33},{2,34},{3,35},{4,36},{5,37},{6,38},{7,39},{8,40},{9,... | collective-permute-start | bytes 3145736 | tf_op jit(solution)/shard_map/ppermute | solution.py:8
  549.2 92.9 %collective-permute-start.62 = (f32[8192,128]{1,0:T(8,128)}, f32[8192,128]{1,0:T(8,128)}, u32[]{:S(2)}, u32[]{:S(2)}) collective-permute-start(f32[8192,128]{1,0:T(8,128)} %fusion.5), channel_id=1, source_target_pairs={{0,64},{1,65},{2,66},{3,67},{4,68},{5,69},{6,70},{7,71},{8,72},{9,... | collective-permute-start | bytes 12582920 | tf_op jit(solution)/shard_map/ppermute | solution.py:8
  663.2 44.0 %collective-permute-start.63 = (bf16[64,128,128]{2,1,0:T(8,128)(2,1)}, bf16[64,128,128]{2,1,0:T(8,128)(2,1)}, u32[]{:S(2)}, u32[]{:S(2)}) collective-permute-start(bf16[64,128,128]{2,1,0:T(8,128)(2,1)} %broadcast_select_fusion.1), channel_id=1, source_target_pairs={{0,64},{1,65},{2,66},{3,67},{4,68},{5,69},{6,70},{7,71},{8,72},{9,... | collective-permute-start | bytes 6291464 | tf_op jit(solution)/shard_map/ppermute | solution.py:8
  712.1 18.9 %collective-permute-start.64 = (bf16[32,128,128]{2,1,0:T(8,128)(2,1)S(1)}, bf16[32,128,128]{2,1,0:T(8,128)(2,1)S(1)}, u32[]{:S(2)}, u32[]{:S(2)}) collective-permute-start(bf16[32,128,128]{2,1,0:T(8,128)(2,1)S(1)} %broadcast_select_fusion.3), channel_id=1, source_target_pairs={{0,32},{1,33},{2,34},{3,35},{4,36},{5,37},{6,38},{7,39},{8,40},{9,... | collective-permute-start | bytes 3145736 | tf_op jit(solution)/shard_map/ppermute | solution.py:8
  759.5 11.9 %collective-permute-start.69 = (bf16[1,128,128]{2,1,0:T(8,128)(2,1)S(1)}, bf16[1,128,128]{2,1,0:T(8,128)(2,1)S(1)}, u32[]{:S(2)}, u32[]{:S(2)}) collective-permute-start(bf16[1,128,128]{2,1,0:T(8,128)(2,1)S(1)} %broadcast_select_fusion.37), channel_id=1, source_target_pairs={{0,1},{1,0},{2,3},{3,2},{4,5},{5,4},{6,7},{7,6},{8,9},{9,8},{10,11... | collective-permute-start | bytes 98312 | tf_op jit(solution)/shard_map/ppermute | solution.py:8
  790.0 12.9 %collective-permute-start.74 = (bf16[16,128,128]{2,1,0:T(8,128)(2,1)S(1)}, bf16[16,128,128]{2,1,0:T(8,128)(2,1)S(1)}, u32[]{:S(2)}, u32[]{:S(2)}) collective-permute-start(bf16[16,128,128]{2,1,0:T(8,128)(2,1)S(1)} %maximum_select_fusion.18), channel_id=1, source_target_pairs={{0,16},{1,17},{2,18},{3,19},{4,20},{5,21},{6,22},{7,23},{8,24},{9,... | collective-permute-start | bytes 1572872 | tf_op jit(solution)/shard_map/ppermute | solution.py:8
  803.1 21.7 %collective-permute-start.75 = (bf16[32,128,128]{2,1,0:T(8,128)(2,1)S(1)}, bf16[32,128,128]{2,1,0:T(8,128)(2,1)S(1)}, u32[]{:S(2)}, u32[]{:S(2)}) collective-permute-start(bf16[32,128,128]{2,1,0:T(8,128)(2,1)S(1)} %maximum_select_fusion.10), channel_id=1, source_target_pairs={{0,32},{1,33},{2,34},{3,35},{4,36},{5,37},{6,38},{7,39},{8,40},{9,... | collective-permute-start | bytes 3145736 | tf_op jit(solution)/shard_map/ppermute | solution.py:8
  825.2 46.6 %collective-permute-start.76 = (bf16[64,128,128]{2,1,0:T(8,128)(2,1)S(1)}, bf16[64,128,128]{2,1,0:T(8,128)(2,1)}, u32[]{:S(2)}, u32[]{:S(2)}) collective-permute-start(bf16[64,128,128]{2,1,0:T(8,128)(2,1)S(1)} %maximum_select_fusion.4), channel_id=1, source_target_pairs={{0,64},{1,65},{2,66},{3,67},{4,68},{5,69},{6,70},{7,71},{8,72},{9,... | collective-permute-start | bytes 6291464 | tf_op jit(solution)/shard_map/ppermute | solution.py:8
  894.9 44.9 %collective-permute-start.77 = (bf16[64,128,128]{2,1,0:T(8,128)(2,1)}, bf16[64,128,128]{2,1,0:T(8,128)(2,1)}, u32[]{:S(2)}, u32[]{:S(2)}) collective-permute-start(bf16[64,128,128]{2,1,0:T(8,128)(2,1)} %broadcast_select_fusion), channel_id=1, source_target_pairs={{0,64},{1,65},{2,66},{3,67},{4,68},{5,69},{6,70},{7,71},{8,72},{9,... | collective-permute-start | bytes 6291464 | tf_op jit(solution)/shard_map/ppermute | solution.py:8
  944.7 19.8 %collective-permute-start.78 = (bf16[32,128,128]{2,1,0:T(8,128)(2,1)S(1)}, bf16[32,128,128]{2,1,0:T(8,128)(2,1)S(1)}, u32[]{:S(2)}, u32[]{:S(2)}) collective-permute-start(bf16[32,128,128]{2,1,0:T(8,128)(2,1)S(1)} %broadcast_select_fusion.2), channel_id=1, source_target_pairs={{0,32},{1,33},{2,34},{3,35},{4,36},{5,37},{6,38},{7,39},{8,40},{9,... | collective-permute-start | bytes 3145736 | tf_op jit(solution)/shard_map/ppermute | solution.py:8
  1017.9 15.6 %collective-permute-start.88 = (bf16[16,128,128]{2,1,0:T(8,128)(2,1)S(1)}, bf16[16,128,128]{2,1,0:T(8,128)(2,1)S(1)}, u32[]{:S(2)}, u32[]{:S(2)}) collective-permute-start(bf16[16,128,128]{2,1,0:T(8,128)(2,1)S(1)} %maximum_select_fusion.19), channel_id=1, source_target_pairs={{0,16},{1,17},{2,18},{3,19},{4,20},{5,21},{6,22},{7,23},{8,24},{9,... | collective-permute-start | bytes 1572872 | tf_op jit(solution)/shard_map/ppermute | solution.py:8
  1033.7 21.9 %collective-permute-start.89 = (bf16[32,128,128]{2,1,0:T(8,128)(2,1)S(1)}, bf16[32,128,128]{2,1,0:T(8,128)(2,1)S(1)}, u32[]{:S(2)}, u32[]{:S(2)}) collective-permute-start(bf16[32,128,128]{2,1,0:T(8,128)(2,1)S(1)} %maximum_select_fusion.11), channel_id=1, source_target_pairs={{0,32},{1,33},{2,34},{3,35},{4,36},{5,37},{6,38},{7,39},{8,40},{9,... | collective-permute-start | bytes 3145736 | tf_op jit(solution)/shard_map/ppermute | solution.py:8
  1055.9 46.4 %collective-permute-start.90 = (bf16[64,128,128]{2,1,0:T(8,128)(2,1)S(1)}, bf16[64,128,128]{2,1,0:T(8,128)(2,1)}, u32[]{:S(2)}, u32[]{:S(2)}) collective-permute-start(bf16[64,128,128]{2,1,0:T(8,128)(2,1)S(1)} %maximum_select_fusion.5), channel_id=1, source_target_pairs={{0,64},{1,65},{2,66},{3,67},{4,68},{5,69},{6,70},{7,71},{8,72},{9,... | collective-permute-start | bytes 6291464 | tf_op jit(solution)/shard_map/ppermute | solution.py:8
  (89 other events, 509.1 us)
where the time goes:
time: 1150 us; the launch traced here: 1130 us
  waiting for transfers between devices  754 us (66%)
  starting transfers between devices  177 us (15%)
  matrix products  93.7 us (8%)
  other arithmetic  53.4 us (5%)
  local copies, waits for them, and re-layouts  24 us (2%)
  between operations  24 us (2%)
    ppermute x91, waiting for transfers between devices, partner(): lax.ppermute(array, axis, [(i, i ^ 1 << bit) for i in range(lax.axis_size...  754 us
    ppermute x91, starting transfers between devices, partner(): lax.ppermute(array, axis, [(i, i ^ 1 << bit) for i in range(lax.axis_size...  177 us
    dot_general x8, matrix products, shards(): update = jnp.dot(masked, pivot_band, precision=lax.Precision.HIGHEST)  64.1 us
    dot_general x6, matrix products, lift_rows(): jnp.einsum('rp,rab->pab', select, column.reshape(groups, block_cols, bloc...  29.6 us
  transfers between devices with their start and end apart: 91, of which 91 were waited for; matrix products, arithmetic and copies ran while one was open for 3% of the time, Pallas kernels for 0%

commit v1 on v0

v1 whole, which is shorter than its diff:
```python
import jax
import jax.numpy as jnp
from jax import lax
from jax.sharding import PartitionSpec as P

AXIS = "cube"
SHIFT = {"y": 5, "z": 3, "x": 1}


def permute(array, pairs):
    return lax.ppermute(array, AXIS, pairs)


def moved(device, axis, count, step):
    shift = SHIFT[axis]
    position = (device >> shift) & (count - 1)
    return device - (position << shift) + (((position + step) % count) << shift)


STAGES = (
    ((("z", "z"), 2), (("x", "x"), 4)),
    ((("x", "z"), 4), (("z", "x"), 4)),
    ((("y", "y"), 2), (("x", "z"), 4), (("z", "x"), 4)),
    ((("x", "y"), 4), (("z", "x"), 4), (("y", "z"), 4)),
)


def gather_stage(block, device, axes, count):
    devices = lax.axis_size(AXIS)
    pieces = [block]
    for step in range(1, count):
        pairs = [(moved(i, axes[i & 1], count, step), i) for i in range(devices)]
        pieces.append(permute(block, pairs))
    position = jnp.where(
        device & 1 == 0,
        (device >> SHIFT[axes[0]]) & (count - 1),
        (device >> SHIFT[axes[1]]) & (count - 1),
    )
    placed = []
    for spot in range(count):
        which = jnp.bitwise_and(spot - position, count - 1)
        if count == 2:
            placed.append(jnp.where(which == 0, pieces[0], pieces[1]))
        else:
            placed.append(lax.select_n(which, *pieces))
    return jnp.stack(placed, 0)


def gather_rows(block, device, tier_num):
    rows, cols = block.shape
    devices = lax.axis_size(AXIS)
    stages = STAGES[tier_num]
    half = block
    for axes, count in stages:
        half = gather_stage(half, device, axes, count)
    other = permute(half, [(i, i ^ 1) for i in range(devices)])
    even = jnp.where(device & 1 == 0, half, other)
    odd = jnp.where(device & 1 == 0, other, half)
    order = sorted(a for (a, _), _ in stages)
    order = [a for a in "yzx" if a in order]
    halves = []
    for core, part in ((0, even), (1, odd)):
        held = [axes[core] for axes, _ in reversed(stages)]
        turn = [held.index(a) for a in order]
        part = jnp.transpose(part, turn + [len(turn), len(turn) + 1])
        halves.append(part.reshape(-1, rows, cols))
    return jnp.stack(halves, 1).reshape(-1, rows, cols)


def shards(
    front_leaf,
    front_lower,
    front_upper,
    front_root,
    inv_leaf,
    inv_lower,
    inv_upper,
    inv_root,
    pivots_leaf,
    pivots_lower,
    pivots_upper,
    pivots_root,
    child_sides,
):
    fronts = (front_leaf, front_lower, front_upper, front_root)
    inverses = (inv_leaf, inv_lower, inv_upper, inv_root)
    tables = (pivots_leaf, pivots_lower, pivots_upper, pivots_root)
    device = lax.axis_index(AXIS)
    devices = lax.axis_size(AXIS)
    width = front_leaf.shape[1]
    column = front_leaf
    results = []
    for tier_num in range(4):
        groups = fronts[tier_num].shape[0] // width
        front_num = device // groups
        local = device % groups
        teams = [list(range(i, i + groups)) for i in range(0, devices, groups)]
        table = tables[tier_num]
        pivot_row = lax.dynamic_index_in_dim(table, front_num, 0, keepdims=False)
        first, second = pivot_row[0], pivot_row[1]
        is_first, is_second = local == first, local == second

        scaled = jnp.dot(column, inverses[tier_num], preferred_element_type=jnp.float32)
        scaled = scaled.astype(jnp.bfloat16)
        rows = lax.all_to_all(
            scaled.reshape(groups, width, width), AXIS, 0, 0, axis_index_groups=teams, tiled=True
        )
        own = jnp.concatenate(
            [
                lax.dynamic_index_in_dim(rows, first, 0, keepdims=False),
                lax.dynamic_index_in_dim(rows, second, 0, keepdims=False),
            ],
            1,
        )
        panels = gather_rows(own, device, tier_num)
        blocks = jnp.arange(groups, dtype=jnp.int32)
        live_first = (blocks != first)[:, None, None]
        live = ((blocks != first) & (blocks != second))[:, None, None]
        zero = jnp.zeros((), jnp.bfloat16)
        factor0 = panels[:, :, :width]
        scaled1 = panels[:, :, width:]
        masked0 = jnp.where(live_first, factor0, zero).reshape(-1, width)
        top1 = lax.dynamic_index_in_dim(scaled1, first, 0, keepdims=False)
        change1 = jnp.dot(masked0, top1, preferred_element_type=jnp.float32)
        factor1 = (scaled1.reshape(-1, width).astype(jnp.float32) - change1).astype(jnp.bfloat16)
        masked1 = jnp.where(live, factor1.reshape(groups, width, width), zero).reshape(-1, width)

        cube = column.reshape(groups, width, width)
        band0 = lax.dynamic_index_in_dim(cube, first, 0, keepdims=False)
        band1 = lax.dynamic_index_in_dim(cube, second, 0, keepdims=False)
        fac01 = lax.dynamic_index_in_dim(factor0, second, 0, keepdims=False)
        band1 = (
            band1.astype(jnp.float32) - jnp.dot(fac01, band0, preferred_element_type=jnp.float32)
        ).astype(jnp.bfloat16)
        update = jnp.dot(
            jnp.concatenate([masked0, masked1], 1),
            jnp.concatenate([band0, band1], 0),
            preferred_element_type=jnp.float32,
        )
        final = jnp.where(
            is_first,
            factor0.reshape(-1, width).astype(jnp.float32),
            jnp.where(
                is_second, factor1.astype(jnp.float32), column.astype(jnp.float32) - update
            ),
        )
        results.append(final)
        if tier_num < 3:
            sent = final.astype(jnp.bfloat16)
            received = permute(sent, [(i, i ^ groups) for i in range(devices)])
            side_row = child_sides[tier_num]
            parent_half = (device // groups) & 1
            total = fronts[tier_num + 1].reshape(2, groups, width, width).astype(jnp.float32)
            halves = jnp.arange(2, dtype=jnp.int32)
            for part, flip in ((final.reshape(groups, width, width), 0), (received.reshape(groups, width, width), 1)):
                front_of = front_num ^ flip
                pivots_of = lax.dynamic_index_in_dim(table, front_of, 0, keepdims=False)
                sides = lax.dynamic_slice_in_dim(side_row, front_of * groups, groups, 0)
                stays = (blocks != pivots_of[0]) & (blocks != pivots_of[1])
                lands = (
                    (lax.dynamic_index_in_dim(side_row, front_of * groups + local, 0, keepdims=False) == parent_half)
                    & (local != pivots_of[0])
                    & (local != pivots_of[1])
                )
                keep = (sides[None, :] == halves[:, None]) & stays[None, :] & lands
                total = total + jnp.where(
                    keep[:, :, None, None], part[None].astype(jnp.float32), 0.0
                )
            column = total.astype(jnp.bfloat16).reshape(-1, width)
    return tuple(results)


def solution(mesh):
    across, down, whole = P(None, AXIS), P(AXIS, None), P()
    return jax.shard_map(
        shards,
        mesh=mesh,
        in_specs=(across,) * 4 + (down,) * 4 + (whole,) * 5,
        out_specs=(across,) * 4,
        check_vma=False,
    )
```

time: 1150 us -> 558 us (0.49); the launches traced: 1130 us -> 547 us
  waiting for transfers between devices: 754 us -> 220 us
  starting transfers between devices: 177 us -> 71.2 us
  local copies, waits for them, and re-layouts: 24 us -> 89.5 us
  matrix products: 93.7 us -> 41.6 us
  other arithmetic: 53.4 us -> 90 us
    ppermute x91 -> x33, waiting for transfers between devices: 754 us -> 132 us  [permute(): return lax.ppermute(array, AXIS, pairs)]
    ppermute x91 -> x33, starting transfers between devices: 177 us -> 42.9 us  [permute(): return lax.ppermute(array, AXIS, pairs)]
    all_to_all x0 -> x4, waiting for transfers between devices: none -> 88.8 us  [shards(): lax.all_to_all(scaled.reshape(groups, width, width), AXIS, 0, 0, axis_ind...]
    dot_general x14 -> x16, matrix products: 93.7 us -> 41.6 us  [the longest x4 17.6 us: shards(): change1 = jnp.dot(masked0, top1, preferred_element_type=jnp.float32)]
    convert_element_type x7 -> x11, other arithmetic: 4.58 us -> 42.1 us  [the longest x6 31.6 us: shards(): column = total.astype(jnp.bfloat16).reshape(-1, width)]
    convert_element_type x0 -> x4, local copies, waits for them, and re-layouts: none -> 28.4 us  [the longest x1 9.05 us: shards(): factor0.reshape(-1, width).astype(jnp.float32)]
    all_to_all x0 -> x4, starting transfers between devices: none -> 28.3 us  [shards(): lax.all_to_all(scaled.reshape(groups, width, width), AXIS, 0, 0, axis_ind...]
    select_n x132 -> x5, other arithmetic: 38.3 us -> 12.9 us  [the longest x4 7.47 us: gather_rows(): even = jnp.where(device & 1 == 0, half, other)]
  transfers between devices with their start and end apart: 91 -> 37, of which waited for: 91 -> 29; matrix products, arithmetic and copies ran while one was open for 3% -> 9% of each run, Pallas kernels for 0% -> 0%
where the time goes in v1:
time: 558 us; the launch traced here: 547 us
  waiting for transfers between devices  220 us (39%)
  other arithmetic  90 us (16%)
  local copies, waits for them, and re-layouts  89.5 us (16%)
  starting transfers between devices  71.2 us (13%)
  matrix products  41.6 us (7%)
  between operations  34.6 us (6%)
    ppermute x33, waiting for transfers between devices, permute(): return lax.ppermute(array, AXIS, pairs)  132 us
    all_to_all x4, waiting for transfers between devices, shards(): lax.all_to_all(scaled.reshape(groups, width, width), AXIS, 0, 0, axis_ind...  88.8 us
    ppermute x33, starting transfers between devices, permute(): return lax.ppermute(array, AXIS, pairs)  42.9 us
    convert_element_type x6, other arithmetic, shards(): column = total.astype(jnp.bfloat16).reshape(-1, width)  31.6 us
    all_to_all x4, starting transfers between devices, shards(): lax.all_to_all(scaled.reshape(groups, width, width), AXIS, 0, 0, axis_ind...  28.3 us
    unnamed x112, local copies, waits for them, and re-layouts  23.1 us
    dot_general x4, matrix products, shards(): change1 = jnp.dot(masked0, top1, preferred_element_type=jnp.float32)  17.6 us
    another operation x28, other arithmetic, gather_stage(): return jnp.stack(placed, 0)  15.6 us
  transfers between devices with their start and end apart: 37, of which 29 were waited for; matrix products, arithmetic and copies ran while one was open for 9% of the time, Pallas kernels for 0%

profile of v1, /device:TPU:1, one launch (start us, length us, event | category | flops | bytes accessed | tf_op | source)
XLA Modules:
  0.0 547.4 jit_solution(1490732303590443477)
XLA Ops:
  2.8 7.2 %all-to-all-start = ((bf16[16,128,128]{2,1,0:T(8,128)(2,1)}), bf16[16,128,128]{2,1,0:T(8,128)(2,1)S(1)}, u32[]{:S(2)}, u32[]{:S(2)}) async-start(bf16[16,128,128]{2,1,0:T(8,128)(2,1)} %bitcast.1), calls=%async_computation | async-start | bytes 1048576 | tf_op jit(solution)/shard_map/all_to_all | solution.py:105
  43.4 10.7 %collective-permute-done.5 = bf16[2048,128]{1,0:T(8,128)(2,1)S(1)} collective-permute-done((bf16[2048,128]{1,0:T(8,128)(2,1)S(1)}, bf16[2048,128]{1,0:T(8,128)(2,1)S(1)}, u32[]{:S(2)}, u32[]{:S(2)}) %collective-permute-start.5) | collective-permute-done | bytes 524320 | tf_op jit(solution)/shard_map/ppermute | solution.py:11
  57.2 8.7 %all-to-all-start.1 = ((bf16[32,128,128]{2,1,0:T(8,128)(2,1)}), bf16[32,128,128]{2,1,0:T(8,128)(2,1)}, u32[]{:S(2)}, u32[]{:S(2)}) async-start(bf16[32,128,128]{2,1,0:T(8,128)(2,1)} %bitcast.428), calls=%async_computation.1 | async-start | bytes 2097152 | tf_op jit(solution)/shard_map/all_to_all | solution.py:105
  70.5 12.6 %all-to-all-done.1 = bf16[32,128,128]{2,1,0:T(8,128)(2,1)} async-done(((bf16[32,128,128]{2,1,0:T(8,128)(2,1)}), bf16[32,128,128]{2,1,0:T(8,128)(2,1)}, u32[]{:S(2)}, u32[]{:S(2)}) %all-to-all-start.1) | async-done | bytes 1048608 | tf_op jit(solution)/shard_map/all_to_all | solution.py:105
  130.1 17.6 %collective-permute-done.13 = bf16[4096,128]{1,0:T(8,128)(2,1)S(1)} collective-permute-done((bf16[4096,128]{1,0:T(8,128)(2,1)}, bf16[4096,128]{1,0:T(8,128)(2,1)S(1)}, u32[]{:S(2)}, u32[]{:S(2)}) %collective-permute-start.13) | collective-permute-done | bytes 1048608 | tf_op jit(solution)/shard_map/ppermute | solution.py:11
  155.4 5.7 %all-to-all-start.2 = ((bf16[64,128,128]{2,1,0:T(8,128)(2,1)}), bf16[64,128,128]{2,1,0:T(8,128)(2,1)}, u32[]{:S(2)}, u32[]{:S(2)}) async-start(bf16[64,128,128]{2,1,0:T(8,128)(2,1)} %bitcast.410), calls=%async_computation.2 | async-start | bytes 4194304 | tf_op jit(solution)/shard_map/all_to_all | solution.py:105
  165.5 23.8 %all-to-all-done.2 = bf16[64,128,128]{2,1,0:T(8,128)(2,1)} async-done(((bf16[64,128,128]{2,1,0:T(8,128)(2,1)}), bf16[64,128,128]{2,1,0:T(8,128)(2,1)}, u32[]{:S(2)}, u32[]{:S(2)}) %all-to-all-start.2) | async-done | bytes 2097184 | tf_op jit(solution)/shard_map/all_to_all | solution.py:105
  204.8 10.2 %collective-permute-done.18 = bf16[4,2,128,256]{3,2,0,1:T(8,128)(2,1)S(1)} collective-permute-done((bf16[4,2,128,256]{3,2,0,1:T(8,128)(2,1)S(1)}, bf16[4,2,128,256]{3,2,0,1:T(8,128)(2,1)S(1)}, u32[]{:S(2)}, u32[]{:S(2)}) %collective-permute-start.18) | collective-permute-done | bytes 524320 | tf_op jit(solution)/shard_map/ppermute | solution.py:11
  251.1 6.4 %copy.66 = bf16[16384,128]{0,1:T(8,128)(2,1)} copy(bf16[16384,128]{1,0:T(8,128)(2,1)} %param.16) | data formatting | bytes 8388608 | tf_op args[3]
  264.3 29.1 %collective-permute-done.22 = bf16[8192,128]{1,0:T(8,128)(2,1)S(1)} collective-permute-done((bf16[8192,128]{1,0:T(8,128)(2,1)}, bf16[8192,128]{1,0:T(8,128)(2,1)S(1)}, u32[]{:S(2)}, u32[]{:S(2)}) %collective-permute-start.22) | collective-permute-done | bytes 2097184 | tf_op jit(solution)/shard_map/ppermute | solution.py:11
  302.4 17.8 %fusion.7 = bf16[16384,128]{0,1:T(8,128)(2,1)S(1)} fusion(f32[16,8,128,128]{3,2,1,0:T(8,128)S(1)} %bitcast.398, f32[16,8,128,128]{3,2,1,0:T(8,128)S(1)} %bitcast.399, pred[16384]{0:T(1024)(128)(4,1)S(1)} %bitcast.442, pred[16384]{0:T(1024)(128)(4,1)S(1)} %bitcast.441, bf16[16384,128]{0,1:T(8,128)(2,1)S(1)} %copy-done.5), kind=kLoop, calls=%fused_computation.14 | loop fusion | flops 12582912 | bytes 25198592 | tf_op jit(solution)/shard_map/convert_element_type | solution.py:169
  323.6 6.8 %all-to-all-start.3 = ((bf16[128,128,128]{2,1,0:T(8,128)(2,1)}), bf16[128,128,128]{2,1,0:T(8,128)(2,1)}, u32[]{:S(2)}, u32[]{:S(2)}) async-start(bf16[128,128,128]{2,1,0:T(8,128)(2,1)} %bitcast.401), calls=%async_computation.3 | async-start | bytes 8388608 | tf_op jit(solution)/shard_map/all_to_all | solution.py:105
  335.0 48.1 %all-to-all-done.3 = bf16[128,128,128]{2,1,0:T(8,128)(2,1)} async-done(((bf16[128,128,128]{2,1,0:T(8,128)(2,1)}), bf16[128,128,128]{2,1,0:T(8,128)(2,1)}, u32[]{:S(2)}, u32[]{:S(2)}) %all-to-all-start.3) | async-done | bytes 4194336 | tf_op jit(solution)/shard_map/all_to_all | solution.py:105
  404.6 12.7 %collective-permute-done.29 = bf16[4,4,128,256]{3,2,1,0:T(8,128)(2,1)S(1)} collective-permute-done((bf16[4,4,128,256]{3,2,1,0:T(8,128)(2,1)}, bf16[4,4,128,256]{3,2,1,0:T(8,128)(2,1)S(1)}, u32[]{:S(2)}, u32[]{:S(2)}) %collective-permute-start.29) | collective-permute-done | bytes 1048608 | tf_op jit(solution)/shard_map/ppermute | solution.py:11
  420.7 10.3 %collective-permute-done.31 = bf16[4,4,128,256]{3,2,1,0:T(8,128)(2,1)} collective-permute-done((bf16[4,4,128,256]{3,2,1,0:T(8,128)(2,1)}, bf16[4,4,128,256]{3,2,1,0:T(8,128)(2,1)}, u32[]{:S(2)}, u32[]{:S(2)}) %collective-permute-start.31) | collective-permute-done | bytes 1048608 | tf_op jit(solution)/shard_map/ppermute | solution.py:11
  441.7 7.2 %copy.83 = f32[16384,128]{1,0:T(8,128)} copy(bf16[16384,128]{0,1:T(8,128)(2,1)} %copy.66) | data formatting | bytes 12582912 | tf_op jit(solution)/shard_map/convert_element_type | solution.py:153
  465.6 6.3 %pad_maximum_fusion = bf16[64,2,128,256]{3,2,0,1:T(8,128)(2,1)} fusion(bf16[64,1,128,256]{3,2,0,1:T(8,128)(2,1)} %bitcast.408, bf16[64,1,128,256]{3,2,0,1:T(8,128)(2,1)S(1)} %bitcast.404), kind=kLoop, calls=%fused_computation.17 | loop fusion | flops 4194304 | bytes 16777216 | tf_op jit(solution)/shard_map/stack | solution.py:67
  471.9 7.9 %copy.70 = bf16[64,2,128,256]{3,2,1,0:T(8,128)(2,1)} copy(bf16[64,2,128,256]{3,2,0,1:T(8,128)(2,1)} %pad_maximum_fusion) | data formatting | bytes 16777216 | tf_op jit(solution)/shard_map/stack | solution.py:67
  494.2 9.0 %copy.81 = f32[16384,128]{0,1:T(8,128)} copy(f32[16384,128]{1,0:T(8,128)} %bitcast_convert_fusion) | data formatting | bytes 16777216 | tf_op jit(solution)/shard_map/convert_element_type | solution.py:125
  503.3 9.1 %copy.80 = f32[16384,128]{0,1:T(8,128)} copy(f32[16384,128]{1,0:T(8,128)} %bitcast_convert_fusion.1) | data formatting | bytes 16777216 | tf_op jit(solution)/shard_map/convert_element_type | solution.py:142
  512.3 6.4 %copy.82 = bf16[16384,128]{0,1:T(8,128)(2,1)} copy(bf16[16384,128]{1,0:T(8,128)(2,1)} %bitcast.395) | data formatting | bytes 8388608 | tf_op jit(solution)/shard_map/reshape | solution.py:122
  518.7 10.2 %broadcast_select_fusion.1 = (bf16[16384,128]{0,1:T(8,128)(2,1)}, bf16[16384,128]{0,1:T(8,128)(2,1)}) fusion(pred[16384]{0:T(1024)(128)(4,1)S(1)} %broadcast_bitcast_fusion, f32[16384,128]{0,1:T(8,128)} %copy.81, bf16[16384,128]{1,0:T(8,128)(2,1)} %bitcast.396, bf16[128,128,128]{2,1,0:T(8,128)(2,1)} %copy-done.8, s32[]{:T(128)S(6)} %select_n.1379), kind=kOutput, calls=%fused_computation.51 | convolution fusion | flops 543162368 | bytes 21020676 | tf_op jit(solution)/shard_map/dot_general | solution.py:124
  529.9 8.1 %fusion.2 = f32[16384,128]{0,1:T(8,128)} fusion(f32[16384,128]{0,1:T(8,128)S(1)} %copy-done.4, bf16[16384,128]{0,1:T(8,128)(2,1)} %get-tuple-element.129, bf16[16384,128]{0,1:T(8,128)(2,1)} %copy.82, bf16[16384,128]{0,1:T(8,128)(2,1)S(1)} %copy-done.3, bf16[16384,128]{0,1:T(8,128)(2,1)} %get-tuple-element.130, pred[]{:T(512)S(6)} %eq.317, pred[]{:T(512)S(6)} %eq.306, ...), kind=kOutput, calls=%fused_computation.5 | convolution fusion | flops 1101135872 | bytes 33619968 | tf_op jit(solution)/shard_map/dot_general | solution.py:135
  538.0 9.0 %copy.78 = f32[16384,128]{1,0:T(8,128)} copy(f32[16384,128]{0,1:T(8,128)} %fusion.2) | data formatting | bytes 16777216
  (328 shorter events, 212.3 us)
Async XLA Ops:
  2.8 17.1 %all-to-all-start = ((bf16[16,128,128]{2,1,0:T(8,128)(2,1)}), bf16[16,128,128]{2,1,0:T(8,128)(2,1)S(1)}, u32[]{:S(2)}, u32[]{:S(2)}) async-start(bf16[16,128,128]{2,1,0:T(8,128)(2,1)} %bitcast.1), calls=%async_computation | async-start | bytes 1048576 | tf_op jit(solution)/shard_map/all_to_all | solution.py:105
  23.2 9.9 %collective-permute-start.1 = (bf16[2,128,256]{2,1,0:T(8,128)(2,1)S(1)}, bf16[2,128,256]{2,1,0:T(8,128)(2,1)S(1)}, u32[]{:S(2)}, u32[]{:S(2)}) collective-permute-start(bf16[2,128,256]{2,1,0:T(8,128)(2,1)S(1)} %pad_maximum_fusion.12), channel_id=1, source_target_pairs={{2,0},{3,1},{4,2},{5,3},{6,4},{7,5},{0,6},{1,7},{10,8},{11,9},{12,... | collective-permute-start | bytes 393224 | tf_op jit(solution)/shard_map/ppermute | solution.py:11
  25.1 8.0 %collective-permute-start.2 = (bf16[2,128,256]{2,1,0:T(8,128)(2,1)S(1)}, bf16[2,128,256]{2,1,0:T(8,128)(2,1)S(1)}, u32[]{:S(2)}, u32[]{:S(2)}) collective-permute-start(bf16[2,128,256]{2,1,0:T(8,128)(2,1)S(1)} %pad_maximum_fusion.12), channel_id=1, source_target_pairs={{4,0},{5,1},{6,2},{7,3},{0,4},{1,5},{2,6},{3,7},{12,8},{13,9},{14,... | collective-permute-start | bytes 393224 | tf_op jit(solution)/shard_map/ppermute | solution.py:11
  25.4 9.1 %collective-permute-start.3 = (bf16[2,128,256]{2,1,0:T(8,128)(2,1)S(1)}, bf16[2,128,256]{2,1,0:T(8,128)(2,1)S(1)}, u32[]{:S(2)}, u32[]{:S(2)}) collective-permute-start(bf16[2,128,256]{2,1,0:T(8,128)(2,1)S(1)} %pad_maximum_fusion.12), channel_id=1, source_target_pairs={{6,0},{7,1},{0,2},{1,3},{2,4},{3,5},{4,6},{5,7},{14,8},{15,9},{8,1... | collective-permute-start | bytes 393224 | tf_op jit(solution)/shard_map/ppermute | solution.py:11
  38.7 15.4 %collective-permute-start.5 = (bf16[2048,128]{1,0:T(8,128)(2,1)S(1)}, bf16[2048,128]{1,0:T(8,128)(2,1)S(1)}, u32[]{:S(2)}, u32[]{:S(2)}) collective-permute-start(bf16[2048,128]{1,0:T(8,128)(2,1)S(1)} %get-tuple-element.119), channel_id=1, source_target_pairs={{0,16},{1,17},{2,18},{3,19},{4,20},{5,21},{6,22},{7,23},{8,24},{9,... | collective-permute-start | bytes 1572872 | tf_op jit(solution)/shard_map/ppermute | solution.py:11
  57.2 25.9 %all-to-all-start.1 = ((bf16[32,128,128]{2,1,0:T(8,128)(2,1)}), bf16[32,128,128]{2,1,0:T(8,128)(2,1)}, u32[]{:S(2)}, u32[]{:S(2)}) async-start(bf16[32,128,128]{2,1,0:T(8,128)(2,1)} %bitcast.428), calls=%async_computation.1 | async-start | bytes 2097152 | tf_op jit(solution)/shard_map/all_to_all | solution.py:105
  94.1 9.1 %collective-permute-start.11 = (bf16[4,128,256]{2,1,0:T(8,128)(2,1)}, bf16[4,128,256]{2,1,0:T(8,128)(2,1)}, u32[]{:S(2)}, u32[]{:S(2)}) collective-permute-start(bf16[4,128,256]{2,1,0:T(8,128)(2,1)} %pad_maximum_fusion.10), channel_id=1, source_target_pairs={{24,0},{7,1},{26,2},{1,3},{28,4},{3,5},{30,6},{5,7},{0,8},{15,9},{... | collective-permute-start | bytes 786440 | tf_op jit(solution)/shard_map/ppermute | solution.py:11
  95.3 7.9 %collective-permute-start.9 = (bf16[4,128,256]{2,1,0:T(8,128)(2,1)}, bf16[4,128,256]{2,1,0:T(8,128)(2,1)}, u32[]{:S(2)}, u32[]{:S(2)}) collective-permute-start(bf16[4,128,256]{2,1,0:T(8,128)(2,1)} %pad_maximum_fusion.10), channel_id=1, source_target_pairs={{8,0},{3,1},{10,2},{5,3},{12,4},{7,5},{14,6},{1,7},{16,8},{11,9},{... | collective-permute-start | bytes 786440 | tf_op jit(solution)/shard_map/ppermute | solution.py:11
  107.0 9.0 %collective-permute-start.12 = (bf16[4,4,128,256]{3,2,0,1:T(8,128)(2,1)}, bf16[4,4,128,256]{3,2,0,1:T(8,128)(2,1)}, u32[]{:S(2)}, u32[]{:S(2)}) collective-permute-start(bf16[4,4,128,256]{3,2,0,1:T(8,128)(2,1)} %pad_maximum_fusion.6), channel_id=1, source_target_pairs={{0,1},{1,0},{2,3},{3,2},{4,5},{5,4},{6,7},{7,6},{8,9},{9,8},{10,11... | collective-permute-start | bytes 3145736 | tf_op jit(solution)/shard_map/ppermute | solution.py:11
  122.2 25.4 %collective-permute-start.13 = (bf16[4096,128]{1,0:T(8,128)(2,1)}, bf16[4096,128]{1,0:T(8,128)(2,1)S(1)}, u32[]{:S(2)}, u32[]{:S(2)}) collective-permute-start(bf16[4096,128]{1,0:T(8,128)(2,1)} %get-tuple-element.123), channel_id=1, source_target_pairs={{0,32},{1,33},{2,34},{3,35},{4,36},{5,37},{6,38},{7,39},{8,40},{9,... | collective-permute-start | bytes 3145736 | tf_op jit(solution)/shard_map/ppermute | solution.py:11
  155.4 33.9 %all-to-all-start.2 = ((bf16[64,128,128]{2,1,0:T(8,128)(2,1)}), bf16[64,128,128]{2,1,0:T(8,128)(2,1)}, u32[]{:S(2)}, u32[]{:S(2)}) async-start(bf16[64,128,128]{2,1,0:T(8,128)(2,1)} %bitcast.410), calls=%async_computation.2 | async-start | bytes 4194304 | tf_op jit(solution)/shard_map/all_to_all | solution.py:105
  201.3 13.6 %collective-permute-start.18 = (bf16[4,2,128,256]{3,2,0,1:T(8,128)(2,1)S(1)}, bf16[4,2,128,256]{3,2,0,1:T(8,128)(2,1)S(1)}, u32[]{:S(2)}, u32[]{:S(2)}) collective-permute-start(bf16[4,2,128,256]{3,2,0,1:T(8,128)(2,1)S(1)} %pad_maximum_fusion.9), channel_id=1, source_target_pairs={{8,0},{3,1},{10,2},{5,3},{12,4},{7,5},{14,6},{1,7},{16,8},{11,9},{... | collective-permute-start | bytes 1572872 | tf_op jit(solution)/shard_map/ppermute | solution.py:11
  203.2 11.7 %collective-permute-start.19 = (bf16[4,2,128,256]{3,2,0,1:T(8,128)(2,1)S(1)}, bf16[4,2,128,256]{3,2,0,1:T(8,128)(2,1)S(1)}, u32[]{:S(2)}, u32[]{:S(2)}) collective-permute-start(bf16[4,2,128,256]{3,2,0,1:T(8,128)(2,1)S(1)} %pad_maximum_fusion.9), channel_id=1, source_target_pairs={{16,0},{5,1},{18,2},{7,3},{20,4},{1,5},{22,6},{3,7},{24,8},{13,9},... | collective-permute-start | bytes 1572872 | tf_op jit(solution)/shard_map/ppermute | solution.py:11
  204.4 14.2 %collective-permute-start.20 = (bf16[4,2,128,256]{3,2,0,1:T(8,128)(2,1)S(1)}, bf16[4,2,128,256]{3,2,0,1:T(8,128)(2,1)S(1)}, u32[]{:S(2)}, u32[]{:S(2)}) collective-permute-start(bf16[4,2,128,256]{3,2,0,1:T(8,128)(2,1)S(1)} %pad_maximum_fusion.9), channel_id=1, source_target_pairs={{24,0},{7,1},{26,2},{1,3},{28,4},{3,5},{30,6},{5,7},{0,8},{15,9},{... | collective-permute-start | bytes 1572872 | tf_op jit(solution)/shard_map/ppermute | solution.py:11
  221.3 11.5 %collective-permute-start.21 = (bf16[4,4,2,128,256]{4,3,1,0,2:T(8,128)(2,1)}, bf16[4,4,2,128,256]{4,3,1,0,2:T(8,128)(2,1)}, u32[]{:S(2)}, u32[]{:S(2)}) collective-permute-start(bf16[4,4,2,128,256]{4,3,1,0,2:T(8,128)(2,1)} %pad_maximum_fusion.4), channel_id=1, source_target_pairs={{0,1},{1,0},{2,3},{3,2},{4,5},{5,4},{6,7},{7,6},{8,9},{9,8},{10,11... | collective-permute-start | bytes 6291464 | tf_op jit(solution)/shard_map/ppermute | solution.py:11
  244.3 49.1 %collective-permute-start.22 = (bf16[8192,128]{1,0:T(8,128)(2,1)}, bf16[8192,128]{1,0:T(8,128)(2,1)S(1)}, u32[]{:S(2)}, u32[]{:S(2)}) collective-permute-start(bf16[8192,128]{1,0:T(8,128)(2,1)} %get-tuple-element.127), channel_id=1, source_target_pairs={{0,64},{1,65},{2,66},{3,67},{4,68},{5,69},{6,70},{7,71},{8,72},{9,... | collective-permute-start | bytes 6291464 | tf_op jit(solution)/shard_map/ppermute | solution.py:11
  323.6 59.4 %all-to-all-start.3 = ((bf16[128,128,128]{2,1,0:T(8,128)(2,1)}), bf16[128,128,128]{2,1,0:T(8,128)(2,1)}, u32[]{:S(2)}, u32[]{:S(2)}) async-start(bf16[128,128,128]{2,1,0:T(8,128)(2,1)} %bitcast.401), calls=%async_computation.3 | async-start | bytes 8388608 | tf_op jit(solution)/shard_map/all_to_all | solution.py:105
  390.0 8.0 %collective-permute-start.26 = (bf16[4,128,256]{2,1,0:T(8,128)(2,1)S(1)}, bf16[4,128,256]{2,1,0:T(8,128)(2,1)S(1)}, u32[]{:S(2)}, u32[]{:S(2)}) collective-permute-start(bf16[4,128,256]{2,1,0:T(8,128)(2,1)S(1)} %pad_maximum_fusion.11), channel_id=1, source_target_pairs={{8,0},{3,1},{10,2},{5,3},{12,4},{7,5},{14,6},{1,7},{16,8},{11,9},{... | collective-permute-start | bytes 786440 | tf_op jit(solution)/shard_map/ppermute | solution.py:11
  391.8 7.1 %collective-permute-start.27 = (bf16[4,128,256]{2,1,0:T(8,128)(2,1)S(1)}, bf16[4,128,256]{2,1,0:T(8,128)(2,1)S(1)}, u32[]{:S(2)}, u32[]{:S(2)}) collective-permute-start(bf16[4,128,256]{2,1,0:T(8,128)(2,1)S(1)} %pad_maximum_fusion.11), channel_id=1, source_target_pairs={{16,0},{5,1},{18,2},{7,3},{20,4},{1,5},{22,6},{3,7},{24,8},{13,9},... | collective-permute-start | bytes 786440 | tf_op jit(solution)/shard_map/ppermute | solution.py:11
  392.5 9.2 %collective-permute-start.28 = (bf16[4,128,256]{2,1,0:T(8,128)(2,1)S(1)}, bf16[4,128,256]{2,1,0:T(8,128)(2,1)S(1)}, u32[]{:S(2)}, u32[]{:S(2)}) collective-permute-start(bf16[4,128,256]{2,1,0:T(8,128)(2,1)S(1)} %pad_maximum_fusion.11), channel_id=1, source_target_pairs={{24,0},{7,1},{26,2},{1,3},{28,4},{3,5},{30,6},{5,7},{0,8},{15,9},{... | collective-permute-start | bytes 786440 | tf_op jit(solution)/shard_map/ppermute | solution.py:11
  403.0 14.3 %collective-permute-start.29 = (bf16[4,4,128,256]{3,2,1,0:T(8,128)(2,1)}, bf16[4,4,128,256]{3,2,1,0:T(8,128)(2,1)S(1)}, u32[]{:S(2)}, u32[]{:S(2)}) collective-permute-start(bf16[4,4,128,256]{3,2,1,0:T(8,128)(2,1)} %pad_maximum_fusion.7), channel_id=1, source_target_pairs={{32,0},{9,1},{34,2},{11,3},{36,4},{13,5},{38,6},{15,7},{40,8},{17,... | collective-permute-start | bytes 3145736 | tf_op jit(solution)/shard_map/ppermute | solution.py:11
  403.9 15.7 %collective-permute-start.30 = (bf16[4,4,128,256]{3,2,1,0:T(8,128)(2,1)}, bf16[4,4,128,256]{3,2,1,0:T(8,128)(2,1)S(1)}, u32[]{:S(2)}, u32[]{:S(2)}) collective-permute-start(bf16[4,4,128,256]{3,2,1,0:T(8,128)(2,1)} %pad_maximum_fusion.7), channel_id=1, source_target_pairs={{64,0},{17,1},{66,2},{19,3},{68,4},{21,5},{70,6},{23,7},{72,8},{25... | collective-permute-start | bytes 3145736 | tf_op jit(solution)/shard_map/ppermute | solution.py:11
  404.4 26.6 %collective-permute-start.31 = (bf16[4,4,128,256]{3,2,1,0:T(8,128)(2,1)}, bf16[4,4,128,256]{3,2,1,0:T(8,128)(2,1)}, u32[]{:S(2)}, u32[]{:S(2)}) collective-permute-start(bf16[4,4,128,256]{3,2,1,0:T(8,128)(2,1)} %pad_maximum_fusion.7), channel_id=1, source_target_pairs={{96,0},{25,1},{98,2},{27,3},{100,4},{29,5},{102,6},{31,7},{104,8},... | collective-permute-start | bytes 3145736 | tf_op jit(solution)/shard_map/ppermute | solution.py:11
  437.8 21.3 %collective-permute-start.32 = (bf16[4,4,4,128,256]{4,3,2,1,0:T(8,128)(2,1)}, bf16[4,4,4,128,256]{4,3,2,1,0:T(8,128)(2,1)}, u32[]{:S(2)}, u32[]{:S(2)}) collective-permute-start(bf16[4,4,4,128,256]{4,3,2,1,0:T(8,128)(2,1)} %pad_maximum_fusion.2), channel_id=1, source_target_pairs={{0,1},{1,0},{2,3},{3,2},{4,5},{5,4},{6,7},{7,6},{8,9},{9,8},{10,11... | collective-permute-start | bytes 12582920 | tf_op jit(solution)/shard_map/ppermute | solution.py:11
  (68 other events, 895.8 us)

commit v2 on v1

v2 whole, which is shorter than its diff:
```python
import functools

import jax
import jax.numpy as jnp
from jax import lax
from jax.experimental import pallas as pl
from jax.experimental.pallas import tpu as pltpu
from jax.sharding import PartitionSpec as P

AXIS = "cube"
SHIFT = {"y": 5, "z": 3, "x": 1}


def permute(array, pairs):
    return lax.ppermute(array, AXIS, pairs)


def moved(device, axis, count, step):
    shift = SHIFT[axis]
    position = (device >> shift) & (count - 1)
    return device - (position << shift) + (((position + step) % count) << shift)


STAGES = (
    ((("z", "z"), 2), (("x", "x"), 4)),
    ((("x", "z"), 4), (("z", "x"), 4)),
    ((("y", "y"), 2), (("x", "z"), 4), (("z", "x"), 4)),
    ((("x", "y"), 4), (("z", "x"), 4), (("y", "z"), 4)),
)


def axis_position(device, axis, count):
    return (device >> SHIFT[axis]) & (count - 1)


def gather_pieces(block, axes, count):
    devices = lax.axis_size(AXIS)
    pieces = [block]
    for step in range(1, count):
        pieces.append(permute(block, [(moved(i, axes[i & 1], count, step), i) for i in range(devices)]))
    return pieces


def gather_stage(block, device, axes, count):
    pieces = gather_pieces(block, axes, count)
    position = jnp.where(
        device & 1 == 0, axis_position(device, axes[0], count), axis_position(device, axes[1], count)
    )
    placed = []
    for spot in range(count):
        which = jnp.bitwise_and(spot - position, count - 1)
        if count == 2:
            placed.append(jnp.where(which == 0, pieces[0], pieces[1]))
        else:
            placed.append(lax.select_n(which, *pieces))
    return jnp.concatenate(placed, 0)


def gather_rows(block, device, tier_num):
    devices = lax.axis_size(AXIS)
    stages = STAGES[tier_num]
    half = block[None]
    for axes, count in stages[:-1]:
        half = gather_stage(half, device, axes, count)
    axes, count = stages[-1]
    pieces = gather_pieces(half, axes, count)
    others = [permute(piece, [(i, i ^ 1) for i in range(devices)]) for piece in pieces]
    return pieces, others


def place_of(tier_num, groups, r):
    places = []
    for core in range(2):
        place, scale = 0, 1
        for axes, count in STAGES[tier_num]:
            place = place + axis_position(r, axes[core], count) * scale
            scale *= count
        places.append(place + core * (groups // 2))
    return jnp.where(r & 1 == 0, places[0], places[1])


ROLE_NONE, ROLE_FIRST, ROLE_SECOND = 0, 1, 2


def tier_kernel(tier_num, groups, width, span, count, info, column_any, column_ref, *refs):
    pieces, (final_ref, kept_ref, panel, band, bands_in, sems, band_sems) = (
        refs[: 2 * count],
        refs[2 * count :],
    )
    first, second, role, core = info[0], info[1], info[2], info[3]
    place = functools.partial(place_of, tier_num, groups)
    chunk = pl.program_id(0)
    part = groups // (2 * count)
    zero = jnp.zeros((width, width), jnp.bfloat16)

    @pl.when(chunk == 0)
    def _():
        copies = []
        for side in range(2):
            holder = core if side == 0 else 1 - core
            position = jnp.where(holder == 0, info[4], info[5])
            for step in range(count):
                slot = holder * (groups // 2) + ((position + step) & (count - 1)) * part
                copies.append(
                    pltpu.make_async_copy(
                        pieces[side * count + step],
                        panel.at[pl.ds(slot, part)],
                        sems.at[side * count + step],
                    )
                )
        for which, block in ((0, first), (1, second)):
            copies.append(
                pltpu.make_async_copy(
                    column_any.at[pl.ds(pl.multiple_of(block * width, width), width)],
                    bands_in.at[which],
                    band_sems.at[which],
                )
            )
        for copy in copies:
            copy.start()
        for copy in copies:
            copy.wait()
        at_first, at_second = place(first), place(second)
        top = panel[at_first, :, width:]

        def scale_rows(i, carry):
            both = panel[pl.ds(i * span, span)].reshape(span * width, 2 * width)
            change = jnp.dot(both[:, :width], top, preferred_element_type=jnp.float32)
            fixed = (both[:, width:].astype(jnp.float32) - change).astype(jnp.bfloat16)
            panel[pl.ds(i * span, span), :, width:] = fixed.reshape(span, width, width)
            return carry

        lax.fori_loop(0, groups // span, scale_rows, 0)
        panel[at_first, :, width:] = top
        lower = bands_in[1].astype(jnp.float32) - jnp.dot(
            panel[at_second, :, :width], bands_in[0], preferred_element_type=jnp.float32
        )
        band[:width] = bands_in[0]
        band[width:] = lower.astype(jnp.bfloat16)

        @pl.when(role == ROLE_NONE)
        def _():
            panel[at_first, :, :width] = zero
            panel[at_first, :, width:] = zero
            panel[at_second, :, width:] = zero

    for j in range(span):
        r = chunk * span + j
        rows = pl.ds(j * width, width)
        at = place(r)

        @pl.when(role == ROLE_NONE)
        def _():
            update = jnp.dot(panel[at], band[...], preferred_element_type=jnp.float32)
            value = column_ref[rows].astype(jnp.float32) - update
            final_ref[rows] = value
            if kept_ref is not None:
                value = jnp.where((r == first) | (r == second), 0.0, value)
                kept_ref[rows] = value.astype(jnp.bfloat16)

        @pl.when(role == ROLE_FIRST)
        def _():
            final_ref[rows] = panel[at, :, :width].astype(jnp.float32)

        @pl.when(role == ROLE_SECOND)
        def _():
            final_ref[rows] = panel[at, :, width:].astype(jnp.float32)

        if kept_ref is not None:

            @pl.when(role != ROLE_NONE)
            def _():
                kept_ref[rows] = zero


def eliminate(tier_num, column, pieces, others, info, keep):
    rows, width = column.shape
    groups = rows // width
    count = len(pieces)
    span = min(8, groups)
    block = pl.BlockSpec((span * width, width), lambda i, info: (i, 0))
    anywhere = pl.BlockSpec(memory_space=pl.ANY)
    body = functools.partial(tier_kernel, tier_num, groups, width, span, count)
    if not keep:
        inner = body

        def body(info, column_any, column_ref, *refs):
            at = 2 * count + 1
            inner(info, column_any, column_ref, *refs[:at], None, *refs[at:])

    out_shape = [jax.ShapeDtypeStruct((rows, width), jnp.float32)]
    if keep:
        out_shape.append(jax.ShapeDtypeStruct((rows, width), jnp.bfloat16))
    return pl.pallas_call(
        body,
        grid_spec=pltpu.PrefetchScalarGridSpec(
            num_scalar_prefetch=1,
            grid=(groups // span,),
            in_specs=[anywhere, block] + [anywhere] * (2 * count),
            out_specs=[block] * len(out_shape),
            scratch_shapes=[
                pltpu.VMEM((groups, width, 2 * width), jnp.bfloat16),
                pltpu.VMEM((2 * width, width), jnp.bfloat16),
                pltpu.VMEM((2, width, width), jnp.bfloat16),
                pltpu.SemaphoreType.DMA((2 * count,)),
                pltpu.SemaphoreType.DMA((2,)),
            ],
        ),
        out_shape=out_shape,
        compiler_params=pltpu.CompilerParams(vmem_limit_bytes=32 * 1024 * 1024),
        cost_estimate=pl.CostEstimate(
            flops=6 * rows * width * width, bytes_accessed=12 * rows * width, transcendentals=0
        ),
    )(info, column, column, *pieces, *others)


def shards(
    front_leaf,
    front_lower,
    front_upper,
    front_root,
    inv_leaf,
    inv_lower,
    inv_upper,
    inv_root,
    pivots_leaf,
    pivots_lower,
    pivots_upper,
    pivots_root,
    child_sides,
):
    fronts = (front_leaf, front_lower, front_upper, front_root)
    inverses = (inv_leaf, inv_lower, inv_upper, inv_root)
    tables = (pivots_leaf, pivots_lower, pivots_upper, pivots_root)
    device = lax.axis_index(AXIS)
    devices = lax.axis_size(AXIS)
    width = front_leaf.shape[1]
    column = front_leaf
    results = []
    for tier_num in range(4):
        groups = fronts[tier_num].shape[0] // width
        front_num = device // groups
        local = device % groups
        teams = [list(range(i, i + groups)) for i in range(0, devices, groups)]
        table = tables[tier_num]
        pivot_row = lax.dynamic_index_in_dim(table, front_num, 0, keepdims=False)
        first, second = pivot_row[0], pivot_row[1]
        is_first, is_second = local == first, local == second

        scaled = jnp.dot(column, inverses[tier_num], preferred_element_type=jnp.float32)
        scaled = scaled.astype(jnp.bfloat16)
        rows = lax.all_to_all(
            scaled.reshape(groups, width, width), AXIS, 0, 0, axis_index_groups=teams, tiled=True
        )
        own = jnp.concatenate(
            [
                lax.dynamic_index_in_dim(rows, first, 0, keepdims=False),
                lax.dynamic_index_in_dim(rows, second, 0, keepdims=False),
            ],
            1,
        )
        pieces, others = gather_rows(own, device, tier_num)
        axes, count = STAGES[tier_num][-1]
        role = jnp.where(is_first, ROLE_FIRST, jnp.where(is_second, ROLE_SECOND, ROLE_NONE))
        info = jnp.stack(
            [
                first,
                second,
                role,
                device & 1,
                axis_position(device, axes[0], count),
                axis_position(device, axes[1], count),
            ]
        ).astype(jnp.int32)
        made = eliminate(tier_num, column, pieces, others, info, tier_num < 3)
        results.append(made[0])
        if tier_num < 3:
            kept = made[1]
            received = permute(kept, [(i, i ^ groups) for i in range(devices)])
            blocks = jnp.arange(groups, dtype=jnp.int32)
            side_row = child_sides[tier_num]
            parent_half = (device // groups) & 1
            total = fronts[tier_num + 1].reshape(2, groups, width, width).astype(jnp.float32)
            halves = jnp.arange(2, dtype=jnp.int32)
            for part, flip in ((kept.reshape(groups, width, width), 0), (received.reshape(groups, width, width), 1)):
                front_of = front_num ^ flip
                sides = lax.dynamic_slice_in_dim(side_row, front_of * groups, groups, 0)
                own_side = lax.dynamic_index_in_dim(
                    side_row, front_of * groups + local, 0, keepdims=False
                )
                keep = (sides[None, :] == halves[:, None]) & (own_side == parent_half)
                total = total + jnp.where(
                    keep[:, :, None, None], part[None].astype(jnp.float32), 0.0
                )
            column = total.astype(jnp.bfloat16).reshape(-1, width)
    return tuple(results)


def solution(mesh):
    across, down, whole = P(None, AXIS), P(AXIS, None), P()
    return jax.shard_map(
        shards,
        mesh=mesh,
        in_specs=(across,) * 4 + (down,) * 4 + (whole,) * 5,
        out_specs=(across,) * 4,
        check_vma=False,
    )
```

time: 558 us -> 447 us (0.80); the launches traced: 547 us -> 445 us
  other arithmetic: 90 us -> 16.9 us
  local copies, waits for them, and re-layouts: 89.5 us -> 20.2 us
  Pallas kernels: 0 us -> 57.2 us
  matrix products: 41.6 us -> 9 us
  starting transfers between devices: 71.2 us -> 98.6 us
  between operations: 34.6 us -> 25.8 us
    pallas_call x0 -> x4, Pallas kernels: none -> 57.2 us  [eliminate(): pl.pallas_call(body, grid_spec=pltpu.PrefetchScalarGridSpec(num_scalar_pr...]
    dot_general x12 -> x0, matrix products: 32.6 us -> none  [the longest x4 17.6 us: shards(): change1 = jnp.dot(masked0, top1, preferred_element_type=jnp.float32)]
    convert_element_type x4 -> x0, local copies, waits for them, and re-layouts: 28.4 us -> none  [the longest x1 9.05 us: shards(): factor0.reshape(-1, width).astype(jnp.float32)]
    ppermute x33 -> x45, starting transfers between devices: 42.9 us -> 66.5 us  [permute(): return lax.ppermute(array, AXIS, pairs)]
    another operation x32 -> x0, other arithmetic: 22.6 us -> none  [the longest x28 15.6 us: gather_stage(): return jnp.stack(placed, 0)]
    convert_element_type x6 -> x3, other arithmetic: 31.6 us -> 12.7 us  [shards(): column = total.astype(jnp.bfloat16).reshape(-1, width)]
    unnamed x112 -> x36, local copies, waits for them, and re-layouts: 23.1 us -> 8.23 us
    select_n x5 -> x10, other arithmetic: 12.9 us -> 0.51 us  [the longest x8 0.46 us: gather_stage(): placed.append(lax.select_n(which, *pieces))]
  transfers between devices with their start and end apart: 37 -> 49, of which waited for: 29 -> 21; matrix products, arithmetic and copies ran while one was open for 9% -> 3% of each run, Pallas kernels for 0% -> 0%
where the time goes in v2:
time: 447 us; the launch traced here: 445 us
  waiting for transfers between devices  218 us (49%)
  starting transfers between devices  98.6 us (22%)
  Pallas kernels  57.2 us (13%)
  between operations  25.8 us (6%)
  local copies, waits for them, and re-layouts  20.2 us (5%)
  other arithmetic  16.9 us (4%)
  matrix products  9 us (2%)
    ppermute x45, waiting for transfers between devices, permute(): return lax.ppermute(array, AXIS, pairs)  129 us
    all_to_all x4, waiting for transfers between devices, shards(): lax.all_to_all(scaled.reshape(groups, width, width), AXIS, 0, 0, axis_ind...  89.2 us
    ppermute x45, starting transfers between devices, permute(): return lax.ppermute(array, AXIS, pairs)  66.5 us
    pallas_call x4, Pallas kernels, eliminate(): pl.pallas_call(body, grid_spec=pltpu.PrefetchScalarGridSpec(num_scalar_pr...  57.2 us
    all_to_all x4, starting transfers between devices, shards(): lax.all_to_all(scaled.reshape(groups, width, width), AXIS, 0, 0, axis_ind...  32.1 us
    convert_element_type x3, other arithmetic, shards(): column = total.astype(jnp.bfloat16).reshape(-1, width)  12.7 us
    dot_general x4, matrix products, shards(): jnp.dot(column, inverses[tier_num], preferred_element_type=jnp.float32)  9 us
  transfers between devices with their start and end apart: 49, of which 21 were waited for; matrix products, arithmetic and copies ran while one was open for 3% of the time, Pallas kernels for 0%

profile of v2, /device:TPU:1, one launch (start us, length us, event | category | flops | bytes accessed | tf_op | source)
XLA Modules:
  0.0 445.4 jit_solution(9720345424780475765)
XLA Ops:
  2.9 7.2 %all-to-all-start = ((bf16[16,128,128]{2,1,0:T(8,128)(2,1)}), bf16[16,128,128]{2,1,0:T(8,128)(2,1)S(1)}, u32[]{:S(2)}, u32[]{:S(2)}) async-start(bf16[16,128,128]{2,1,0:T(8,128)(2,1)} %bitcast.7), calls=%async_computation | async-start | bytes 1048576 | tf_op jit(solution)/shard_map/all_to_all | solution.py:252
  15.2 4.7 %all-to-all-done = bf16[16,128,128]{2,1,0:T(8,128)(2,1)S(1)} async-done(((bf16[16,128,128]{2,1,0:T(8,128)(2,1)}), bf16[16,128,128]{2,1,0:T(8,128)(2,1)S(1)}, u32[]{:S(2)}, u32[]{:S(2)}) %all-to-all-start) | async-done | bytes 524320 | tf_op jit(solution)/shard_map/all_to_all | solution.py:252
  28.7 5.4 %collective-permute-start.7 = (bf16[2,128,256]{2,1,0:T(8,128)(2,1)S(1)}, bf16[2,128,256]{2,1,0:T(8,128)(2,1)S(1)}, u32[]{:S(2)}, u32[]{:S(2)}) collective-permute-start(bf16[2,128,256]{2,1,0:T(8,128)(2,1)S(1)} %collective-permute-done.3.refs_3_), channel_id=1, source_target_pairs={{0,1},{1,0},{2,3},{3,2},{4,5},{5,4},{6,7},{7,6},{8,9},{9,8},{10,11... | collective-permute-start | bytes 393224 | tf_op jit(solution)/shard_map/ppermute | solution.py:15
  38.4 6.1 %shard_map.156 = (f32[2048,128]{1,0:T(8,128)}, bf16[2048,128]{1,0:T(8,128)(2,1)S(1)}) custom-call(s32[6]{0:T(128)S(1)} %stack.47.info, bf16[2048,128]{1,0:T(8,128)(2,1)S(1)} %copy-done.3, bf16[2048,128]{1,0:T(8,128)(2,1)S(1)} %copy-done.3, bf16[2,128,256]{2,1,0:T(8,128)(2,1)S(1)} %pad_maximum_fusion.4.refs_0_, ...), custom_call_target="tpu_custom_call" | custom-call | flops 201326592 | bytes 3145728 | tf_op jit(solution)/shard_map/pallas_call | solution.py:194
  50.0 10.1 %collective-permute-done.8 = bf16[2048,128]{1,0:T(8,128)(2,1)S(1)} collective-permute-done((bf16[2048,128]{1,0:T(8,128)(2,1)S(1)}, bf16[2048,128]{1,0:T(8,128)(2,1)S(1)}, u32[]{:S(2)}, u32[]{:S(2)}) %collective-permute-start.8) | collective-permute-done | bytes 524320 | tf_op jit(solution)/shard_map/ppermute | solution.py:15
  63.2 6.6 %all-to-all-start.1 = ((bf16[32,128,128]{2,1,0:T(8,128)(2,1)}), bf16[32,128,128]{2,1,0:T(8,128)(2,1)S(1)}, u32[]{:S(2)}, u32[]{:S(2)}) async-start(bf16[32,128,128]{2,1,0:T(8,128)(2,1)} %bitcast.27), calls=%async_computation.1 | async-start | bytes 2097152 | tf_op jit(solution)/shard_map/all_to_all | solution.py:252
  74.3 12.7 %all-to-all-done.1 = bf16[32,128,128]{2,1,0:T(8,128)(2,1)S(1)} async-done(((bf16[32,128,128]{2,1,0:T(8,128)(2,1)}), bf16[32,128,128]{2,1,0:T(8,128)(2,1)S(1)}, u32[]{:S(2)}, u32[]{:S(2)}) %all-to-all-start.1) | async-done | bytes 1048608 | tf_op jit(solution)/shard_map/all_to_all | solution.py:252
  98.0 4.5 %collective-permute-done.14.refs_3_ = bf16[4,128,256]{2,1,0:T(8,128)(2,1)S(1)} collective-permute-done((bf16[4,128,256]{2,1,0:T(8,128)(2,1)S(1)}, bf16[4,128,256]{2,1,0:T(8,128)(2,1)S(1)}, u32[]{:S(2)}, u32[]{:S(2)}) %collective-permute-start.14) | collective-permute-done | bytes 262176 | tf_op jit(solution)/shard_map/ppermute | solution.py:15
  113.4 7.8 %shard_map.157 = (f32[4096,128]{1,0:T(8,128)}, bf16[4096,128]{1,0:T(8,128)(2,1)S(1)}) custom-call(s32[6]{0:T(128)S(1)} %stack.50.info, bf16[4096,128]{1,0:T(8,128)(2,1)S(1)} %fusion.7.column_any.column_ref, bf16[4096,128]{1,0:T(8,128)(2,1)S(1)} %fusion.7.column_any.column_ref, bf16[4,128,256]{2,1,0:T(8,128)(2,1)S(1)} %pad_maximum_fusion.2.refs_0_, ...), custom_call_target="tpu_custom_call" | custom-call | flops 402653184 | bytes 6291456 | tf_op jit(solution)/shard_map/pallas_call | solution.py:194
  124.2 21.9 %collective-permute-done.19 = bf16[4096,128]{1,0:T(8,128)(2,1)S(1)} collective-permute-done((bf16[4096,128]{1,0:T(8,128)(2,1)S(1)}, bf16[4096,128]{1,0:T(8,128)(2,1)S(1)}, u32[]{:S(2)}, u32[]{:S(2)}) %collective-permute-start.19) | collective-permute-done | bytes 1048608 | tf_op jit(solution)/shard_map/ppermute | solution.py:15
  146.5 5.6 %fusion.4.column_any.column_ref = bf16[8192,128]{1,0:T(8,128)(2,1)S(1)} fusion(bf16[8192,128]{1,0:T(8,128)(2,1)} %param.15, f32[32,128,128]{2,1,0:T(8,128)S(1)} %convert.9, f32[32,128,128]{2,1,0:T(8,128)S(1)} %convert.8, pred[8192]{0:T(1024)(128)(4,1)S(1)} %bitcast.165, pred[8192]{0:T(1024)(128)(4,1)S(1)} %bitcast.166), kind=kLoop, calls=%fused_computation.10 | loop fusion | flops 6291456 | bytes 8404992 | tf_op jit(solution)/shard_map/convert_element_type | solution.py:295
  154.1 8.6 %all-to-all-start.2 = ((bf16[64,128,128]{2,1,0:T(8,128)(2,1)}), bf16[64,128,128]{2,1,0:T(8,128)(2,1)}, u32[]{:S(2)}, u32[]{:S(2)}) async-start(bf16[64,128,128]{2,1,0:T(8,128)(2,1)} %bitcast.159), calls=%async_computation.2 | async-start | bytes 4194304 | tf_op jit(solution)/shard_map/all_to_all | solution.py:252
  167.3 23.5 %all-to-all-done.2 = bf16[64,128,128]{2,1,0:T(8,128)(2,1)} async-done(((bf16[64,128,128]{2,1,0:T(8,128)(2,1)}), bf16[64,128,128]{2,1,0:T(8,128)(2,1)}, u32[]{:S(2)}, u32[]{:S(2)}) %all-to-all-start.2) | async-done | bytes 2097184 | tf_op jit(solution)/shard_map/all_to_all | solution.py:252
  209.5 8.8 %collective-permute-done.26.refs_3_ = bf16[8,128,256]{2,1,0:T(8,128)(2,1)S(1)} collective-permute-done((bf16[8,128,256]{2,1,0:T(8,128)(2,1)S(1)}, bf16[8,128,256]{2,1,0:T(8,128)(2,1)S(1)}, u32[]{:S(2)}, u32[]{:S(2)}) %collective-permute-start.26) | collective-permute-done | bytes 524320 | tf_op jit(solution)/shard_map/ppermute | solution.py:15
  225.5 15.5 %shard_map.158 = (f32[8192,128]{1,0:T(8,128)}, bf16[8192,128]{1,0:T(8,128)(2,1)}) custom-call(s32[6]{0:T(128)S(1)} %stack.52.info, bf16[8192,128]{1,0:T(8,128)(2,1)S(1)} %fusion.4.column_any.column_ref, bf16[8192,128]{1,0:T(8,128)(2,1)S(1)} %fusion.4.column_any.column_ref, bf16[8,128,256]{2,1,0:T(8,128)(2,1)S(1)} %pad_maximum_fusion.1.refs_0_, ...), custom_call_target="tpu_custom_call" | custom-call | flops 805306368 | bytes 12582912 | tf_op jit(solution)/shard_map/pallas_call | solution.py:194
  247.8 42.8 %collective-permute-done.31 = bf16[8192,128]{1,0:T(8,128)(2,1)S(1)} collective-permute-done((bf16[8192,128]{1,0:T(8,128)(2,1)}, bf16[8192,128]{1,0:T(8,128)(2,1)S(1)}, u32[]{:S(2)}, u32[]{:S(2)}) %collective-permute-start.31) | collective-permute-done | bytes 2097184 | tf_op jit(solution)/shard_map/ppermute | solution.py:15
  291.3 5.7 %fusion.1.column_any.column_ref = bf16[16384,128]{1,0:T(8,128)(2,1)S(1)} fusion(bf16[16384,128]{1,0:T(8,128)(2,1)S(1)} %copy-done.10, f32[64,128,128]{2,1,0:T(8,128)S(1)} %convert.11, f32[64,128,128]{2,1,0:T(8,128)S(1)} %convert.10, pred[16384]{0:T(1024)(128)(4,1)S(1)} %bitcast.163, pred[16384]{0:T(1024)(128)(4,1)S(1)} %bitcast.164), kind=kLoop, calls=%fused_computation.4 | loop fusion | flops 12582912 | bytes 16809984 | tf_op jit(solution)/shard_map/convert_element_type | solution.py:295
  300.4 9.8 %all-to-all-start.3 = ((bf16[128,128,128]{2,1,0:T(8,128)(2,1)}), bf16[128,128,128]{2,1,0:T(8,128)(2,1)}, u32[]{:S(2)}, u32[]{:S(2)}) async-start(bf16[128,128,128]{2,1,0:T(8,128)(2,1)} %bitcast.158), calls=%async_computation.3 | async-start | bytes 8388608 | tf_op jit(solution)/shard_map/all_to_all | solution.py:252
  314.5 48.3 %all-to-all-done.3 = bf16[128,128,128]{2,1,0:T(8,128)(2,1)} async-done(((bf16[128,128,128]{2,1,0:T(8,128)(2,1)}), bf16[128,128,128]{2,1,0:T(8,128)(2,1)}, u32[]{:S(2)}, u32[]{:S(2)}) %all-to-all-start.3) | async-done | bytes 4194336 | tf_op jit(solution)/shard_map/all_to_all | solution.py:252
  372.7 3.9 collective-permute-done.36
  382.5 4.4 collective-permute-start.41
  386.9 19.3 %collective-permute-done.40.refs_3_ = bf16[16,128,256]{2,1,0:T(8,128)(2,1)S(1)} collective-permute-done((bf16[16,128,256]{2,1,0:T(8,128)(2,1)S(1)}, bf16[16,128,256]{2,1,0:T(8,128)(2,1)S(1)}, u32[]{:S(2)}, u32[]{:S(2)}) %collective-permute-start.40) | collective-permute-done | bytes 1048608 | tf_op jit(solution)/shard_map/ppermute | solution.py:15
  406.2 3.5 collective-permute-start.44
  417.5 27.8 %shard_map.159 = f32[16384,128]{1,0:T(8,128)} custom-call(s32[6]{0:T(128)S(1)} %stack.55.info, bf16[16384,128]{1,0:T(8,128)(2,1)S(1)} %copy-done.2, bf16[16384,128]{1,0:T(8,128)(2,1)S(1)} %copy-done.2, bf16[16,128,256]{2,1,0:T(8,128)(2,1)S(1)} %pad_maximum_fusion.refs_0_, bf16[16,128,256]{2,1,0:T(8,128)(2,1)} %collective-permute-done.38.refs_1_, ...), custom_call_target="tpu_custom_call" | custom-call | flops 1610612736 | bytes 25165824 | tf_op jit(solution)/shard_map/pallas_call | solution.py:194
  (179 shorter events, 105.2 us)
Async XLA Ops:
  2.9 17.1 %all-to-all-start = ((bf16[16,128,128]{2,1,0:T(8,128)(2,1)}), bf16[16,128,128]{2,1,0:T(8,128)(2,1)S(1)}, u32[]{:S(2)}, u32[]{:S(2)}) async-start(bf16[16,128,128]{2,1,0:T(8,128)(2,1)} %bitcast.7), calls=%async_computation | async-start | bytes 1048576 | tf_op jit(solution)/shard_map/all_to_all | solution.py:252
  23.6 10.5 %collective-permute-start.2 = (bf16[2,128,256]{2,1,0:T(8,128)(2,1)S(1)}, bf16[2,128,256]{2,1,0:T(8,128)(2,1)S(1)}, u32[]{:S(2)}, u32[]{:S(2)}) collective-permute-start(bf16[2,128,256]{2,1,0:T(8,128)(2,1)S(1)} %pad_maximum_fusion.4.refs_0_), channel_id=1, source_target_pairs={{4,0},{5,1},{6,2},{7,3},{0,4},{1,5},{2,6},{3,7},{12,8},{13,9},{14,... | collective-permute-start | bytes 393224 | tf_op jit(solution)/shard_map/ppermute | solution.py:15
  26.3 7.8 %collective-permute-start.1 = (bf16[2,128,256]{2,1,0:T(8,128)(2,1)S(1)}, bf16[2,128,256]{2,1,0:T(8,128)(2,1)S(1)}, u32[]{:S(2)}, u32[]{:S(2)}) collective-permute-start(bf16[2,128,256]{2,1,0:T(8,128)(2,1)S(1)} %pad_maximum_fusion.4.refs_0_), channel_id=1, source_target_pairs={{2,0},{3,1},{4,2},{5,3},{6,4},{7,5},{0,6},{1,7},{10,8},{11,9},{12,... | collective-permute-start | bytes 393224 | tf_op jit(solution)/shard_map/ppermute | solution.py:15
  27.0 10.3 %collective-permute-start.4 = (bf16[2,128,256]{2,1,0:T(8,128)(2,1)S(1)}, bf16[2,128,256]{2,1,0:T(8,128)(2,1)S(1)}, u32[]{:S(2)}, u32[]{:S(2)}) collective-permute-start(bf16[2,128,256]{2,1,0:T(8,128)(2,1)S(1)} %pad_maximum_fusion.4.refs_0_), channel_id=1, source_target_pairs={{0,1},{1,0},{2,3},{3,2},{4,5},{5,4},{6,7},{7,6},{8,9},{9,8},{10,11... | collective-permute-start | bytes 393224 | tf_op jit(solution)/shard_map/ppermute | solution.py:15
  28.7 8.6 %collective-permute-start.7 = (bf16[2,128,256]{2,1,0:T(8,128)(2,1)S(1)}, bf16[2,128,256]{2,1,0:T(8,128)(2,1)S(1)}, u32[]{:S(2)}, u32[]{:S(2)}) collective-permute-start(bf16[2,128,256]{2,1,0:T(8,128)(2,1)S(1)} %collective-permute-done.3.refs_3_), channel_id=1, source_target_pairs={{0,1},{1,0},{2,3},{3,2},{4,5},{5,4},{6,7},{7,6},{8,9},{9,8},{10,11... | collective-permute-start | bytes 393224 | tf_op jit(solution)/shard_map/ppermute | solution.py:15
  44.5 15.6 %collective-permute-start.8 = (bf16[2048,128]{1,0:T(8,128)(2,1)S(1)}, bf16[2048,128]{1,0:T(8,128)(2,1)S(1)}, u32[]{:S(2)}, u32[]{:S(2)}) collective-permute-start(bf16[2048,128]{1,0:T(8,128)(2,1)S(1)} %get-tuple-element.11), channel_id=1, source_target_pairs={{0,16},{1,17},{2,18},{3,19},{4,20},{5,21},{6,22},{7,23},{8,24},{9,... | collective-permute-start | bytes 1572872 | tf_op jit(solution)/shard_map/ppermute | solution.py:15
  63.2 23.7 %all-to-all-start.1 = ((bf16[32,128,128]{2,1,0:T(8,128)(2,1)}), bf16[32,128,128]{2,1,0:T(8,128)(2,1)S(1)}, u32[]{:S(2)}, u32[]{:S(2)}) async-start(bf16[32,128,128]{2,1,0:T(8,128)(2,1)} %bitcast.27), calls=%async_computation.1 | async-start | bytes 2097152 | tf_op jit(solution)/shard_map/all_to_all | solution.py:252
  92.9 9.6 %collective-permute-start.14 = (bf16[4,128,256]{2,1,0:T(8,128)(2,1)S(1)}, bf16[4,128,256]{2,1,0:T(8,128)(2,1)S(1)}, u32[]{:S(2)}, u32[]{:S(2)}) collective-permute-start(bf16[4,128,256]{2,1,0:T(8,128)(2,1)S(1)} %pad_maximum_fusion.2.refs_0_), channel_id=1, source_target_pairs={{24,0},{7,1},{26,2},{1,3},{28,4},{3,5},{30,6},{5,7},{0,8},{15,9},{... | collective-permute-start | bytes 786440 | tf_op jit(solution)/shard_map/ppermute | solution.py:15
  93.4 11.5 %collective-permute-start.13 = (bf16[4,128,256]{2,1,0:T(8,128)(2,1)S(1)}, bf16[4,128,256]{2,1,0:T(8,128)(2,1)S(1)}, u32[]{:S(2)}, u32[]{:S(2)}) collective-permute-start(bf16[4,128,256]{2,1,0:T(8,128)(2,1)S(1)} %pad_maximum_fusion.2.refs_0_), channel_id=1, source_target_pairs={{16,0},{5,1},{18,2},{7,3},{20,4},{1,5},{22,6},{3,7},{24,8},{13,9},... | collective-permute-start | bytes 786440 | tf_op jit(solution)/shard_map/ppermute | solution.py:15
  95.1 9.8 %collective-permute-start.12 = (bf16[4,128,256]{2,1,0:T(8,128)(2,1)S(1)}, bf16[4,128,256]{2,1,0:T(8,128)(2,1)S(1)}, u32[]{:S(2)}, u32[]{:S(2)}) collective-permute-start(bf16[4,128,256]{2,1,0:T(8,128)(2,1)S(1)} %pad_maximum_fusion.2.refs_0_), channel_id=1, source_target_pairs={{8,0},{3,1},{10,2},{5,3},{12,4},{7,5},{14,6},{1,7},{16,8},{11,9},{... | collective-permute-start | bytes 786440 | tf_op jit(solution)/shard_map/ppermute | solution.py:15
  95.9 12.6 %collective-permute-start.15 = (bf16[4,128,256]{2,1,0:T(8,128)(2,1)S(1)}, bf16[4,128,256]{2,1,0:T(8,128)(2,1)S(1)}, u32[]{:S(2)}, u32[]{:S(2)}) collective-permute-start(bf16[4,128,256]{2,1,0:T(8,128)(2,1)S(1)} %pad_maximum_fusion.2.refs_0_), channel_id=1, source_target_pairs={{0,1},{1,0},{2,3},{3,2},{4,5},{5,4},{6,7},{7,6},{8,9},{9,8},{10,11... | collective-permute-start | bytes 786440 | tf_op jit(solution)/shard_map/ppermute | solution.py:15
  121.2 24.9 %collective-permute-start.19 = (bf16[4096,128]{1,0:T(8,128)(2,1)S(1)}, bf16[4096,128]{1,0:T(8,128)(2,1)S(1)}, u32[]{:S(2)}, u32[]{:S(2)}) collective-permute-start(bf16[4096,128]{1,0:T(8,128)(2,1)S(1)} %get-tuple-element.13), channel_id=1, source_target_pairs={{0,32},{1,33},{2,34},{3,35},{4,36},{5,37},{6,38},{7,39},{8,40},{9,... | collective-permute-start | bytes 3145736 | tf_op jit(solution)/shard_map/ppermute | solution.py:15
  154.1 36.6 %all-to-all-start.2 = ((bf16[64,128,128]{2,1,0:T(8,128)(2,1)}), bf16[64,128,128]{2,1,0:T(8,128)(2,1)}, u32[]{:S(2)}, u32[]{:S(2)}) async-start(bf16[64,128,128]{2,1,0:T(8,128)(2,1)} %bitcast.159), calls=%async_computation.2 | async-start | bytes 4194304 | tf_op jit(solution)/shard_map/all_to_all | solution.py:252
  203.1 15.3 %collective-permute-start.26 = (bf16[8,128,256]{2,1,0:T(8,128)(2,1)S(1)}, bf16[8,128,256]{2,1,0:T(8,128)(2,1)S(1)}, u32[]{:S(2)}, u32[]{:S(2)}) collective-permute-start(bf16[8,128,256]{2,1,0:T(8,128)(2,1)S(1)} %pad_maximum_fusion.1.refs_0_), channel_id=1, source_target_pairs={{24,0},{7,1},{26,2},{1,3},{28,4},{3,5},{30,6},{5,7},{0,8},{15,9},{... | collective-permute-start | bytes 1572872 | tf_op jit(solution)/shard_map/ppermute | solution.py:15
  203.9 17.8 %collective-permute-start.25 = (bf16[8,128,256]{2,1,0:T(8,128)(2,1)S(1)}, bf16[8,128,256]{2,1,0:T(8,128)(2,1)}, u32[]{:S(2)}, u32[]{:S(2)}) collective-permute-start(bf16[8,128,256]{2,1,0:T(8,128)(2,1)S(1)} %pad_maximum_fusion.1.refs_0_), channel_id=1, source_target_pairs={{16,0},{5,1},{18,2},{7,3},{20,4},{1,5},{22,6},{3,7},{24,8},{13,9},... | collective-permute-start | bytes 1572872 | tf_op jit(solution)/shard_map/ppermute | solution.py:15
  205.3 16.4 %collective-permute-start.24 = (bf16[8,128,256]{2,1,0:T(8,128)(2,1)S(1)}, bf16[8,128,256]{2,1,0:T(8,128)(2,1)}, u32[]{:S(2)}, u32[]{:S(2)}) collective-permute-start(bf16[8,128,256]{2,1,0:T(8,128)(2,1)S(1)} %pad_maximum_fusion.1.refs_0_), channel_id=1, source_target_pairs={{8,0},{3,1},{10,2},{5,3},{12,4},{7,5},{14,6},{1,7},{16,8},{11,9},{... | collective-permute-start | bytes 1572872 | tf_op jit(solution)/shard_map/ppermute | solution.py:15
  206.4 19.1 %collective-permute-start.27 = (bf16[8,128,256]{2,1,0:T(8,128)(2,1)S(1)}, bf16[8,128,256]{2,1,0:T(8,128)(2,1)}, u32[]{:S(2)}, u32[]{:S(2)}) collective-permute-start(bf16[8,128,256]{2,1,0:T(8,128)(2,1)S(1)} %pad_maximum_fusion.1.refs_0_), channel_id=1, source_target_pairs={{0,1},{1,0},{2,3},{3,2},{4,5},{5,4},{6,7},{7,6},{8,9},{9,8},{10,11... | collective-permute-start | bytes 1572872 | tf_op jit(solution)/shard_map/ppermute | solution.py:15
  241.0 49.6 %collective-permute-start.31 = (bf16[8192,128]{1,0:T(8,128)(2,1)}, bf16[8192,128]{1,0:T(8,128)(2,1)S(1)}, u32[]{:S(2)}, u32[]{:S(2)}) collective-permute-start(bf16[8192,128]{1,0:T(8,128)(2,1)} %get-tuple-element.15), channel_id=1, source_target_pairs={{0,64},{1,65},{2,66},{3,67},{4,68},{5,69},{6,70},{7,71},{8,72},{9,... | collective-permute-start | bytes 6291464 | tf_op jit(solution)/shard_map/ppermute | solution.py:15
  300.4 62.4 %all-to-all-start.3 = ((bf16[128,128,128]{2,1,0:T(8,128)(2,1)}), bf16[128,128,128]{2,1,0:T(8,128)(2,1)}, u32[]{:S(2)}, u32[]{:S(2)}) async-start(bf16[128,128,128]{2,1,0:T(8,128)(2,1)} %bitcast.158), calls=%async_computation.3 | async-start | bytes 8388608 | tf_op jit(solution)/shard_map/all_to_all | solution.py:252
  370.0 9.4 %collective-permute-start.37 = (bf16[4,128,256]{2,1,0:T(8,128)(2,1)S(1)}, bf16[4,128,256]{2,1,0:T(8,128)(2,1)S(1)}, u32[]{:S(2)}, u32[]{:S(2)}) collective-permute-start(bf16[4,128,256]{2,1,0:T(8,128)(2,1)S(1)} %pad_maximum_fusion.3), channel_id=1, source_target_pairs={{24,0},{7,1},{26,2},{1,3},{28,4},{3,5},{30,6},{5,7},{0,8},{15,9},{... | collective-permute-start | bytes 786440 | tf_op jit(solution)/shard_map/ppermute | solution.py:15
  379.7 26.5 %collective-permute-start.40 = (bf16[16,128,256]{2,1,0:T(8,128)(2,1)S(1)}, bf16[16,128,256]{2,1,0:T(8,128)(2,1)S(1)}, u32[]{:S(2)}, u32[]{:S(2)}) collective-permute-start(bf16[16,128,256]{2,1,0:T(8,128)(2,1)S(1)} %pad_maximum_fusion.refs_0_), channel_id=1, source_target_pairs={{96,0},{25,1},{98,2},{27,3},{100,4},{29,5},{102,6},{31,7},{104,8},... | collective-permute-start | bytes 3145736 | tf_op jit(solution)/shard_map/ppermute | solution.py:15
  379.8 29.9 %collective-permute-start.39 = (bf16[16,128,256]{2,1,0:T(8,128)(2,1)S(1)}, bf16[16,128,256]{2,1,0:T(8,128)(2,1)S(1)}, u32[]{:S(2)}, u32[]{:S(2)}) collective-permute-start(bf16[16,128,256]{2,1,0:T(8,128)(2,1)S(1)} %pad_maximum_fusion.refs_0_), channel_id=1, source_target_pairs={{64,0},{17,1},{66,2},{19,3},{68,4},{21,5},{70,6},{23,7},{72,8},{25... | collective-permute-start | bytes 3145736 | tf_op jit(solution)/shard_map/ppermute | solution.py:15
  380.9 28.8 %collective-permute-start.38 = (bf16[16,128,256]{2,1,0:T(8,128)(2,1)S(1)}, bf16[16,128,256]{2,1,0:T(8,128)(2,1)}, u32[]{:S(2)}, u32[]{:S(2)}) collective-permute-start(bf16[16,128,256]{2,1,0:T(8,128)(2,1)S(1)} %pad_maximum_fusion.refs_0_), channel_id=1, source_target_pairs={{32,0},{9,1},{34,2},{11,3},{36,4},{13,5},{38,6},{15,7},{40,8},{17,... | collective-permute-start | bytes 3145736 | tf_op jit(solution)/shard_map/ppermute | solution.py:15
  382.5 30.8 %collective-permute-start.41 = (bf16[16,128,256]{2,1,0:T(8,128)(2,1)S(1)}, bf16[16,128,256]{2,1,0:T(8,128)(2,1)}, u32[]{:S(2)}, u32[]{:S(2)}) collective-permute-start(bf16[16,128,256]{2,1,0:T(8,128)(2,1)S(1)} %pad_maximum_fusion.refs_0_), channel_id=1, source_target_pairs={{0,1},{1,0},{2,3},{3,2},{4,5},{5,4},{6,7},{7,6},{8,9},{9,8},{10,11... | collective-permute-start | bytes 3145736 | tf_op jit(solution)/shard_map/ppermute | solution.py:15
  (43 other events, 636.5 us)

commit v3 on v2

--- a/solution.py
+++ b/solution.py
@@ -25,7 +25,7 @@
     ((("z", "z"), 2), (("x", "x"), 4)),
     ((("x", "z"), 4), (("z", "x"), 4)),
     ((("y", "y"), 2), (("x", "z"), 4), (("z", "x"), 4)),
-    ((("x", "y"), 4), (("z", "x"), 4), (("y", "z"), 4)),
+    ((("y", "y"), 4), (("x", "z"), 4), (("z", "x"), 4)),
 )
 
 
@@ -56,16 +56,18 @@
     return jnp.concatenate(placed, 0)
 
 
-def gather_rows(block, device, tier_num):
+def gather_rows(block, device, tier_num, early):
     devices = lax.axis_size(AXIS)
     stages = STAGES[tier_num]
     half = block[None]
     for axes, count in stages[:-1]:
         half = gather_stage(half, device, axes, count)
+    if early is not None:
+        half, early = lax.optimization_barrier((half, early))
     axes, count = stages[-1]
     pieces = gather_pieces(half, axes, count)
     others = [permute(piece, [(i, i ^ 1) for i in range(devices)]) for piece in pieces]
-    return pieces, others
+    return pieces, others, early
 
 
 def place_of(tier_num, groups, r):
@@ -144,19 +146,26 @@
             panel[at_first, :, width:] = zero
             panel[at_second, :, width:] = zero
 
+    places = [place(chunk * span + j) for j in range(span)]
+
+    @pl.when(role == ROLE_NONE)
+    def _():
+        both = jnp.concatenate([panel[at] for at in places], 0)
+        update = jnp.dot(both, band[...], preferred_element_type=jnp.float32)
+        value = column_ref[...].astype(jnp.float32) - update
+        final_ref[...] = value
+        if kept_ref is not None:
+            kept_ref[...] = value.astype(jnp.bfloat16)
+            for block in (first, second):
+
+                @pl.when((block >= chunk * span) & (block < (chunk + 1) * span))
+                def _():
+                    spot = pl.multiple_of((block - chunk * span) * width, width)
+                    kept_ref[pl.ds(spot, width)] = zero
+
     for j in range(span):
-        r = chunk * span + j
         rows = pl.ds(j * width, width)
-        at = place(r)
-
-        @pl.when(role == ROLE_NONE)
-        def _():
-            update = jnp.dot(panel[at], band[...], preferred_element_type=jnp.float32)
-            value = column_ref[rows].astype(jnp.float32) - update
-            final_ref[rows] = value
-            if kept_ref is not None:
-                value = jnp.where((r == first) | (r == second), 0.0, value)
-                kept_ref[rows] = value.astype(jnp.bfloat16)
+        at = places[j]
 
         @pl.when(role == ROLE_FIRST)
         def _():
@@ -166,11 +175,11 @@
         def _():
             final_ref[rows] = panel[at, :, width:].astype(jnp.float32)
 
-        if kept_ref is not None:
-
-            @pl.when(role != ROLE_NONE)
-            def _():
-                kept_ref[rows] = zero
+    if kept_ref is not None:
+
+        @pl.when(role != ROLE_NONE)
+        def _():
+            kept_ref[...] = jnp.zeros_like(kept_ref)
 
 
 def eliminate(tier_num, column, pieces, others, info, keep):
@@ -237,6 +246,41 @@
     width = front_leaf.shape[1]
     column = front_leaf
     results = []
+    zero = jnp.zeros((), jnp.bfloat16)
+
+    def pivots_of(tier_num):
+        groups = fronts[tier_num].shape[0] // width
+        row = lax.dynamic_index_in_dim(tables[tier_num], device // groups, 0, keepdims=False)
+        return row[0], row[1]
+
+    def pivot_pair(block, tier_num):
+        first, second = pivots_of(tier_num)
+        local = device % (fronts[tier_num].shape[0] // width)
+        return jnp.concatenate(
+            [jnp.where(local == first, block, zero), jnp.where(local == second, block, zero)], 1
+        )
+
+    bits = devices.bit_length() - 1
+    scales = jnp.stack([pivot_pair(inv_upper, 2), pivot_pair(inv_root, 3)])
+    for bit in range(bits - 1):
+        scales = scales + permute(scales, [(i, i ^ (1 << bit)) for i in range(devices)])
+    root_scale = scales[1] + permute(scales[1], [(i, i ^ (1 << (bits - 1))) for i in range(devices)])
+    row_scales = {2: scales[0], 3: root_scale}
+
+    def raw_rows(front, tier_num):
+        groups = front.shape[0] // width
+        teams = [list(range(i, i + groups)) for i in range(0, devices, groups)]
+        rows = lax.all_to_all(
+            front.reshape(groups, width, width), AXIS, 0, 0, axis_index_groups=teams, tiled=True
+        )
+        return jnp.concatenate(
+            [lax.dynamic_index_in_dim(rows, block, 0, keepdims=False) for block in pivots_of(tier_num)],
+            1,
+        )
+
+    upper_own = raw_rows(front_upper, 2)
+    root_own = raw_rows(front_root, 3)
+    carried_rows = None
     for tier_num in range(4):
         groups = fronts[tier_num].shape[0] // width
         front_num = device // groups
@@ -247,19 +291,40 @@
         first, second = pivot_row[0], pivot_row[1]
         is_first, is_second = local == first, local == second
 
-        scaled = jnp.dot(column, inverses[tier_num], preferred_element_type=jnp.float32)
-        scaled = scaled.astype(jnp.bfloat16)
-        rows = lax.all_to_all(
-            scaled.reshape(groups, width, width), AXIS, 0, 0, axis_index_groups=teams, tiled=True
-        )
-        own = jnp.concatenate(
-            [
-                lax.dynamic_index_in_dim(rows, first, 0, keepdims=False),
-                lax.dynamic_index_in_dim(rows, second, 0, keepdims=False),
-            ],
-            1,
-        )
-        pieces, others = gather_rows(own, device, tier_num)
+        if tier_num < 2:
+            scaled = jnp.dot(column, inverses[tier_num], preferred_element_type=jnp.float32)
+            scaled = scaled.astype(jnp.bfloat16)
+            if tier_num == 1:
+                scaled, upper_own, row_scales = lax.optimization_barrier((scaled, upper_own, row_scales))
+            rows = lax.all_to_all(
+                scaled.reshape(groups, width, width), AXIS, 0, 0, axis_index_groups=teams, tiled=True
+            )
+            own = jnp.concatenate(
+                [
+                    lax.dynamic_index_in_dim(rows, first, 0, keepdims=False),
+                    lax.dynamic_index_in_dim(rows, second, 0, keepdims=False),
+                ],
+                1,
+            )
+        else:
+            raw, scale = (upper_own if tier_num == 2 else root_own), row_scales[tier_num]
+            summed = (raw.astype(jnp.float32) + carried_rows).astype(jnp.bfloat16)
+            own = jnp.concatenate(
+                [
+                    jnp.dot(
+                        summed[:, i : i + width],
+                        scale[:, i : i + width],
+                        preferred_element_type=jnp.float32,
+                    ).astype(jnp.bfloat16)
+                    for i in (0, width)
+                ],
+                1,
+            )
+        if tier_num < 2:
+            pieces, others, _ = gather_rows(own, device, tier_num, None)
+        else:
+            pieces, others, upper_half = gather_rows(own, device, tier_num, received[0])
+            column = assemble([upper_half, received[1]])
         axes, count = STAGES[tier_num][-1]
         role = jnp.where(is_first, ROLE_FIRST, jnp.where(is_second, ROLE_SECOND, ROLE_NONE))
         info = jnp.stack(
@@ -276,23 +341,45 @@
         results.append(made[0])
         if tier_num < 3:
             kept = made[1]
-            received = permute(kept, [(i, i ^ groups) for i in range(devices)])
-            blocks = jnp.arange(groups, dtype=jnp.int32)
             side_row = child_sides[tier_num]
             parent_half = (device // groups) & 1
-            total = fronts[tier_num + 1].reshape(2, groups, width, width).astype(jnp.float32)
-            halves = jnp.arange(2, dtype=jnp.int32)
-            for part, flip in ((kept.reshape(groups, width, width), 0), (received.reshape(groups, width, width), 1)):
-                front_of = front_num ^ flip
-                sides = lax.dynamic_slice_in_dim(side_row, front_of * groups, groups, 0)
-                own_side = lax.dynamic_index_in_dim(
-                    side_row, front_of * groups + local, 0, keepdims=False
+            if tier_num >= 1:
+                if tier_num == 2:
+                    kept, root_own = lax.optimization_barrier((kept, root_own))
+                rows = lax.all_to_all(
+                    kept.reshape(groups, width, width), AXIS, 0, 0, axis_index_groups=teams, tiled=True
                 )
-                keep = (sides[None, :] == halves[:, None]) & (own_side == parent_half)
-                total = total + jnp.where(
-                    keep[:, :, None, None], part[None].astype(jnp.float32), 0.0
-                )
-            column = total.astype(jnp.bfloat16).reshape(-1, width)
+                found = []
+                for pivot in pivots_of(tier_num + 1):
+                    source = pivot % groups
+                    reaches = side_row[front_num * groups + source] == pivot // groups
+                    block = lax.dynamic_index_in_dim(rows, source, 0, keepdims=False)
+                    found.append(jnp.where(reaches, block, zero))
+                found = jnp.concatenate(found, 1)
+                met = permute(found, [(i, i ^ groups) for i in range(devices)])
+                carried_rows = jnp.where(
+                    side_row[device] == parent_half, found.astype(jnp.float32), 0.0
+                ) + jnp.where(side_row[device ^ groups] == parent_half, met.astype(jnp.float32), 0.0)
+            swap = [(i, i ^ groups) for i in range(devices)]
+            mine = kept.reshape(groups, width, width)
+            received = [permute(part, swap) for part in (mine[: groups // 2], mine[groups // 2 :])]
+
+            def assemble(received, tier_num=tier_num, groups=groups, front_num=front_num, mine=mine):
+                side_row = child_sides[tier_num]
+                parent_half = (device // groups) & 1
+                total = fronts[tier_num + 1].reshape(2, groups, width, width).astype(jnp.float32)
+                halves = jnp.arange(2, dtype=jnp.int32)
+                for part, flip in ((mine, 0), (jnp.concatenate(received, 0), 1)):
+                    sides = lax.dynamic_slice_in_dim(side_row, (front_num ^ flip) * groups, groups, 0)
+                    own_side = side_row[device ^ (groups * flip)]
+                    keep = (sides[None, :] == halves[:, None]) & (own_side == parent_half)
+                    total = total + jnp.where(
+                        keep[:, :, None, None], part[None].astype(jnp.float32), 0.0
+                    )
+                return total.astype(jnp.bfloat16).reshape(-1, width)
+
+            if tier_num == 0:
+                column = assemble(received)
     return tuple(results)
 
 

time: 447 us -> 453 us (1.013)
  waiting for transfers between devices: 218 us -> 153 us
  starting transfers between devices: 98.6 us -> 154 us
  blocking collectives: 0 us -> 23.2 us
  Pallas kernels: 57.2 us -> 35.6 us
  between operations: 25.8 us -> 36 us
  other arithmetic: 16.9 us -> 23 us
  matrix products: 9 us -> 4.03 us
    all_to_all x4 -> x2, waiting for transfers between devices: 89.2 us -> 12.7 us  [shards(): lax.all_to_all(scaled.reshape(groups, width, width), AXIS, 0, 0, axis_ind...]
    ppermute x45 -> x57, starting transfers between devices: 66.5 us -> 122 us  [permute(): return lax.ppermute(array, AXIS, pairs)]
    all_to_all x0 -> x3, waiting for transfers between devices: none -> 25.6 us  [the longest x1 25.6 us: shards(): lax.all_to_all(kept.reshape(groups, width, width), AXIS, 0, 0, axis_index...]
    all_to_all x0 -> x1, blocking collectives: none -> 23.2 us  [shards(): lax.all_to_all(kept.reshape(groups, width, width), AXIS, 0, 0, axis_index...]
    pallas_call x4, Pallas kernels: 57.2 us -> 35.6 us  [eliminate(): pl.pallas_call(body, grid_spec=pltpu.PrefetchScalarGridSpec(num_scalar_pr...]
    all_to_all x4 -> x2, starting transfers between devices: 32.1 us -> 12.7 us  [shards(): lax.all_to_all(scaled.reshape(groups, width, width), AXIS, 0, 0, axis_ind...]
    all_to_all x0 -> x3, starting transfers between devices: none -> 18.7 us  [the longest x2 13.9 us: raw_rows(): lax.all_to_all(front.reshape(groups, width, width), AXIS, 0, 0, axis_inde...]
    ppermute x45 -> x57, waiting for transfers between devices: 129 us -> 115 us  [permute(): return lax.ppermute(array, AXIS, pairs)]
  transfers between devices with their start and end apart: 49 -> 62, of which waited for: 21 -> 22; matrix products, arithmetic and copies ran while one was open for 3% -> 8% of each run, Pallas kernels for 0% -> 1%
where the time goes in v3:
time: 453 us; the launch traced here: 451 us
  starting transfers between devices  154 us (34%)
  waiting for transfers between devices  153 us (34%)
  between operations  36 us (8%)
  Pallas kernels  35.6 us (8%)
  blocking collectives  23.2 us (5%)
  other arithmetic  23 us (5%)
  local copies, waits for them, and re-layouts  22.8 us (5%)
    ppermute x57, starting transfers between devices, permute(): return lax.ppermute(array, AXIS, pairs)  122 us
    ppermute x57, waiting for transfers between devices, permute(): return lax.ppermute(array, AXIS, pairs)  115 us
    pallas_call x4, Pallas kernels, eliminate(): pl.pallas_call(body, grid_spec=pltpu.PrefetchScalarGridSpec(num_scalar_pr...  35.6 us
    all_to_all x1, waiting for transfers between devices, shards(): lax.all_to_all(kept.reshape(groups, width, width), AXIS, 0, 0, axis_index...  25.6 us
    all_to_all x1, blocking collectives, shards(): lax.all_to_all(kept.reshape(groups, width, width), AXIS, 0, 0, axis_index...  23.2 us
    all_to_all x2, starting transfers between devices, raw_rows(): lax.all_to_all(front.reshape(groups, width, width), AXIS, 0, 0, axis_inde...  13.9 us
    all_to_all x2, starting transfers between devices, shards(): lax.all_to_all(scaled.reshape(groups, width, width), AXIS, 0, 0, axis_ind...  12.7 us
    all_to_all x2, waiting for transfers between devices, shards(): lax.all_to_all(scaled.reshape(groups, width, width), AXIS, 0, 0, axis_ind...  12.7 us
  transfers between devices with their start and end apart: 62, of which 22 were waited for; matrix products, arithmetic and copies ran while one was open for 8% of the time, Pallas kernels for 1%

profile of v3, /device:TPU:1, one launch (start us, length us, event | category | flops | bytes accessed | tf_op | source)
XLA Modules:
  0.0 451.3 jit_solution(14853869904530240020)
XLA Ops:
  13.4 6.0 %all-to-all-start = ((bf16[16,128,128]{2,1,0:T(8,128)(2,1)}), bf16[16,128,128]{2,1,0:T(8,128)(2,1)S(1)}, u32[]{:S(2)}, u32[]{:S(2)}) async-start(bf16[16,128,128]{2,1,0:T(8,128)(2,1)} %bitcast.7), calls=%async_computation | async-start | bytes 1048576 | tf_op jit(solution)/shard_map/all_to_all | solution.py:299
  26.9 4.8 %collective-permute-done.12 = bf16[2,128,256]{2,1,0:T(8,128)(2,1)S(1)} collective-permute-done((bf16[2,128,256]{2,1,0:T(8,128)(2,1)S(1)}, bf16[2,128,256]{2,1,0:T(8,128)(2,1)S(1)}, u32[]{:S(2)}, u32[]{:S(2)}) %collective-permute-start.12) | collective-permute-done | bytes 131104 | tf_op jit(solution)/shard_map/ppermute | solution.py:15
  33.4 8.8 %all-to-all-start.1 = ((bf16[64,128,128]{2,1,0:T(8,128)(2,1)}), bf16[64,128,128]{2,1,0:T(8,128)(2,1)}, u32[]{:S(2)}, u32[]{:S(2)}) async-start(bf16[64,128,128]{2,1,0:T(8,128)(2,1)} %bitcast.28), calls=%async_computation.1 | async-start | bytes 4194304 | tf_op jit(solution)/shard_map/all_to_all | solution.py:273
  48.9 22.3 %collective-permute-done.14 = bf16[2,128,256]{2,1,0:T(8,128)(2,1)S(1)} collective-permute-done((bf16[2,128,256]{2,1,0:T(8,128)(2,1)S(1)}, bf16[2,128,256]{2,1,0:T(8,128)(2,1)S(1)}, u32[]{:S(2)}, u32[]{:S(2)}) %collective-permute-start.14) | collective-permute-done | bytes 131104 | tf_op jit(solution)/shard_map/ppermute | solution.py:15
  95.3 5.6 %collective-permute-done.8 = bf16[8,128,128]{2,1,0:T(8,128)(2,1)S(1)} collective-permute-done((bf16[8,128,128]{2,1,0:T(8,128)(2,1)S(1)}, bf16[8,128,128]{2,1,0:T(8,128)(2,1)S(1)}, u32[]{:S(2)}, u32[]{:S(2)}) %collective-permute-start.8) | collective-permute-done | bytes 262176 | tf_op jit(solution)/shard_map/ppermute | solution.py:15
  105.4 6.7 %all-to-all-start.2 = ((bf16[32,128,128]{2,1,0:T(8,128)(2,1)}), bf16[32,128,128]{2,1,0:T(8,128)(2,1)S(1)}, u32[]{:S(2)}, u32[]{:S(2)}) async-start(bf16[32,128,128]{2,1,0:T(8,128)(2,1)} %bitcast.39), calls=%async_computation.2 | async-start | bytes 2097152 | tf_op jit(solution)/shard_map/all_to_all | solution.py:299
  116.7 12.7 %all-to-all-done.2 = bf16[32,128,128]{2,1,0:T(8,128)(2,1)S(1)} async-done(((bf16[32,128,128]{2,1,0:T(8,128)(2,1)}), bf16[32,128,128]{2,1,0:T(8,128)(2,1)S(1)}, u32[]{:S(2)}, u32[]{:S(2)}) %all-to-all-start.2) | async-done | bytes 1048608 | tf_op jit(solution)/shard_map/all_to_all | solution.py:299
  155.9 4.7 %shard_map.157 = (f32[4096,128]{1,0:T(8,128)}, bf16[4096,128]{1,0:T(8,128)(2,1)S(1)}) custom-call(s32[6]{0:T(128)S(1)} %stack.57.info, bf16[4096,128]{1,0:T(8,128)(2,1)S(1)} %fusion.7.column_any.column_ref, bf16[4096,128]{1,0:T(8,128)(2,1)S(1)} %fusion.7.column_any.column_ref, bf16[4,128,256]{2,1,0:T(8,128)(2,1)S(1)} %pad_maximum_fusion.2.refs_0_, ...), custom_call_target="tpu_custom_call" | custom-call | flops 402653184 | bytes 6291456 | tf_op jit(solution)/shard_map/pallas_call | solution.py:203
  160.6 23.2 %all_to_all.30 = bf16[32,128,128]{2,1,0:T(8,128)(2,1)S(1)} all-to-all(bf16[32,128,128]{2,1,0:T(8,128)(2,1)S(1)} %bitcast.171), channel_id=1, replica_groups={{0,1,2,3,4,5,6,7,8,9,10,11,12,13,14,15,16,17,18,19,20,21,22,23,24,25,26..., dimensions={0} | all-to-all | bytes 2097152 | tf_op jit(solution)/shard_map/all_to_all | solution.py:349
  183.8 5.1 %all-to-all-start.4 = ((bf16[128,128,128]{2,1,0:T(8,128)(2,1)}), bf16[128,128,128]{2,1,0:T(8,128)(2,1)}, u32[]{:S(2)}, u32[]{:S(2)}) async-start(bf16[128,128,128]{2,1,0:T(8,128)(2,1)} %bitcast.174), calls=%async_computation.4 | async-start | bytes 8388608 | tf_op jit(solution)/shard_map/all_to_all | solution.py:273
  201.3 33.3 %collective-permute-done.27 = bf16[128,256]{1,0:T(8,128)(2,1)S(1)} collective-permute-done((bf16[128,256]{1,0:T(8,128)(2,1)S(1)}, bf16[128,256]{1,0:T(8,128)(2,1)S(1)}, u32[]{:S(2)}, u32[]{:S(2)}) %collective-permute-start.27) | collective-permute-done | bytes 65568 | tf_op jit(solution)/shard_map/ppermute | solution.py:15
  238.6 5.8 %collective-permute-start.30 = (bf16[2,128,256]{2,1,0:T(8,128)(2,1)S(1)}, bf16[2,128,256]{2,1,0:T(8,128)(2,1)S(1)}, u32[]{:S(2)}, u32[]{:S(2)}) collective-permute-start(bf16[2,128,256]{2,1,0:T(8,128)(2,1)S(1)} %pad_maximum_fusion.6), channel_id=1, source_target_pairs={{4,0},{17,1},{6,2},{19,3},{0,4},{21,5},{2,6},{23,7},{12,8},{25,9},... | collective-permute-start | bytes 393224 | tf_op jit(solution)/shard_map/ppermute | solution.py:15
  249.6 9.8 %collective-permute-done.32 = bf16[16,128,128]{2,1,0:T(8,128)(2,1)S(1)} collective-permute-done((bf16[16,128,128]{2,1,0:T(8,128)(2,1)S(1)}, bf16[16,128,128]{2,1,0:T(8,128)(2,1)S(1)}, u32[]{:S(2)}, u32[]{:S(2)}) %collective-permute-start.32) | collective-permute-done | bytes 524320 | tf_op jit(solution)/shard_map/ppermute | solution.py:15
  269.2 6.5 %collective-permute-done.34.refs_1_ = bf16[8,128,256]{2,1,0:T(8,128)(2,1)S(1)} collective-permute-done((bf16[8,128,256]{2,1,0:T(8,128)(2,1)S(1)}, bf16[8,128,256]{2,1,0:T(8,128)(2,1)S(1)}, u32[]{:S(2)}, u32[]{:S(2)}) %collective-permute-start.34) | collective-permute-done | bytes 524320 | tf_op jit(solution)/shard_map/ppermute | solution.py:15
  283.4 5.6 %fusion.4.column_any.column_ref = bf16[8192,128]{1,0:T(8,128)(2,1)S(1)} fusion(bf16[8192,128]{1,0:T(8,128)(2,1)} %param.15, f32[32,128,128]{2,1,0:T(8,128)S(1)} %maximum_convert_fusion.1, f32[32,128,128]{2,1,0:T(8,128)S(1)} %copy-done.10, pred[8192]{0:T(1024)(128)(4,1)S(1)} %bitcast.182, pred[8192]{0:T(1024)(128)(4,1)S(1)} %bitcast.183), kind=kLoop, calls=%fused_computation.8 | loop fusion | flops 6291456 | bytes 8404992 | tf_op jit(solution)/shard_map/convert_element_type | solution.py:379
  289.1 9.7 %shard_map.158 = (f32[8192,128]{1,0:T(8,128)}, bf16[8192,128]{1,0:T(8,128)(2,1)}) custom-call(s32[6]{0:T(128)S(1)} %stack.62.info, bf16[8192,128]{1,0:T(8,128)(2,1)S(1)} %fusion.4.column_any.column_ref, bf16[8192,128]{1,0:T(8,128)(2,1)S(1)} %fusion.4.column_any.column_ref, bf16[8,128,256]{2,1,0:T(8,128)(2,1)S(1)} %pad_maximum_fusion.1.refs_0_, ...), custom_call_target="tpu_custom_call" | custom-call | flops 805306368 | bytes 12582912 | tf_op jit(solution)/shard_map/pallas_call | solution.py:203
  298.8 4.9 %all-to-all-start.5 = ((bf16[64,128,128]{2,1,0:T(8,128)(2,1)}), bf16[64,128,128]{2,1,0:T(8,128)(2,1)S(1)}, u32[]{:S(2)}, u32[]{:S(2)}) async-start(bf16[64,128,128]{2,1,0:T(8,128)(2,1)} %bitcast.71), calls=%async_computation.5 | async-start | bytes 4194304 | tf_op jit(solution)/shard_map/all_to_all | solution.py:349
  306.2 25.6 %all-to-all-done.5 = bf16[64,128,128]{2,1,0:T(8,128)(2,1)S(1)} async-done(((bf16[64,128,128]{2,1,0:T(8,128)(2,1)}), bf16[64,128,128]{2,1,0:T(8,128)(2,1)S(1)}, u32[]{:S(2)}, u32[]{:S(2)}) %all-to-all-start.5) | async-done | bytes 2097184 | tf_op jit(solution)/shard_map/all_to_all | solution.py:349
  355.6 12.9 %collective-permute-done.48 = bf16[32,128,128]{2,1,0:T(8,128)(2,1)S(1)} collective-permute-done((bf16[32,128,128]{2,1,0:T(8,128)(2,1)S(1)}, bf16[32,128,128]{2,1,0:T(8,128)(2,1)S(1)}, u32[]{:S(2)}, u32[]{:S(2)}) %collective-permute-start.48) | collective-permute-done | bytes 1048608 | tf_op jit(solution)/shard_map/ppermute | solution.py:15
  372.9 24.1 %collective-permute-start.53 = (bf16[16,128,256]{2,1,0:T(8,128)(2,1)S(1)}, bf16[16,128,256]{2,1,0:T(8,128)(2,1)}, u32[]{:S(2)}, u32[]{:S(2)}) collective-permute-start(bf16[16,128,256]{2,1,0:T(8,128)(2,1)S(1)} %pad_maximum_fusion.refs_0_), channel_id=1, source_target_pairs={{0,1},{1,0},{2,3},{3,2},{4,5},{5,4},{6,7},{7,6},{8,9},{9,8},{10,11... | collective-permute-start | bytes 3145736 | tf_op jit(solution)/shard_map/ppermute | solution.py:15
  397.0 12.8 %collective-permute-start.54 = (bf16[16,128,256]{2,1,0:T(8,128)(2,1)S(1)}, bf16[16,128,256]{2,1,0:T(8,128)(2,1)}, u32[]{:S(2)}, u32[]{:S(2)}) collective-permute-start(bf16[16,128,256]{2,1,0:T(8,128)(2,1)S(1)} %collective-permute-done.50.refs_1_), channel_id=1, source_target_pairs={{0,1},{1,0},{2,3},{3,2},{4,5},{5,4},{6,7},{7,6},{8,9},{9,8},{10,11... | collective-permute-start | bytes 3145736 | tf_op jit(solution)/shard_map/ppermute | solution.py:15
  411.5 11.2 %collective-permute-start.56 = (bf16[16,128,256]{2,1,0:T(8,128)(2,1)}, bf16[16,128,256]{2,1,0:T(8,128)(2,1)}, u32[]{:S(2)}, u32[]{:S(2)}) collective-permute-start(bf16[16,128,256]{2,1,0:T(8,128)(2,1)} %collective-permute-done.52.refs_3_), channel_id=1, source_target_pairs={{0,1},{1,0},{2,3},{3,2},{4,5},{5,4},{6,7},{7,6},{8,9},{9,8},{10,11... | collective-permute-start | bytes 3145736 | tf_op jit(solution)/shard_map/ppermute | solution.py:15
  428.8 5.6 %fusion.1.column_any.column_ref = bf16[16384,128]{1,0:T(8,128)(2,1)S(1)} fusion(bf16[16384,128]{1,0:T(8,128)(2,1)S(1)} %copy-done.9, f32[64,128,128]{2,1,0:T(8,128)S(1)} %maximum_convert_fusion, f32[64,128,128]{2,1,0:T(8,128)S(1)} %convert_element_type.135, pred[16384]{0:T(1024)(128)(4,1)S(1)} %bitcast.180, pred[16384]{0:T(1024)(128)(4,1)S(1)} %bitcast.181), kind=kLoop, calls=%fused_computation.2 | loop fusion | flops 12582912 | bytes 16809984 | tf_op jit(solution)/shard_map/convert_element_type | solution.py:379
  434.4 16.7 %shard_map.159 = f32[16384,128]{1,0:T(8,128)} custom-call(s32[6]{0:T(128)S(1)} %stack.64.info, bf16[16384,128]{1,0:T(8,128)(2,1)S(1)} %fusion.1.column_any.column_ref, bf16[16384,128]{1,0:T(8,128)(2,1)S(1)} %fusion.1.column_any.column_ref, bf16[16,128,256]{2,1,0:T(8,128)(2,1)S(1)} %pad_maximum_fusion.refs_0_, ...), custom_call_target="tpu_custom_call" | custom-call | flops 1610612736 | bytes 25165824 | tf_op jit(solution)/shard_map/pallas_call | solution.py:203
  (235 shorter events, 130.9 us)
Async XLA Ops:
  13.4 19.6 %all-to-all-start = ((bf16[16,128,128]{2,1,0:T(8,128)(2,1)}), bf16[16,128,128]{2,1,0:T(8,128)(2,1)S(1)}, u32[]{:S(2)}, u32[]{:S(2)}) async-start(bf16[16,128,128]{2,1,0:T(8,128)(2,1)} %bitcast.7), calls=%async_computation | async-start | bytes 1048576 | tf_op jit(solution)/shard_map/all_to_all | solution.py:299
  33.4 70.6 %all-to-all-start.1 = ((bf16[64,128,128]{2,1,0:T(8,128)(2,1)}), bf16[64,128,128]{2,1,0:T(8,128)(2,1)}, u32[]{:S(2)}, u32[]{:S(2)}) async-start(bf16[64,128,128]{2,1,0:T(8,128)(2,1)} %bitcast.28), calls=%async_computation.1 | async-start | bytes 4194304 | tf_op jit(solution)/shard_map/all_to_all | solution.py:273
  42.3 29.0 %collective-permute-start.14 = (bf16[2,128,256]{2,1,0:T(8,128)(2,1)S(1)}, bf16[2,128,256]{2,1,0:T(8,128)(2,1)S(1)}, u32[]{:S(2)}, u32[]{:S(2)}) collective-permute-start(bf16[2,128,256]{2,1,0:T(8,128)(2,1)S(1)} %add.232), channel_id=1, source_target_pairs={{0,16},{1,17},{2,18},{3,19},{4,20},{5,21},{6,22},{7,23},{8,24},{9,... | collective-permute-start | bytes 393224 | tf_op jit(solution)/shard_map/ppermute | solution.py:15
  45.3 32.9 %collective-permute-start.1 = (bf16[2,128,256]{2,1,0:T(8,128)(2,1)S(1)}, bf16[2,128,256]{2,1,0:T(8,128)(2,1)S(1)}, u32[]{:S(2)}, u32[]{:S(2)}) collective-permute-start(bf16[2,128,256]{2,1,0:T(8,128)(2,1)S(1)} %pad_maximum_fusion.4.refs_0_), channel_id=1, source_target_pairs={{2,0},{3,1},{4,2},{5,3},{6,4},{7,5},{0,6},{1,7},{10,8},{11,9},{12,... | collective-permute-start | bytes 393224 | tf_op jit(solution)/shard_map/ppermute | solution.py:15
  47.8 30.5 %collective-permute-start.2 = (bf16[2,128,256]{2,1,0:T(8,128)(2,1)S(1)}, bf16[2,128,256]{2,1,0:T(8,128)(2,1)S(1)}, u32[]{:S(2)}, u32[]{:S(2)}) collective-permute-start(bf16[2,128,256]{2,1,0:T(8,128)(2,1)S(1)} %pad_maximum_fusion.4.refs_0_), channel_id=1, source_target_pairs={{4,0},{5,1},{6,2},{7,3},{0,4},{1,5},{2,6},{3,7},{12,8},{13,9},{14,... | collective-permute-start | bytes 393224 | tf_op jit(solution)/shard_map/ppermute | solution.py:15
  48.3 30.3 %collective-permute-start.3 = (bf16[2,128,256]{2,1,0:T(8,128)(2,1)S(1)}, bf16[2,128,256]{2,1,0:T(8,128)(2,1)S(1)}, u32[]{:S(2)}, u32[]{:S(2)}) collective-permute-start(bf16[2,128,256]{2,1,0:T(8,128)(2,1)S(1)} %pad_maximum_fusion.4.refs_0_), channel_id=1, source_target_pairs={{6,0},{7,1},{0,2},{1,3},{2,4},{3,5},{4,6},{5,7},{14,8},{15,9},{8,1... | collective-permute-start | bytes 393224 | tf_op jit(solution)/shard_map/ppermute | solution.py:15
  79.5 14.2 %collective-permute-start.16 = (bf16[128,256]{1,0:T(8,128)(2,1)S(1)}, bf16[128,256]{1,0:T(8,128)(2,1)S(1)}, u32[]{:S(2)}, u32[]{:S(2)}) collective-permute-start(bf16[128,256]{1,0:T(8,128)(2,1)S(1)} %get-tuple-element.69), channel_id=1, source_target_pairs={{0,64},{1,65},{2,66},{3,67},{4,68},{5,69},{6,70},{7,71},{8,72},{9,... | collective-permute-start | bytes 196616 | tf_op jit(solution)/shard_map/ppermute | solution.py:15
  105.4 23.9 %all-to-all-start.2 = ((bf16[32,128,128]{2,1,0:T(8,128)(2,1)}), bf16[32,128,128]{2,1,0:T(8,128)(2,1)S(1)}, u32[]{:S(2)}, u32[]{:S(2)}) async-start(bf16[32,128,128]{2,1,0:T(8,128)(2,1)} %bitcast.39), calls=%async_computation.2 | async-start | bytes 2097152 | tf_op jit(solution)/shard_map/all_to_all | solution.py:299
  183.8 97.1 %all-to-all-start.4 = ((bf16[128,128,128]{2,1,0:T(8,128)(2,1)}), bf16[128,128,128]{2,1,0:T(8,128)(2,1)}, u32[]{:S(2)}, u32[]{:S(2)}) async-start(bf16[128,128,128]{2,1,0:T(8,128)(2,1)} %bitcast.174), calls=%async_computation.4 | async-start | bytes 8388608 | tf_op jit(solution)/shard_map/all_to_all | solution.py:273
  198.5 36.1 %collective-permute-start.27 = (bf16[128,256]{1,0:T(8,128)(2,1)S(1)}, bf16[128,256]{1,0:T(8,128)(2,1)S(1)}, u32[]{:S(2)}, u32[]{:S(2)}) collective-permute-start(bf16[128,256]{1,0:T(8,128)(2,1)S(1)} %pad_maximum_fusion.8), channel_id=1, source_target_pairs={{0,32},{1,33},{2,34},{3,35},{4,36},{5,37},{6,38},{7,39},{8,40},{9,... | collective-permute-start | bytes 196616 | tf_op jit(solution)/shard_map/ppermute | solution.py:15
  259.4 16.3 %collective-permute-start.34 = (bf16[8,128,256]{2,1,0:T(8,128)(2,1)S(1)}, bf16[8,128,256]{2,1,0:T(8,128)(2,1)S(1)}, u32[]{:S(2)}, u32[]{:S(2)}) collective-permute-start(bf16[8,128,256]{2,1,0:T(8,128)(2,1)S(1)} %pad_maximum_fusion.1.refs_0_), channel_id=1, source_target_pairs={{8,0},{3,1},{10,2},{5,3},{12,4},{7,5},{14,6},{1,7},{16,8},{11,9},{... | collective-permute-start | bytes 1572872 | tf_op jit(solution)/shard_map/ppermute | solution.py:15
  263.9 15.1 %collective-permute-start.36 = (bf16[8,128,256]{2,1,0:T(8,128)(2,1)S(1)}, bf16[8,128,256]{2,1,0:T(8,128)(2,1)S(1)}, u32[]{:S(2)}, u32[]{:S(2)}) collective-permute-start(bf16[8,128,256]{2,1,0:T(8,128)(2,1)S(1)} %pad_maximum_fusion.1.refs_0_), channel_id=1, source_target_pairs={{24,0},{7,1},{26,2},{1,3},{28,4},{3,5},{30,6},{5,7},{0,8},{15,9},{... | collective-permute-start | bytes 1572872 | tf_op jit(solution)/shard_map/ppermute | solution.py:15
  265.4 16.5 %collective-permute-start.33 = (bf16[16,128,128]{2,1,0:T(8,128)(2,1)}, bf16[16,128,128]{2,1,0:T(8,128)(2,1)}, u32[]{:S(2)}, u32[]{:S(2)}) collective-permute-start(bf16[16,128,128]{2,1,0:T(8,128)(2,1)} %bitcast.176), channel_id=1, source_target_pairs={{0,32},{1,33},{2,34},{3,35},{4,36},{5,37},{6,38},{7,39},{8,40},{9,... | collective-permute-start | bytes 1572872 | tf_op jit(solution)/shard_map/ppermute | solution.py:15
  269.1 19.9 %collective-permute-start.37 = (bf16[8,128,256]{2,1,0:T(8,128)(2,1)S(1)}, bf16[8,128,256]{2,1,0:T(8,128)(2,1)}, u32[]{:S(2)}, u32[]{:S(2)}) collective-permute-start(bf16[8,128,256]{2,1,0:T(8,128)(2,1)S(1)} %pad_maximum_fusion.1.refs_0_), channel_id=1, source_target_pairs={{0,1},{1,0},{2,3},{3,2},{4,5},{5,4},{6,7},{7,6},{8,9},{9,8},{10,11... | collective-permute-start | bytes 1572872 | tf_op jit(solution)/shard_map/ppermute | solution.py:15
  298.8 33.0 %all-to-all-start.5 = ((bf16[64,128,128]{2,1,0:T(8,128)(2,1)}), bf16[64,128,128]{2,1,0:T(8,128)(2,1)S(1)}, u32[]{:S(2)}, u32[]{:S(2)}) async-start(bf16[64,128,128]{2,1,0:T(8,128)(2,1)} %bitcast.71), calls=%async_computation.5 | async-start | bytes 4194304 | tf_op jit(solution)/shard_map/all_to_all | solution.py:349
  345.1 23.4 %collective-permute-start.48 = (bf16[32,128,128]{2,1,0:T(8,128)(2,1)S(1)}, bf16[32,128,128]{2,1,0:T(8,128)(2,1)S(1)}, u32[]{:S(2)}, u32[]{:S(2)}) collective-permute-start(bf16[32,128,128]{2,1,0:T(8,128)(2,1)S(1)} %bitcast.175), channel_id=1, source_target_pairs={{0,64},{1,65},{2,66},{3,67},{4,68},{5,69},{6,70},{7,71},{8,72},{9,... | collective-permute-start | bytes 3145736 | tf_op jit(solution)/shard_map/ppermute | solution.py:15
  368.5 28.4 %collective-permute-start.50 = (bf16[16,128,256]{2,1,0:T(8,128)(2,1)S(1)}, bf16[16,128,256]{2,1,0:T(8,128)(2,1)S(1)}, u32[]{:S(2)}, u32[]{:S(2)}) collective-permute-start(bf16[16,128,256]{2,1,0:T(8,128)(2,1)S(1)} %pad_maximum_fusion.refs_0_), channel_id=1, source_target_pairs={{8,0},{3,1},{10,2},{5,3},{12,4},{7,5},{14,6},{1,7},{16,8},{11,9},{... | collective-permute-start | bytes 3145736 | tf_op jit(solution)/shard_map/ppermute | solution.py:15
  370.8 39.0 %collective-permute-start.51 = (bf16[16,128,256]{2,1,0:T(8,128)(2,1)S(1)}, bf16[16,128,256]{2,1,0:T(8,128)(2,1)S(1)}, u32[]{:S(2)}, u32[]{:S(2)}) collective-permute-start(bf16[16,128,256]{2,1,0:T(8,128)(2,1)S(1)} %pad_maximum_fusion.refs_0_), channel_id=1, source_target_pairs={{16,0},{5,1},{18,2},{7,3},{20,4},{1,5},{22,6},{3,7},{24,8},{13,9},... | collective-permute-start | bytes 3145736 | tf_op jit(solution)/shard_map/ppermute | solution.py:15
  372.6 38.9 %collective-permute-start.52 = (bf16[16,128,256]{2,1,0:T(8,128)(2,1)S(1)}, bf16[16,128,256]{2,1,0:T(8,128)(2,1)}, u32[]{:S(2)}, u32[]{:S(2)}) collective-permute-start(bf16[16,128,256]{2,1,0:T(8,128)(2,1)S(1)} %pad_maximum_fusion.refs_0_), channel_id=1, source_target_pairs={{24,0},{7,1},{26,2},{1,3},{28,4},{3,5},{30,6},{5,7},{0,8},{15,9},{... | collective-permute-start | bytes 3145736 | tf_op jit(solution)/shard_map/ppermute | solution.py:15
  372.6 53.7 %collective-permute-start.49 = (bf16[32,128,128]{2,1,0:T(8,128)(2,1)}, bf16[32,128,128]{2,1,0:T(8,128)(2,1)}, u32[]{:S(2)}, u32[]{:S(2)}) collective-permute-start(bf16[32,128,128]{2,1,0:T(8,128)(2,1)} %bitcast.82), channel_id=1, source_target_pairs={{0,64},{1,65},{2,66},{3,67},{4,68},{5,69},{6,70},{7,71},{8,72},{9,... | collective-permute-start | bytes 3145736 | tf_op jit(solution)/shard_map/ppermute | solution.py:15
  372.9 61.5 %collective-permute-start.53 = (bf16[16,128,256]{2,1,0:T(8,128)(2,1)S(1)}, bf16[16,128,256]{2,1,0:T(8,128)(2,1)}, u32[]{:S(2)}, u32[]{:S(2)}) collective-permute-start(bf16[16,128,256]{2,1,0:T(8,128)(2,1)S(1)} %pad_maximum_fusion.refs_0_), channel_id=1, source_target_pairs={{0,1},{1,0},{2,3},{3,2},{4,5},{5,4},{6,7},{7,6},{8,9},{9,8},{10,11... | collective-permute-start | bytes 3145736 | tf_op jit(solution)/shard_map/ppermute | solution.py:15
  397.0 37.4 %collective-permute-start.54 = (bf16[16,128,256]{2,1,0:T(8,128)(2,1)S(1)}, bf16[16,128,256]{2,1,0:T(8,128)(2,1)}, u32[]{:S(2)}, u32[]{:S(2)}) collective-permute-start(bf16[16,128,256]{2,1,0:T(8,128)(2,1)S(1)} %collective-permute-done.50.refs_1_), channel_id=1, source_target_pairs={{0,1},{1,0},{2,3},{3,2},{4,5},{5,4},{6,7},{7,6},{8,9},{9,8},{10,11... | collective-permute-start | bytes 3145736 | tf_op jit(solution)/shard_map/ppermute | solution.py:15
  409.8 24.7 %collective-permute-start.55 = (bf16[16,128,256]{2,1,0:T(8,128)(2,1)S(1)}, bf16[16,128,256]{2,1,0:T(8,128)(2,1)}, u32[]{:S(2)}, u32[]{:S(2)}) collective-permute-start(bf16[16,128,256]{2,1,0:T(8,128)(2,1)S(1)} %collective-permute-done.51.refs_2_), channel_id=1, source_target_pairs={{0,1},{1,0},{2,3},{3,2},{4,5},{5,4},{6,7},{7,6},{8,9},{9,8},{10,11... | collective-permute-start | bytes 3145736 | tf_op jit(solution)/shard_map/ppermute | solution.py:15
  411.5 23.0 %collective-permute-start.56 = (bf16[16,128,256]{2,1,0:T(8,128)(2,1)}, bf16[16,128,256]{2,1,0:T(8,128)(2,1)}, u32[]{:S(2)}, u32[]{:S(2)}) collective-permute-start(bf16[16,128,256]{2,1,0:T(8,128)(2,1)} %collective-permute-done.52.refs_3_), channel_id=1, source_target_pairs={{0,1},{1,0},{2,3},{3,2},{4,5},{5,4},{6,7},{7,6},{8,9},{9,8},{10,11... | collective-permute-start | bytes 3145736 | tf_op jit(solution)/shard_map/ppermute | solution.py:15
  (58 other events, 707.1 us)

commit v4 on v3

--- a/solution.py
+++ b/solution.py
@@ -60,14 +60,20 @@
     devices = lax.axis_size(AXIS)
     stages = STAGES[tier_num]
     half = block[None]
-    for axes, count in stages[:-1]:
-        half = gather_stage(half, device, axes, count)
-    if early is not None:
-        half, early = lax.optimization_barrier((half, early))
-    axes, count = stages[-1]
-    pieces = gather_pieces(half, axes, count)
+    received = []
+    for stage, (axes, count) in enumerate(stages):
+        if stage == len(stages) - 1:
+            if early is not None:
+                half, received[0] = lax.optimization_barrier((half, received[0]))
+            pieces = gather_pieces(half, axes, count)
+        else:
+            half = gather_stage(half, device, axes, count)
+            if early is not None and stage == 0:
+                swap, *parts = early
+                half, *parts = lax.optimization_barrier((half, *parts))
+                received = [permute(part, swap) for part in parts]
     others = [permute(piece, [(i, i ^ 1) for i in range(devices)]) for piece in pieces]
-    return pieces, others, early
+    return pieces, others, received
 
 
 def place_of(tier_num, groups, r):
@@ -260,26 +266,18 @@
             [jnp.where(local == first, block, zero), jnp.where(local == second, block, zero)], 1
         )
 
-    bits = devices.bit_length() - 1
-    scales = jnp.stack([pivot_pair(inv_upper, 2), pivot_pair(inv_root, 3)])
-    for bit in range(bits - 1):
-        scales = scales + permute(scales, [(i, i ^ (1 << bit)) for i in range(devices)])
-    root_scale = scales[1] + permute(scales[1], [(i, i ^ (1 << (bits - 1))) for i in range(devices)])
-    row_scales = {2: scales[0], 3: root_scale}
-
-    def raw_rows(front, tier_num):
-        groups = front.shape[0] // width
-        teams = [list(range(i, i + groups)) for i in range(0, devices, groups)]
-        rows = lax.all_to_all(
-            front.reshape(groups, width, width), AXIS, 0, 0, axis_index_groups=teams, tiled=True
-        )
+    root_scaled = jnp.dot(front_root, inv_root, preferred_element_type=jnp.float32)
+    root_scaled = root_scaled.astype(jnp.bfloat16).reshape(devices, width, width)
+    root_parts = [root_scaled[:, : width // 2], root_scaled[:, width // 2 :]]
+    root_rows = [None, None]
+    sibling_scale = permute(inv_root, [(i, i ^ (devices // 2)) for i in range(devices)])
+
+    def pivot_rows(rows, tier_num):
         return jnp.concatenate(
             [lax.dynamic_index_in_dim(rows, block, 0, keepdims=False) for block in pivots_of(tier_num)],
             1,
         )
 
-    upper_own = raw_rows(front_upper, 2)
-    root_own = raw_rows(front_root, 3)
     carried_rows = None
     for tier_num in range(4):
         groups = fronts[tier_num].shape[0] // width
@@ -291,11 +289,13 @@
         first, second = pivot_row[0], pivot_row[1]
         is_first, is_second = local == first, local == second
 
-        if tier_num < 2:
+        if tier_num < 3:
             scaled = jnp.dot(column, inverses[tier_num], preferred_element_type=jnp.float32)
             scaled = scaled.astype(jnp.bfloat16)
-            if tier_num == 1:
-                scaled, upper_own, row_scales = lax.optimization_barrier((scaled, upper_own, row_scales))
+            if tier_num > 0:
+                scaled, root_rows[tier_num - 1] = lax.optimization_barrier(
+                    (scaled, root_rows[tier_num - 1])
+                )
             rows = lax.all_to_all(
                 scaled.reshape(groups, width, width), AXIS, 0, 0, axis_index_groups=teams, tiled=True
             )
@@ -307,24 +307,13 @@
                 1,
             )
         else:
-            raw, scale = (upper_own if tier_num == 2 else root_own), row_scales[tier_num]
-            summed = (raw.astype(jnp.float32) + carried_rows).astype(jnp.bfloat16)
-            own = jnp.concatenate(
-                [
-                    jnp.dot(
-                        summed[:, i : i + width],
-                        scale[:, i : i + width],
-                        preferred_element_type=jnp.float32,
-                    ).astype(jnp.bfloat16)
-                    for i in (0, width)
-                ],
-                1,
-            )
-        if tier_num < 2:
+            raw = jnp.concatenate([pivot_rows(rows, tier_num) for rows in root_rows], 0)
+            own = (raw.astype(jnp.float32) + carried_rows).astype(jnp.bfloat16)
+        if tier_num < 3:
             pieces, others, _ = gather_rows(own, device, tier_num, None)
         else:
-            pieces, others, upper_half = gather_rows(own, device, tier_num, received[0])
-            column = assemble([upper_half, received[1]])
+            pieces, others, received = gather_rows(own, device, tier_num, to_send)
+            column = assemble(received)
         axes, count = STAGES[tier_num][-1]
         role = jnp.where(is_first, ROLE_FIRST, jnp.where(is_second, ROLE_SECOND, ROLE_NONE))
         info = jnp.stack(
@@ -343,11 +332,14 @@
             kept = made[1]
             side_row = child_sides[tier_num]
             parent_half = (device // groups) & 1
-            if tier_num >= 1:
-                if tier_num == 2:
-                    kept, root_own = lax.optimization_barrier((kept, root_own))
+            if tier_num < 2:
+                kept, part = lax.optimization_barrier((kept, root_parts[tier_num]))
+                root_rows[tier_num] = lax.all_to_all(part, AXIS, 0, 0, tiled=True)
+            else:
+                landing = jnp.where(side_row[device] == parent_half, inv_root, sibling_scale)
+                grown = jnp.dot(kept, landing, preferred_element_type=jnp.float32)
                 rows = lax.all_to_all(
-                    kept.reshape(groups, width, width), AXIS, 0, 0, axis_index_groups=teams, tiled=True
+                    grown.astype(jnp.bfloat16).reshape(groups, width, width), AXIS, 0, 0, axis_index_groups=teams, tiled=True
                 )
                 found = []
                 for pivot in pivots_of(tier_num + 1):
@@ -362,7 +354,8 @@
                 ) + jnp.where(side_row[device ^ groups] == parent_half, met.astype(jnp.float32), 0.0)
             swap = [(i, i ^ groups) for i in range(devices)]
             mine = kept.reshape(groups, width, width)
-            received = [permute(part, swap) for part in (mine[: groups // 2], mine[groups // 2 :])]
+            cut = groups * 3 // 8
+            to_send = (swap, mine[:cut], mine[cut:])
 
             def assemble(received, tier_num=tier_num, groups=groups, front_num=front_num, mine=mine):
                 side_row = child_sides[tier_num]
@@ -378,8 +371,8 @@
                     )
                 return total.astype(jnp.bfloat16).reshape(-1, width)
 
-            if tier_num == 0:
-                column = assemble(received)
+            if tier_num < 2:
+                column = assemble([permute(mine, swap)])
     return tuple(results)
 
 

time: 453 us -> 422 us (0.932)
  starting transfers between devices: 154 us -> 129 us
  blocking collectives: 23.2 us -> 0 us
  waiting for transfers between devices: 153 us -> 175 us
  other arithmetic: 23 us -> 14.5 us
  matrix products: 4.03 us -> 11.1 us
  between operations: 36 us -> 30.5 us
    ppermute x57 -> x48, starting transfers between devices: 122 us -> 86.4 us  [permute(): return lax.ppermute(array, AXIS, pairs)]
    all_to_all x2 -> x3, waiting for transfers between devices: 12.7 us -> 41.7 us  [shards(): lax.all_to_all(scaled.reshape(groups, width, width), AXIS, 0, 0, axis_ind...]
    all_to_all x1 -> x0, blocking collectives: 23.2 us -> none  [shards(): lax.all_to_all(kept.reshape(groups, width, width), AXIS, 0, 0, axis_index...]
    all_to_all x2 -> x3, starting transfers between devices: 12.7 us -> 21.6 us  [shards(): lax.all_to_all(scaled.reshape(groups, width, width), AXIS, 0, 0, axis_ind...]
    dot_general x4 -> x2, matrix products: 0.52 us -> 5.52 us  [the longest x1 3.42 us: shards(): jnp.dot(front_root, inv_root, preferred_element_type=jnp.float32)]
    ppermute x57 -> x48, waiting for transfers between devices: 115 us -> 112 us  [permute(): return lax.ppermute(array, AXIS, pairs)]
  transfers between devices with their start and end apart: 62 -> 54, of which waited for: 22 -> 25; matrix products, arithmetic and copies ran while one was open for 8% -> 8% of each run, Pallas kernels for 1% -> 2%
where the time goes in v4:
time: 422 us; the launch traced here: 420 us
  waiting for transfers between devices  175 us (41%)
  starting transfers between devices  129 us (31%)
  Pallas kernels  36 us (9%)
  between operations  30.5 us (7%)
  local copies, waits for them, and re-layouts  22.6 us (5%)
  other arithmetic  14.5 us (3%)
  matrix products  11.1 us (3%)
    ppermute x48, waiting for transfers between devices, permute(): return lax.ppermute(array, AXIS, pairs)  112 us
    ppermute x48, starting transfers between devices, permute(): return lax.ppermute(array, AXIS, pairs)  86.4 us
    all_to_all x3, waiting for transfers between devices, shards(): lax.all_to_all(scaled.reshape(groups, width, width), AXIS, 0, 0, axis_ind...  41.7 us
    pallas_call x4, Pallas kernels, eliminate(): pl.pallas_call(body, grid_spec=pltpu.PrefetchScalarGridSpec(num_scalar_pr...  36 us
    all_to_all x1, waiting for transfers between devices, shards(): lax.all_to_all(grown.astype(jnp.bfloat16).reshape(groups, width, width),...  21.7 us
    all_to_all x3, starting transfers between devices, shards(): lax.all_to_all(scaled.reshape(groups, width, width), AXIS, 0, 0, axis_ind...  21.6 us
    all_to_all x2, starting transfers between devices, shards(): root_rows[tier_num] = lax.all_to_all(part, AXIS, 0, 0, tiled=True)  15.8 us
    convert_element_type x3, other arithmetic, assemble(): return total.astype(jnp.bfloat16).reshape(-1, width)  9.85 us
  transfers between devices with their start and end apart: 54, of which 25 were waited for; matrix products, arithmetic and copies ran while one was open for 8% of the time, Pallas kernels for 2%

profile of v4, /device:TPU:1, one launch (start us, length us, event | category | flops | bytes accessed | tf_op | source)
XLA Modules:
  0.0 419.6 jit_solution(12941374161838583192)
XLA Ops:
  2.8 7.2 %all-to-all-start = ((bf16[16,128,128]{2,1,0:T(8,128)(2,1)}), bf16[16,128,128]{2,1,0:T(8,128)(2,1)S(1)}, u32[]{:S(2)}, u32[]{:S(2)}) async-start(bf16[16,128,128]{2,1,0:T(8,128)(2,1)} %bitcast.7), calls=%async_computation | async-start | bytes 1048576 | tf_op jit(solution)/shard_map/all_to_all | solution.py:299
  14.2 5.6 %all-to-all-done = bf16[16,128,128]{2,1,0:T(8,128)(2,1)S(1)} async-done(((bf16[16,128,128]{2,1,0:T(8,128)(2,1)}), bf16[16,128,128]{2,1,0:T(8,128)(2,1)S(1)}, u32[]{:S(2)}, u32[]{:S(2)}) %all-to-all-start) | async-done | bytes 524320 | tf_op jit(solution)/shard_map/all_to_all | solution.py:299
  40.8 4.4 %shard_map.156 = (f32[2048,128]{1,0:T(8,128)}, bf16[2048,128]{1,0:T(8,128)(2,1)S(1)}) custom-call(s32[6]{0:T(128)S(1)} %stack.45.info, bf16[2048,128]{1,0:T(8,128)(2,1)S(1)} %copy-done.4, bf16[2048,128]{1,0:T(8,128)(2,1)S(1)} %copy-done.4, bf16[2,128,256]{2,1,0:T(8,128)(2,1)S(1)} %pad_maximum_fusion.4.refs_0_, ...), custom_call_target="tpu_custom_call" | custom-call | flops 201326592 | bytes 3145728 | tf_op jit(solution)/shard_map/pallas_call | solution.py:209
  45.3 7.3 %all-to-all-start.1 = ((bf16[128,64,128]{2,1,0:T(8,128)(2,1)}), bf16[128,64,128]{2,1,0:T(8,128)(2,1)S(1)}, u32[]{:S(2)}, u32[]{:S(2)}) async-start(bf16[128,64,128]{2,1,0:T(8,128)(2,1)} %get-tuple-element.26), calls=%async_computation.1 | async-start | bytes 4194304 | tf_op jit(solution)/shard_map/all_to_all | solution.py:337
  58.1 32.3 %collective-permute-done.8 = bf16[16,128,128]{2,1,0:T(8,128)(2,1)S(1)} collective-permute-done((bf16[16,128,128]{2,1,0:T(8,128)(2,1)S(1)}, bf16[16,128,128]{2,1,0:T(8,128)(2,1)S(1)}, u32[]{:S(2)}, u32[]{:S(2)}) %collective-permute-start.8) | collective-permute-done | bytes 524320 | tf_op jit(solution)/shard_map/ppermute | solution.py:15
  93.4 5.5 %all-to-all-start.2 = ((bf16[32,128,128]{2,1,0:T(8,128)(2,1)}), bf16[32,128,128]{2,1,0:T(8,128)(2,1)}, u32[]{:S(2)}, u32[]{:S(2)}) async-start(bf16[32,128,128]{2,1,0:T(8,128)(2,1)} %bitcast.27), calls=%async_computation.2 | async-start | bytes 2097152 | tf_op jit(solution)/shard_map/all_to_all | solution.py:299
  103.5 12.7 %all-to-all-done.2 = bf16[32,128,128]{2,1,0:T(8,128)(2,1)} async-done(((bf16[32,128,128]{2,1,0:T(8,128)(2,1)}), bf16[32,128,128]{2,1,0:T(8,128)(2,1)}, u32[]{:S(2)}, u32[]{:S(2)}) %all-to-all-start.2) | async-done | bytes 1048608 | tf_op jit(solution)/shard_map/all_to_all | solution.py:299
  143.5 4.8 %shard_map.157 = (f32[4096,128]{1,0:T(8,128)}, bf16[4096,128]{1,0:T(8,128)(2,1)S(1)}) custom-call(s32[6]{0:T(128)S(1)} %stack.48.info, bf16[4096,128]{1,0:T(8,128)(2,1)S(1)} %fusion.7.column_any.column_ref, bf16[4096,128]{1,0:T(8,128)(2,1)S(1)} %fusion.7.column_any.column_ref, bf16[4,128,256]{2,1,0:T(8,128)(2,1)S(1)} %pad_maximum_fusion.2.refs_0_, ...), custom_call_target="tpu_custom_call" | custom-call | flops 402653184 | bytes 6291456 | tf_op jit(solution)/shard_map/pallas_call | solution.py:209
  148.3 8.4 %all-to-all-start.3 = ((bf16[128,64,128]{2,1,0:T(8,128)(2,1)}), bf16[128,64,128]{2,1,0:T(8,128)(2,1)}, u32[]{:S(2)}, u32[]{:S(2)}) async-start(bf16[128,64,128]{2,1,0:T(8,128)(2,1)} %get-tuple-element.31), calls=%async_computation.3 | async-start | bytes 4194304 | tf_op jit(solution)/shard_map/all_to_all | solution.py:337
  164.8 37.9 %collective-permute-done.19 = bf16[32,128,128]{2,1,0:T(8,128)(2,1)S(1)} collective-permute-done((bf16[32,128,128]{2,1,0:T(8,128)(2,1)S(1)}, bf16[32,128,128]{2,1,0:T(8,128)(2,1)S(1)}, u32[]{:S(2)}, u32[]{:S(2)}) %collective-permute-start.19) | collective-permute-done | bytes 1048608 | tf_op jit(solution)/shard_map/ppermute | solution.py:15
  207.9 8.9 %all-to-all-start.4 = ((bf16[64,128,128]{2,1,0:T(8,128)(2,1)}), bf16[64,128,128]{2,1,0:T(8,128)(2,1)}, u32[]{:S(2)}, u32[]{:S(2)}) async-start(bf16[64,128,128]{2,1,0:T(8,128)(2,1)} %bitcast.159), calls=%async_computation.4 | async-start | bytes 4194304 | tf_op jit(solution)/shard_map/all_to_all | solution.py:299
  221.5 23.4 %all-to-all-done.4 = bf16[64,128,128]{2,1,0:T(8,128)(2,1)} async-done(((bf16[64,128,128]{2,1,0:T(8,128)(2,1)}), bf16[64,128,128]{2,1,0:T(8,128)(2,1)}, u32[]{:S(2)}, u32[]{:S(2)}) %all-to-all-start.4) | async-done | bytes 2097184 | tf_op jit(solution)/shard_map/all_to_all | solution.py:299
  273.7 3.9 collective-permute-start.30
  283.8 9.7 %shard_map.158 = (f32[8192,128]{1,0:T(8,128)}, bf16[8192,128]{1,0:T(8,128)(2,1)S(1)}) custom-call(s32[6]{0:T(128)S(1)} %stack.50.info, bf16[8192,128]{1,0:T(8,128)(2,1)S(1)} %fusion.4.column_any.column_ref, bf16[8192,128]{1,0:T(8,128)(2,1)S(1)} %fusion.4.column_any.column_ref, bf16[8,128,256]{2,1,0:T(8,128)(2,1)S(1)} %pad_maximum_fusion.1.refs_0_, ...), custom_call_target="tpu_custom_call" | custom-call | flops 805306368 | bytes 12582912 | tf_op jit(solution)/shard_map/pallas_call | solution.py:209
  295.6 5.7 %all-to-all-start.5 = ((bf16[64,128,128]{2,1,0:T(8,128)(2,1)}), bf16[64,128,128]{2,1,0:T(8,128)(2,1)}, u32[]{:S(2)}, u32[]{:S(2)}) async-start(bf16[64,128,128]{2,1,0:T(8,128)(2,1)} %bitcast.160), calls=%async_computation.5 | async-start | bytes 4194304 | tf_op jit(solution)/shard_map/all_to_all | solution.py:341
  307.7 21.7 %all-to-all-done.5 = bf16[64,128,128]{2,1,0:T(8,128)(2,1)} async-done(((bf16[64,128,128]{2,1,0:T(8,128)(2,1)}), bf16[64,128,128]{2,1,0:T(8,128)(2,1)}, u32[]{:S(2)}, u32[]{:S(2)}) %all-to-all-start.5) | async-done | bytes 2097184 | tf_op jit(solution)/shard_map/all_to_all | solution.py:341
  342.0 3.6 collective-permute-start.37
  352.8 4.8 %collective-permute-done.39 = bf16[24,128,128]{2,1,0:T(8,128)(2,1)S(1)} collective-permute-done((bf16[24,128,128]{2,1,0:T(8,128)(2,1)S(1)}, bf16[24,128,128]{2,1,0:T(8,128)(2,1)S(1)}, u32[]{:S(2)}, u32[]{:S(2)}) %collective-permute-start.39) | collective-permute-done | bytes 786464 | tf_op jit(solution)/shard_map/ppermute | solution.py:15
  364.3 4.8 %collective-permute-start.44 = (bf16[16,128,256]{2,1,0:T(8,128)(2,1)S(1)}, bf16[16,128,256]{2,1,0:T(8,128)(2,1)}, u32[]{:S(2)}, u32[]{:S(2)}) collective-permute-start(bf16[16,128,256]{2,1,0:T(8,128)(2,1)S(1)} %pad_maximum_fusion.refs_0_), channel_id=1, source_target_pairs={{0,1},{1,0},{2,3},{3,2},{4,5},{5,4},{6,7},{7,6},{8,9},{9,8},{10,11... | collective-permute-start | bytes 3145736 | tf_op jit(solution)/shard_map/ppermute | solution.py:15
  369.1 3.8 collective-permute-done.41.refs_1_
  372.9 4.1 collective-permute-start.45
  379.5 7.6 %collective-permute-done.43.refs_3_ = bf16[16,128,256]{2,1,0:T(8,128)(2,1)} collective-permute-done((bf16[16,128,256]{2,1,0:T(8,128)(2,1)S(1)}, bf16[16,128,256]{2,1,0:T(8,128)(2,1)}, u32[]{:S(2)}, u32[]{:S(2)}) %collective-permute-start.43) | collective-permute-done | bytes 1048608 | tf_op jit(solution)/shard_map/ppermute | solution.py:15
  396.4 5.7 %fusion.1.column_any.column_ref = bf16[16384,128]{1,0:T(8,128)(2,1)S(1)} fusion(bf16[16384,128]{1,0:T(8,128)(2,1)S(1)} %copy-done.11, f32[64,128,128]{2,1,0:T(8,128)S(1)} %maximum_convert_fusion, f32[64,128,128]{2,1,0:T(8,128)S(1)} %convert.1, pred[16384]{0:T(1024)(128)(4,1)S(1)} %bitcast.162, pred[16384]{0:T(1024)(128)(4,1)S(1)} %bitcast.163), kind=kLoop, calls=%fused_computation.5 | loop fusion | flops 12582912 | bytes 16809984 | tf_op jit(solution)/shard_map/convert_element_type | solution.py:372
  402.2 17.2 %shard_map.159 = f32[16384,128]{1,0:T(8,128)} custom-call(s32[6]{0:T(128)S(1)} %stack.52.info, bf16[16384,128]{1,0:T(8,128)(2,1)S(1)} %fusion.1.column_any.column_ref, bf16[16384,128]{1,0:T(8,128)(2,1)S(1)} %fusion.1.column_any.column_ref, bf16[16,128,256]{2,1,0:T(8,128)(2,1)S(1)} %pad_maximum_fusion.refs_0_, ...), custom_call_target="tpu_custom_call" | custom-call | flops 1610612736 | bytes 25165824 | tf_op jit(solution)/shard_map/pallas_call | solution.py:209
  (206 shorter events, 138.0 us)
Async XLA Ops:
  2.8 17.0 %all-to-all-start = ((bf16[16,128,128]{2,1,0:T(8,128)(2,1)}), bf16[16,128,128]{2,1,0:T(8,128)(2,1)S(1)}, u32[]{:S(2)}, u32[]{:S(2)}) async-start(bf16[16,128,128]{2,1,0:T(8,128)(2,1)} %bitcast.7), calls=%async_computation | async-start | bytes 1048576 | tf_op jit(solution)/shard_map/all_to_all | solution.py:299
  29.2 11.6 %collective-permute-start.4 = (bf16[2,128,256]{2,1,0:T(8,128)(2,1)S(1)}, bf16[2,128,256]{2,1,0:T(8,128)(2,1)S(1)}, u32[]{:S(2)}, u32[]{:S(2)}) collective-permute-start(bf16[2,128,256]{2,1,0:T(8,128)(2,1)S(1)} %pad_maximum_fusion.4.refs_0_), channel_id=1, source_target_pairs={{0,1},{1,0},{2,3},{3,2},{4,5},{5,4},{6,7},{7,6},{8,9},{9,8},{10,11... | collective-permute-start | bytes 393224 | tf_op jit(solution)/shard_map/ppermute | solution.py:15
  45.3 48.2 %all-to-all-start.1 = ((bf16[128,64,128]{2,1,0:T(8,128)(2,1)}), bf16[128,64,128]{2,1,0:T(8,128)(2,1)S(1)}, u32[]{:S(2)}, u32[]{:S(2)}) async-start(bf16[128,64,128]{2,1,0:T(8,128)(2,1)} %get-tuple-element.26), calls=%async_computation.1 | async-start | bytes 4194304 | tf_op jit(solution)/shard_map/all_to_all | solution.py:337
  52.7 37.7 %collective-permute-start.8 = (bf16[16,128,128]{2,1,0:T(8,128)(2,1)S(1)}, bf16[16,128,128]{2,1,0:T(8,128)(2,1)S(1)}, u32[]{:S(2)}, u32[]{:S(2)}) collective-permute-start(bf16[16,128,128]{2,1,0:T(8,128)(2,1)S(1)} %bitcast.156), channel_id=1, source_target_pairs={{0,16},{1,17},{2,18},{3,19},{4,20},{5,21},{6,22},{7,23},{8,24},{9,... | collective-permute-start | bytes 1572872 | tf_op jit(solution)/shard_map/ppermute | solution.py:15
  93.4 22.8 %all-to-all-start.2 = ((bf16[32,128,128]{2,1,0:T(8,128)(2,1)}), bf16[32,128,128]{2,1,0:T(8,128)(2,1)}, u32[]{:S(2)}, u32[]{:S(2)}) async-start(bf16[32,128,128]{2,1,0:T(8,128)(2,1)} %bitcast.27), calls=%async_computation.2 | async-start | bytes 2097152 | tf_op jit(solution)/shard_map/all_to_all | solution.py:299
  125.2 13.3 %collective-permute-start.15 = (bf16[4,128,256]{2,1,0:T(8,128)(2,1)S(1)}, bf16[4,128,256]{2,1,0:T(8,128)(2,1)S(1)}, u32[]{:S(2)}, u32[]{:S(2)}) collective-permute-start(bf16[4,128,256]{2,1,0:T(8,128)(2,1)S(1)} %pad_maximum_fusion.2.refs_0_), channel_id=1, source_target_pairs={{0,1},{1,0},{2,3},{3,2},{4,5},{5,4},{6,7},{7,6},{8,9},{9,8},{10,11... | collective-permute-start | bytes 786440 | tf_op jit(solution)/shard_map/ppermute | solution.py:15
  148.3 59.6 %all-to-all-start.3 = ((bf16[128,64,128]{2,1,0:T(8,128)(2,1)}), bf16[128,64,128]{2,1,0:T(8,128)(2,1)}, u32[]{:S(2)}, u32[]{:S(2)}) async-start(bf16[128,64,128]{2,1,0:T(8,128)(2,1)} %get-tuple-element.31), calls=%async_computation.3 | async-start | bytes 4194304 | tf_op jit(solution)/shard_map/all_to_all | solution.py:337
  156.7 46.0 %collective-permute-start.19 = (bf16[32,128,128]{2,1,0:T(8,128)(2,1)S(1)}, bf16[32,128,128]{2,1,0:T(8,128)(2,1)S(1)}, u32[]{:S(2)}, u32[]{:S(2)}) collective-permute-start(bf16[32,128,128]{2,1,0:T(8,128)(2,1)S(1)} %bitcast.154), channel_id=1, source_target_pairs={{0,32},{1,33},{2,34},{3,35},{4,36},{5,37},{6,38},{7,39},{8,40},{9,... | collective-permute-start | bytes 3145736 | tf_op jit(solution)/shard_map/ppermute | solution.py:15
  207.9 36.9 %all-to-all-start.4 = ((bf16[64,128,128]{2,1,0:T(8,128)(2,1)}), bf16[64,128,128]{2,1,0:T(8,128)(2,1)}, u32[]{:S(2)}, u32[]{:S(2)}) async-start(bf16[64,128,128]{2,1,0:T(8,128)(2,1)} %bitcast.159), calls=%async_computation.4 | async-start | bytes 4194304 | tf_op jit(solution)/shard_map/all_to_all | solution.py:299
  259.8 14.0 %collective-permute-start.26 = (bf16[8,128,256]{2,1,0:T(8,128)(2,1)S(1)}, bf16[8,128,256]{2,1,0:T(8,128)(2,1)}, u32[]{:S(2)}, u32[]{:S(2)}) collective-permute-start(bf16[8,128,256]{2,1,0:T(8,128)(2,1)S(1)} %pad_maximum_fusion.1.refs_0_), channel_id=1, source_target_pairs={{24,0},{7,1},{26,2},{1,3},{28,4},{3,5},{30,6},{5,7},{0,8},{15,9},{... | collective-permute-start | bytes 1572872 | tf_op jit(solution)/shard_map/ppermute | solution.py:15
  259.8 24.1 %collective-permute-start.27 = (bf16[8,128,256]{2,1,0:T(8,128)(2,1)S(1)}, bf16[8,128,256]{2,1,0:T(8,128)(2,1)}, u32[]{:S(2)}, u32[]{:S(2)}) collective-permute-start(bf16[8,128,256]{2,1,0:T(8,128)(2,1)S(1)} %pad_maximum_fusion.1.refs_0_), channel_id=1, source_target_pairs={{0,1},{1,0},{2,3},{3,2},{4,5},{5,4},{6,7},{7,6},{8,9},{9,8},{10,11... | collective-permute-start | bytes 1572872 | tf_op jit(solution)/shard_map/ppermute | solution.py:15
  265.6 18.3 %collective-permute-start.28 = (bf16[8,128,256]{2,1,0:T(8,128)(2,1)S(1)}, bf16[8,128,256]{2,1,0:T(8,128)(2,1)}, u32[]{:S(2)}, u32[]{:S(2)}) collective-permute-start(bf16[8,128,256]{2,1,0:T(8,128)(2,1)S(1)} %collective-permute-done.24.refs_1_), channel_id=1, source_target_pairs={{0,1},{1,0},{2,3},{3,2},{4,5},{5,4},{6,7},{7,6},{8,9},{9,8},{10,11... | collective-permute-start | bytes 1572872 | tf_op jit(solution)/shard_map/ppermute | solution.py:15
  269.0 14.9 %collective-permute-start.29 = (bf16[8,128,256]{2,1,0:T(8,128)(2,1)}, bf16[8,128,256]{2,1,0:T(8,128)(2,1)}, u32[]{:S(2)}, u32[]{:S(2)}) collective-permute-start(bf16[8,128,256]{2,1,0:T(8,128)(2,1)} %collective-permute-done.25.refs_2_), channel_id=1, source_target_pairs={{0,1},{1,0},{2,3},{3,2},{4,5},{5,4},{6,7},{7,6},{8,9},{9,8},{10,11... | collective-permute-start | bytes 1572872 | tf_op jit(solution)/shard_map/ppermute | solution.py:15
  277.7 15.8 %collective-permute-start.31 = (bf16[128,128]{1,0:T(8,128)(2,1)S(1)}, bf16[128,128]{1,0:T(8,128)(2,1)S(1)}, u32[]{:S(2)}, u32[]{:S(2)}) collective-permute-start(bf16[128,128]{1,0:T(8,128)(2,1)S(1)} %copy-done.17), channel_id=1, source_target_pairs={{0,64},{1,65},{2,66},{3,67},{4,68},{5,69},{6,70},{7,71},{8,72},{9,... | collective-permute-start | bytes 98312 | tf_op jit(solution)/shard_map/ppermute | solution.py:15
  295.6 33.8 %all-to-all-start.5 = ((bf16[64,128,128]{2,1,0:T(8,128)(2,1)}), bf16[64,128,128]{2,1,0:T(8,128)(2,1)}, u32[]{:S(2)}, u32[]{:S(2)}) async-start(bf16[64,128,128]{2,1,0:T(8,128)(2,1)} %bitcast.160), calls=%async_computation.5 | async-start | bytes 4194304 | tf_op jit(solution)/shard_map/all_to_all | solution.py:341
  340.5 17.1 %collective-permute-start.39 = (bf16[24,128,128]{2,1,0:T(8,128)(2,1)S(1)}, bf16[24,128,128]{2,1,0:T(8,128)(2,1)S(1)}, u32[]{:S(2)}, u32[]{:S(2)}) collective-permute-start(bf16[24,128,128]{2,1,0:T(8,128)(2,1)S(1)} %bitcast.161), channel_id=1, source_target_pairs={{0,64},{1,65},{2,66},{3,67},{4,68},{5,69},{6,70},{7,71},{8,72},{9,... | collective-permute-start | bytes 2359304 | tf_op jit(solution)/shard_map/ppermute | solution.py:15
  357.6 15.3 %collective-permute-start.41 = (bf16[16,128,256]{2,1,0:T(8,128)(2,1)S(1)}, bf16[16,128,256]{2,1,0:T(8,128)(2,1)}, u32[]{:S(2)}, u32[]{:S(2)}) collective-permute-start(bf16[16,128,256]{2,1,0:T(8,128)(2,1)S(1)} %pad_maximum_fusion.refs_0_), channel_id=1, source_target_pairs={{8,0},{3,1},{10,2},{5,3},{12,4},{7,5},{14,6},{1,7},{16,8},{11,9},{... | collective-permute-start | bytes 3145736 | tf_op jit(solution)/shard_map/ppermute | solution.py:15
  360.3 16.6 %collective-permute-start.42 = (bf16[16,128,256]{2,1,0:T(8,128)(2,1)S(1)}, bf16[16,128,256]{2,1,0:T(8,128)(2,1)}, u32[]{:S(2)}, u32[]{:S(2)}) collective-permute-start(bf16[16,128,256]{2,1,0:T(8,128)(2,1)S(1)} %pad_maximum_fusion.refs_0_), channel_id=1, source_target_pairs={{16,0},{5,1},{18,2},{7,3},{20,4},{1,5},{22,6},{3,7},{24,8},{13,9},... | collective-permute-start | bytes 3145736 | tf_op jit(solution)/shard_map/ppermute | solution.py:15
  362.1 25.0 %collective-permute-start.43 = (bf16[16,128,256]{2,1,0:T(8,128)(2,1)S(1)}, bf16[16,128,256]{2,1,0:T(8,128)(2,1)}, u32[]{:S(2)}, u32[]{:S(2)}) collective-permute-start(bf16[16,128,256]{2,1,0:T(8,128)(2,1)S(1)} %pad_maximum_fusion.refs_0_), channel_id=1, source_target_pairs={{24,0},{7,1},{26,2},{1,3},{28,4},{3,5},{30,6},{5,7},{0,8},{15,9},{... | collective-permute-start | bytes 3145736 | tf_op jit(solution)/shard_map/ppermute | solution.py:15
  362.1 31.7 %collective-permute-start.40 = (bf16[40,128,128]{2,1,0:T(8,128)(2,1)}, bf16[40,128,128]{2,1,0:T(8,128)(2,1)}, u32[]{:S(2)}, u32[]{:S(2)}) collective-permute-start(bf16[40,128,128]{2,1,0:T(8,128)(2,1)} %bitcast.73), channel_id=1, source_target_pairs={{0,64},{1,65},{2,66},{3,67},{4,68},{5,69},{6,70},{7,71},{8,72},{9,... | collective-permute-start | bytes 3932168 | tf_op jit(solution)/shard_map/ppermute | solution.py:15
  364.3 37.8 %collective-permute-start.44 = (bf16[16,128,256]{2,1,0:T(8,128)(2,1)S(1)}, bf16[16,128,256]{2,1,0:T(8,128)(2,1)}, u32[]{:S(2)}, u32[]{:S(2)}) collective-permute-start(bf16[16,128,256]{2,1,0:T(8,128)(2,1)S(1)} %pad_maximum_fusion.refs_0_), channel_id=1, source_target_pairs={{0,1},{1,0},{2,3},{3,2},{4,5},{5,4},{6,7},{7,6},{8,9},{9,8},{10,11... | collective-permute-start | bytes 3145736 | tf_op jit(solution)/shard_map/ppermute | solution.py:15
  372.9 29.3 %collective-permute-start.45 = (bf16[16,128,256]{2,1,0:T(8,128)(2,1)}, bf16[16,128,256]{2,1,0:T(8,128)(2,1)}, u32[]{:S(2)}, u32[]{:S(2)}) collective-permute-start(bf16[16,128,256]{2,1,0:T(8,128)(2,1)} %collective-permute-done.41.refs_1_), channel_id=1, source_target_pairs={{0,1},{1,0},{2,3},{3,2},{4,5},{5,4},{6,7},{7,6},{8,9},{9,8},{10,11... | collective-permute-start | bytes 3145736 | tf_op jit(solution)/shard_map/ppermute | solution.py:15
  376.9 25.2 %collective-permute-start.46 = (bf16[16,128,256]{2,1,0:T(8,128)(2,1)}, bf16[16,128,256]{2,1,0:T(8,128)(2,1)}, u32[]{:S(2)}, u32[]{:S(2)}) collective-permute-start(bf16[16,128,256]{2,1,0:T(8,128)(2,1)} %collective-permute-done.42.refs_2_), channel_id=1, source_target_pairs={{0,1},{1,0},{2,3},{3,2},{4,5},{5,4},{6,7},{7,6},{8,9},{9,8},{10,11... | collective-permute-start | bytes 3145736 | tf_op jit(solution)/shard_map/ppermute | solution.py:15
  387.1 15.1 %collective-permute-start.47 = (bf16[16,128,256]{2,1,0:T(8,128)(2,1)}, bf16[16,128,256]{2,1,0:T(8,128)(2,1)}, u32[]{:S(2)}, u32[]{:S(2)}) collective-permute-start(bf16[16,128,256]{2,1,0:T(8,128)(2,1)} %collective-permute-done.43.refs_3_), channel_id=1, source_target_pairs={{0,1},{1,0},{2,3},{3,2},{4,5},{5,4},{6,7},{7,6},{8,9},{9,8},{10,11... | collective-permute-start | bytes 3145736 | tf_op jit(solution)/shard_map/ppermute | solution.py:15
  (54 other events, 684.3 us)

commit v5 on v4

--- a/solution.py
+++ b/solution.py
@@ -91,11 +91,11 @@
 
 
 def tier_kernel(tier_num, groups, width, span, count, info, column_any, column_ref, *refs):
-    pieces, (final_ref, kept_ref, panel, band, bands_in, sems, band_sems) = (
+    pieces, (final_ref, kept_ref, panel, band, bands_in, top_ref, lower_ref, sems, band_sems) = (
         refs[: 2 * count],
         refs[2 * count :],
     )
-    first, second, role, core = info[0], info[1], info[2], info[3]
+    first, second, role, core, *spots = [info[tier_num * 6 + i] for i in range(6)]
     place = functools.partial(place_of, tier_num, groups)
     chunk = pl.program_id(0)
     part = groups // (2 * count)
@@ -106,7 +106,7 @@
         copies = []
         for side in range(2):
             holder = core if side == 0 else 1 - core
-            position = jnp.where(holder == 0, info[4], info[5])
+            position = jnp.where(holder == 0, spots[0], spots[1])
             for step in range(count):
                 slot = holder * (groups // 2) + ((position + step) & (count - 1)) * part
                 copies.append(
@@ -131,55 +131,51 @@
         at_first, at_second = place(first), place(second)
         top = panel[at_first, :, width:]
 
-        def scale_rows(i, carry):
-            both = panel[pl.ds(i * span, span)].reshape(span * width, 2 * width)
-            change = jnp.dot(both[:, :width], top, preferred_element_type=jnp.float32)
-            fixed = (both[:, width:].astype(jnp.float32) - change).astype(jnp.bfloat16)
-            panel[pl.ds(i * span, span), :, width:] = fixed.reshape(span, width, width)
-            return carry
-
-        lax.fori_loop(0, groups // span, scale_rows, 0)
-        panel[at_first, :, width:] = top
+        top_ref[...] = top
         lower = bands_in[1].astype(jnp.float32) - jnp.dot(
             panel[at_second, :, :width], bands_in[0], preferred_element_type=jnp.float32
         )
+        lower_ref[...] = lower
         band[:width] = bands_in[0]
         band[width:] = lower.astype(jnp.bfloat16)
 
-        @pl.when(role == ROLE_NONE)
+    def patch(block, ref, value):
+        @pl.when((block >= chunk * span) & (block < (chunk + 1) * span))
         def _():
-            panel[at_first, :, :width] = zero
-            panel[at_first, :, width:] = zero
-            panel[at_second, :, width:] = zero
-
-    places = [place(chunk * span + j) for j in range(span)]
+            rows = pl.ds(pl.multiple_of((block - chunk * span) * width, width), width)
+            ref[rows] = value(rows)
+
+    def factors():
+        both = jnp.concatenate([panel[place(chunk * span + j)] for j in range(span)], 0)
+        change = jnp.dot(both[:, :width], top_ref[...], preferred_element_type=jnp.float32)
+        factor1 = (both[:, width:].astype(jnp.float32) - change).astype(jnp.bfloat16)
+        return both[:, :width], factor1
 
     @pl.when(role == ROLE_NONE)
     def _():
-        both = jnp.concatenate([panel[at] for at in places], 0)
-        update = jnp.dot(both, band[...], preferred_element_type=jnp.float32)
+        update = jnp.dot(
+            jnp.concatenate(factors(), 1), band[...], preferred_element_type=jnp.float32
+        )
         value = column_ref[...].astype(jnp.float32) - update
         final_ref[...] = value
+        patch(first, final_ref, lambda rows: column_ref[rows].astype(jnp.float32))
+        patch(second, final_ref, lambda rows: lower_ref[...])
         if kept_ref is not None:
             kept_ref[...] = value.astype(jnp.bfloat16)
-            for block in (first, second):
-
-                @pl.when((block >= chunk * span) & (block < (chunk + 1) * span))
-                def _():
-                    spot = pl.multiple_of((block - chunk * span) * width, width)
-                    kept_ref[pl.ds(spot, width)] = zero
-
-    for j in range(span):
-        rows = pl.ds(j * width, width)
-        at = places[j]
-
-        @pl.when(role == ROLE_FIRST)
-        def _():
-            final_ref[rows] = panel[at, :, :width].astype(jnp.float32)
-
-        @pl.when(role == ROLE_SECOND)
-        def _():
-            final_ref[rows] = panel[at, :, width:].astype(jnp.float32)
+            patch(first, kept_ref, lambda rows: zero)
+            patch(second, kept_ref, lambda rows: zero)
+
+    @pl.when(role == ROLE_FIRST)
+    def _():
+        for j in range(span):
+            final_ref[pl.ds(j * width, width)] = panel[
+                place(chunk * span + j), :, :width
+            ].astype(jnp.float32)
+
+    @pl.when(role == ROLE_SECOND)
+    def _():
+        final_ref[...] = factors()[1].astype(jnp.float32)
+        patch(first, final_ref, lambda rows: top_ref[...].astype(jnp.float32))
 
     if kept_ref is not None:
 
@@ -217,6 +213,8 @@
                 pltpu.VMEM((groups, width, 2 * width), jnp.bfloat16),
                 pltpu.VMEM((2 * width, width), jnp.bfloat16),
                 pltpu.VMEM((2, width, width), jnp.bfloat16),
+                pltpu.VMEM((width, width), jnp.bfloat16),
+                pltpu.VMEM((width, width), jnp.float32),
                 pltpu.SemaphoreType.DMA((2 * count,)),
                 pltpu.SemaphoreType.DMA((2,)),
             ],
@@ -266,17 +264,54 @@
             [jnp.where(local == first, block, zero), jnp.where(local == second, block, zero)], 1
         )
 
-    root_scaled = jnp.dot(front_root, inv_root, preferred_element_type=jnp.float32)
-    root_scaled = root_scaled.astype(jnp.bfloat16).reshape(devices, width, width)
-    root_parts = [root_scaled[:, : width // 2], root_scaled[:, width // 2 :]]
-    root_rows = [None, None]
+    info = []
+    for tier_num in range(4):
+        first, second = pivots_of(tier_num)
+        local = device % (fronts[tier_num].shape[0] // width)
+        role = jnp.where(local == first, ROLE_FIRST, jnp.where(local == second, ROLE_SECOND, ROLE_NONE))
+        axes, count = STAGES[tier_num][-1]
+        spots = [axis_position(device, axis, count) for axis in axes]
+        info += [first, second, role, device & 1, *spots]
+    info = jnp.stack(info).astype(jnp.int32)
+
+    core = device & 1
+    root_first, root_second = pivots_of(3)
+    def spread_root(inverse):
+        root_scaled = jnp.dot(front_root, inverse, preferred_element_type=jnp.float32)
+        root_scaled = root_scaled.astype(jnp.bfloat16).reshape(4, 4, 4, 2, width, width)
+        here = lax.dynamic_index_in_dim(root_scaled, core, 3, keepdims=False)
+        there = lax.dynamic_index_in_dim(root_scaled, 1 - core, 3, keepdims=False)
+        there = permute(there, [(i, i ^ 1) for i in range(devices)])
+        root_block = jnp.stack(
+            [jnp.where(block & 1 == core, here, there) for block in (root_first, root_second)], 3
+        )
+        root_block = jnp.where(core == 0, jnp.transpose(root_block, (2, 0, 1, 3, 4, 5)), root_block)
+        return root_block
+
+    def scatter_stage(block, axes, after):
+        def along(index):
+            return jnp.where(core == 0, axis_position(index, axes[0], 4), axis_position(index, axes[1], 4))
+
+        position = along(device)
+        sent = [
+            lax.dynamic_index_in_dim(block, (position + step) & 3, 0, keepdims=False)
+            for step in range(4)
+        ]
+        if after is not None:
+            after, *sent = lax.optimization_barrier((after, *sent))
+        got = [sent[0]]
+        for step in range(1, 4):
+            got.append(
+                permute(sent[step], [(i, moved(i, axes[i & 1], 4, step)) for i in range(devices)])
+            )
+        panel_dim = got[0].ndim - 3
+        chosen = []
+        for panel, pivot in enumerate((root_first, root_second)):
+            parts = [lax.index_in_dim(piece, panel, panel_dim, keepdims=False) for piece in got]
+            chosen.append(lax.select_n((position - along(pivot)) & 3, *parts))
+        return jnp.stack(chosen, panel_dim), after
+
     sibling_scale = permute(inv_root, [(i, i ^ (devices // 2)) for i in range(devices)])
-
-    def pivot_rows(rows, tier_num):
-        return jnp.concatenate(
-            [lax.dynamic_index_in_dim(rows, block, 0, keepdims=False) for block in pivots_of(tier_num)],
-            1,
-        )
 
     carried_rows = None
     for tier_num in range(4):
@@ -293,9 +328,7 @@
             scaled = jnp.dot(column, inverses[tier_num], preferred_element_type=jnp.float32)
             scaled = scaled.astype(jnp.bfloat16)
             if tier_num > 0:
-                scaled, root_rows[tier_num - 1] = lax.optimization_barrier(
-                    (scaled, root_rows[tier_num - 1])
-                )
+                scaled, root_block = lax.optimization_barrier((scaled, root_block))
             rows = lax.all_to_all(
                 scaled.reshape(groups, width, width), AXIS, 0, 0, axis_index_groups=teams, tiled=True
             )
@@ -307,25 +340,16 @@
                 1,
             )
         else:
-            raw = jnp.concatenate([pivot_rows(rows, tier_num) for rows in root_rows], 0)
+            raw = jnp.concatenate([root_block[0], root_block[1]], 1)
             own = (raw.astype(jnp.float32) + carried_rows).astype(jnp.bfloat16)
         if tier_num < 3:
             pieces, others, _ = gather_rows(own, device, tier_num, None)
+            if tier_num == 0:
+                pieces[1], inverse = lax.optimization_barrier((pieces[1], inv_root))
+                root_block = spread_root(inverse)
         else:
             pieces, others, received = gather_rows(own, device, tier_num, to_send)
             column = assemble(received)
-        axes, count = STAGES[tier_num][-1]
-        role = jnp.where(is_first, ROLE_FIRST, jnp.where(is_second, ROLE_SECOND, ROLE_NONE))
-        info = jnp.stack(
-            [
-                first,
-                second,
-                role,
-                device & 1,
-                axis_position(device, axes[0], count),
-                axis_position(device, axes[1], count),
-            ]
-        ).astype(jnp.int32)
         made = eliminate(tier_num, column, pieces, others, info, tier_num < 3)
         results.append(made[0])
         if tier_num < 3:
@@ -333,8 +357,11 @@
             side_row = child_sides[tier_num]
             parent_half = (device // groups) & 1
             if tier_num < 2:
-                kept, part = lax.optimization_barrier((kept, root_parts[tier_num]))
-                root_rows[tier_num] = lax.all_to_all(part, AXIS, 0, 0, tiled=True)
+                if tier_num == 0:
+                    root_block, kept = scatter_stage(root_block, ("x", "y"), kept)
+                else:
+                    root_block, kept = scatter_stage(root_block, ("y", "z"), kept)
+                    root_block, _ = scatter_stage(root_block, ("z", "x"), None)
             else:
                 landing = jnp.where(side_row[device] == parent_half, inv_root, sibling_scale)
                 grown = jnp.dot(kept, landing, preferred_element_type=jnp.float32)

time: 422 us -> 459 us (1.088); the launches traced: 420 us -> 451 us
  local copies, waits for them, and re-layouts: 22.6 us -> 67.1 us
  waiting for transfers between devices: 175 us -> 147 us
  starting transfers between devices: 129 us -> 137 us
  other arithmetic: 14.5 us -> 21.5 us
    ppermute x48 -> x58, waiting for transfers between devices: 112 us -> 78.9 us  [permute(): return lax.ppermute(array, AXIS, pairs)]
    ppermute x48 -> x58, starting transfers between devices: 86.4 us -> 108 us  [permute(): return lax.ppermute(array, AXIS, pairs)]
    unnamed x48 -> x50, local copies, waits for them, and re-layouts: 5.66 us -> 27 us
    dynamic_slice x3 -> x5, local copies, waits for them, and re-layouts: 0.16 us -> 15.9 us  [the longest x1 15.5 us: spread_root(): here = lax.dynamic_index_in_dim(root_scaled, core, 3, keepdims=False)]
    all_to_all x2 -> x0, starting transfers between devices: 15.8 us -> none  [shards(): root_rows[tier_num] = lax.all_to_all(part, AXIS, 0, 0, tiled=True)]
    reshape x0 -> x1, local copies, waits for them, and re-layouts: none -> 7.71 us  [spread_root(): root_scaled.astype(jnp.bfloat16).reshape(4, 4, 4, 2, width, width)]
  transfers between devices with their start and end apart: 54 -> 62, of which waited for: 25 -> 33; matrix products, arithmetic and copies ran while one was open for 8% -> 8% of each run, Pallas kernels for 2% -> 3%
where the time goes in v5:
time: 459 us; the launch traced here: 451 us
  waiting for transfers between devices  147 us (32%)
  starting transfers between devices  137 us (30%)
  local copies, waits for them, and re-layouts  67.1 us (15%)
  between operations  33.3 us (7%)
  Pallas kernels  32.2 us (7%)
  other arithmetic  21.5 us (5%)
  matrix products  13 us (3%)
    ppermute x58, starting transfers between devices, permute(): return lax.ppermute(array, AXIS, pairs)  108 us
    ppermute x58, waiting for transfers between devices, permute(): return lax.ppermute(array, AXIS, pairs)  78.9 us
    all_to_all x3, waiting for transfers between devices, shards(): lax.all_to_all(scaled.reshape(groups, width, width), AXIS, 0, 0, axis_ind...  43.3 us
    pallas_call x4, Pallas kernels, eliminate(): pl.pallas_call(body, grid_spec=pltpu.PrefetchScalarGridSpec(num_scalar_pr...  32.2 us
    unnamed x50, local copies, waits for them, and re-layouts  27 us
    all_to_all x1, waiting for transfers between devices, shards(): lax.all_to_all(grown.astype(jnp.bfloat16).reshape(groups, width, width),...  24.8 us
    all_to_all x3, starting transfers between devices, shards(): lax.all_to_all(scaled.reshape(groups, width, width), AXIS, 0, 0, axis_ind...  22.7 us
    dynamic_slice x1, local copies, waits for them, and re-layouts, spread_root(): here = lax.dynamic_index_in_dim(root_scaled, core, 3, keepdims=False)  15.5 us
  transfers between devices with their start and end apart: 62, of which 33 were waited for; matrix products, arithmetic and copies ran while one was open for 8% of the time, Pallas kernels for 3%

profile of v5, /device:TPU:1, one launch (start us, length us, event | category | flops | bytes accessed | tf_op | source)
XLA Modules:
  0.0 451.5 jit_solution(5656127421174449928)
XLA Ops:
  2.8 7.2 %all-to-all-start = ((bf16[16,128,128]{2,1,0:T(8,128)(2,1)}), bf16[16,128,128]{2,1,0:T(8,128)(2,1)S(1)}, u32[]{:S(2)}, u32[]{:S(2)}) async-start(bf16[16,128,128]{2,1,0:T(8,128)(2,1)} %bitcast.23), calls=%async_computation | async-start | bytes 1048576 | tf_op jit(solution)/shard_map/all_to_all | solution.py:332
  14.6 5.3 %all-to-all-done = bf16[16,128,128]{2,1,0:T(8,128)(2,1)S(1)} async-done(((bf16[16,128,128]{2,1,0:T(8,128)(2,1)}), bf16[16,128,128]{2,1,0:T(8,128)(2,1)S(1)}, u32[]{:S(2)}, u32[]{:S(2)}) %all-to-all-start) | async-done | bytes 524320 | tf_op jit(solution)/shard_map/all_to_all | solution.py:332
  27.0 5.5 %fusion = bf16[16384,128]{0,1:T(8,128)(2,1)} fusion(bf16[128,128]{1,0:T(8,128)(2,1)S(1)} %copy-done.17, bf16[16384,128]{1,0:T(8,128)(2,1)} %param.16), kind=kOutput, calls=%fused_computation.1 | convolution fusion | flops 538968064 | bytes 8421376 | tf_op jit(solution)/shard_map/dot_general | solution.py:280
  32.5 7.7 %reshape.272 = bf16[4,4,4,2,128,128]{4,3,2,1,0,5:T(2,128)(2,1)} reshape(bf16[16384,128]{0,1:T(8,128)(2,1)} %fusion) | data formatting | bytes 8388608 | tf_op jit(solution)/shard_map/reshape | solution.py:281
  40.2 15.5 %constant_dynamic-slice_fusion.17 = (bf16[4,4,4,1,128,128]{4,3,2,1,0,5:T(2,128)(2,1)}, bf16[4,4,4,1,128,128]{4,3,2,1,0,5:T(2,128)(2,1)}) fusion(bf16[4,4,4,2,128,128]{4,3,2,1,0,5:T(2,128)(2,1)} %reshape.272, s32[]{:T(128)S(6)} %select_n.956, s32[]{:T(128)S(6)} %select_n.957), kind=kLoop, calls=%fused_computation.134 | loop fusion | bytes 8388616 | tf_op jit(solution)/shard_map/jit(dynamic_index_in_dim)/dynamic_slice | solution.py:282
  55.7 10.7 %copy.30 = bf16[4,4,4,1,128,128]{5,4,2,1,0,3:T(8,128)(2,1)} copy(bf16[4,4,4,1,128,128]{4,3,2,1,0,5:T(2,128)(2,1)} %get-tuple-element.67) | data formatting | bytes 4194304
  87.7 5.1 %stack.64.info = s32[24]{0:T(128)S(1)} concatenate(s32[1]{0:T(128)} %bitcast, s32[1]{0:T(128)} %bitcast.1, s32[1]{0:T(128)} %bitcast.4, s32[1]{0:T(128)} %bitcast.5, s32[1]{0:T(128)} %bitcast.6, s32[1]{0:T(128)} %bitcast.6, s32[1]{0:T(128)} %bitcast.7, s32[1]{0:T(128)} %bitcast.8, s32[1]{0:T(128)} %bitcast.11, s32[1]{0:T(128)} %bitcast.5, s32[1]{0:T(128)} %bitcast.12, s32[1]{0:T(128)} %bitcast.6, ...), dimensions={0} | concatenate | bytes 192 | tf_op jit(solution)/shard_map/stack | solution.py:275
  92.7 10.7 %copy.29 = bf16[4,4,4,1,128,128]{5,4,2,1,0,3:T(8,128)(2,1)} copy(bf16[4,4,4,1,128,128]{4,3,2,1,0,5:T(2,128)(2,1)} %get-tuple-element.66) | data formatting | bytes 4194304
  125.7 8.5 %collective-permute-done.9 = bf16[16,128,128]{2,1,0:T(8,128)(2,1)S(1)} collective-permute-done((bf16[16,128,128]{2,1,0:T(8,128)(2,1)S(1)}, bf16[16,128,128]{2,1,0:T(8,128)(2,1)S(1)}, u32[]{:S(2)}, u32[]{:S(2)}) %collective-permute-start.9) | collective-permute-done | bytes 524320 | tf_op jit(solution)/shard_map/ppermute | solution.py:15
  146.2 5.2 %all-to-all-start.1 = ((bf16[32,128,128]{2,1,0:T(8,128)(2,1)}), bf16[32,128,128]{2,1,0:T(8,128)(2,1)S(1)}, u32[]{:S(2)}, u32[]{:S(2)}) async-start(bf16[32,128,128]{2,1,0:T(8,128)(2,1)} %bitcast.46), calls=%async_computation.1 | async-start | bytes 2097152 | tf_op jit(solution)/shard_map/all_to_all | solution.py:332
  155.0 13.6 %all-to-all-done.1 = bf16[32,128,128]{2,1,0:T(8,128)(2,1)S(1)} async-done(((bf16[32,128,128]{2,1,0:T(8,128)(2,1)}), bf16[32,128,128]{2,1,0:T(8,128)(2,1)S(1)}, u32[]{:S(2)}, u32[]{:S(2)}) %all-to-all-start.1) | async-done | bytes 1048608 | tf_op jit(solution)/shard_map/all_to_all | solution.py:332
  218.3 13.3 %collective-permute-done.23 = bf16[32,128,128]{2,1,0:T(8,128)(2,1)S(1)} collective-permute-done((bf16[32,128,128]{2,1,0:T(8,128)(2,1)S(1)}, bf16[32,128,128]{2,1,0:T(8,128)(2,1)S(1)}, u32[]{:S(2)}, u32[]{:S(2)}) %collective-permute-start.23) | collective-permute-done | bytes 1048608 | tf_op jit(solution)/shard_map/ppermute | solution.py:15
  236.8 10.3 %all-to-all-start.2 = ((bf16[64,128,128]{2,1,0:T(8,128)(2,1)}), bf16[64,128,128]{2,1,0:T(8,128)(2,1)}, u32[]{:S(2)}, u32[]{:S(2)}) async-start(bf16[64,128,128]{2,1,0:T(8,128)(2,1)} %bitcast.201), calls=%async_computation.2 | async-start | bytes 4194304 | tf_op jit(solution)/shard_map/all_to_all | solution.py:332
  250.7 24.5 %all-to-all-done.2 = bf16[64,128,128]{2,1,0:T(8,128)(2,1)} async-done(((bf16[64,128,128]{2,1,0:T(8,128)(2,1)}), bf16[64,128,128]{2,1,0:T(8,128)(2,1)}, u32[]{:S(2)}, u32[]{:S(2)}) %all-to-all-start.2) | async-done | bytes 2097184 | tf_op jit(solution)/shard_map/all_to_all | solution.py:332
  282.0 9.3 %collective-permute-start.33 = (bf16[2,128,256]{2,1,0:T(8,128)(2,1)S(1)}, bf16[2,128,256]{2,1,0:T(8,128)(2,1)S(1)}, u32[]{:S(2)}, u32[]{:S(2)}) collective-permute-start(bf16[2,128,256]{2,1,0:T(8,128)(2,1)S(1)} %pad_maximum_fusion.7), channel_id=1, source_target_pairs={{6,0},{25,1},{0,2},{27,3},{2,4},{29,5},{4,6},{31,7},{14,8},{1,9},{... | collective-permute-start | bytes 393224 | tf_op jit(solution)/shard_map/ppermute | solution.py:15
  312.2 5.0 %collective-permute-start.40 = (bf16[8,128,256]{2,1,0:T(8,128)(2,1)}, bf16[8,128,256]{2,1,0:T(8,128)(2,1)}, u32[]{:S(2)}, u32[]{:S(2)}) collective-permute-start(bf16[8,128,256]{2,1,0:T(8,128)(2,1)} %collective-permute-done.36.refs_3_), channel_id=1, source_target_pairs={{0,1},{1,0},{2,3},{3,2},{4,5},{5,4},{6,7},{7,6},{8,9},{9,8},{10,11... | collective-permute-start | bytes 1572872 | tf_op jit(solution)/shard_map/ppermute | solution.py:15
  320.0 8.7 %shard_map.158 = (f32[8192,128]{1,0:T(8,128)}, bf16[8192,128]{1,0:T(8,128)(2,1)S(1)}) custom-call(s32[24]{0:T(128)S(1)} %stack.64.info, bf16[8192,128]{1,0:T(8,128)(2,1)S(1)} %fusion.5.column_any.column_ref, bf16[8192,128]{1,0:T(8,128)(2,1)S(1)} %fusion.5.column_any.column_ref, bf16[8,128,256]{2,1,0:T(8,128)(2,1)S(1)} %pad_maximum_fusion.3.refs_0_, ...), custom_call_target="tpu_custom_call" | custom-call | flops 805306368 | bytes 12582912 | tf_op jit(solution)/shard_map/pallas_call | solution.py:205
  330.8 6.7 %all-to-all-start.3 = ((bf16[64,128,128]{2,1,0:T(8,128)(2,1)}), bf16[64,128,128]{2,1,0:T(8,128)(2,1)}, u32[]{:S(2)}, u32[]{:S(2)}) async-start(bf16[64,128,128]{2,1,0:T(8,128)(2,1)} %bitcast.202), calls=%async_computation.3 | async-start | bytes 4194304 | tf_op jit(solution)/shard_map/all_to_all | solution.py:368
  340.7 24.8 %all-to-all-done.3 = bf16[64,128,128]{2,1,0:T(8,128)(2,1)} async-done(((bf16[64,128,128]{2,1,0:T(8,128)(2,1)}), bf16[64,128,128]{2,1,0:T(8,128)(2,1)}, u32[]{:S(2)}, u32[]{:S(2)}) %all-to-all-start.3) | async-done | bytes 2097184 | tf_op jit(solution)/shard_map/all_to_all | solution.py:368
  388.8 6.0 %collective-permute-done.49 = bf16[24,128,128]{2,1,0:T(8,128)(2,1)S(1)} collective-permute-done((bf16[24,128,128]{2,1,0:T(8,128)(2,1)S(1)}, bf16[24,128,128]{2,1,0:T(8,128)(2,1)S(1)}, u32[]{:S(2)}, u32[]{:S(2)}) %collective-permute-start.49) | collective-permute-done | bytes 786464 | tf_op jit(solution)/shard_map/ppermute | solution.py:15
  399.8 5.3 %collective-permute-start.54 = (bf16[16,128,256]{2,1,0:T(8,128)(2,1)S(1)}, bf16[16,128,256]{2,1,0:T(8,128)(2,1)}, u32[]{:S(2)}, u32[]{:S(2)}) collective-permute-start(bf16[16,128,256]{2,1,0:T(8,128)(2,1)S(1)} %pad_maximum_fusion.2.refs_0_), channel_id=1, source_target_pairs={{0,1},{1,0},{2,3},{3,2},{4,5},{5,4},{6,7},{7,6},{8,9},{9,8},{10,11... | collective-permute-start | bytes 3145736 | tf_op jit(solution)/shard_map/ppermute | solution.py:15
  416.1 7.2 %collective-permute-done.53.refs_3_ = bf16[16,128,256]{2,1,0:T(8,128)(2,1)} collective-permute-done((bf16[16,128,256]{2,1,0:T(8,128)(2,1)S(1)}, bf16[16,128,256]{2,1,0:T(8,128)(2,1)}, u32[]{:S(2)}, u32[]{:S(2)}) %collective-permute-start.53) | collective-permute-done | bytes 1048608 | tf_op jit(solution)/shard_map/ppermute | solution.py:15
  430.6 5.7 %fusion.2.column_any.column_ref = bf16[16384,128]{1,0:T(8,128)(2,1)S(1)} fusion(bf16[16384,128]{1,0:T(8,128)(2,1)S(1)} %copy-done.11, f32[64,128,128]{2,1,0:T(8,128)S(1)} %maximum_convert_fusion, f32[64,128,128]{2,1,0:T(8,128)S(1)} %convert.1, pred[16384]{0:T(1024)(128)(4,1)S(1)} %bitcast.204, pred[16384]{0:T(1024)(128)(4,1)S(1)} %bitcast.205), kind=kLoop, calls=%fused_computation.6 | loop fusion | flops 12582912 | bytes 16809984 | tf_op jit(solution)/shard_map/convert_element_type | solution.py:399
  436.3 15.0 %shard_map.159 = f32[16384,128]{1,0:T(8,128)} custom-call(s32[24]{0:T(128)S(1)} %stack.64.info, bf16[16384,128]{1,0:T(8,128)(2,1)S(1)} %fusion.2.column_any.column_ref, bf16[16384,128]{1,0:T(8,128)(2,1)S(1)} %fusion.2.column_any.column_ref, bf16[16,128,256]{2,1,0:T(8,128)(2,1)S(1)} %pad_maximum_fusion.2.refs_0_, ...), custom_call_target="tpu_custom_call" | custom-call | flops 1610612736 | bytes 25165824 | tf_op jit(solution)/shard_map/pallas_call | solution.py:205
  (234 shorter events, 181.7 us)
Async XLA Ops:
  2.8 17.1 %all-to-all-start = ((bf16[16,128,128]{2,1,0:T(8,128)(2,1)}), bf16[16,128,128]{2,1,0:T(8,128)(2,1)S(1)}, u32[]{:S(2)}, u32[]{:S(2)}) async-start(bf16[16,128,128]{2,1,0:T(8,128)(2,1)} %bitcast.23), calls=%async_computation | async-start | bytes 1048576 | tf_op jit(solution)/shard_map/all_to_all | solution.py:332
  66.4 41.4 %collective-permute-start.8 = (bf16[4,4,4,128,128]{4,3,2,1,0:T(8,128)(2,1)}, bf16[4,4,4,128,128]{4,3,2,1,0:T(8,128)(2,1)}, u32[]{:S(2)}, u32[]{:S(2)}) collective-permute-start(bf16[4,4,4,128,128]{4,3,2,1,0:T(8,128)(2,1)} %bitcast.32), channel_id=1, source_target_pairs={{0,1},{1,0},{2,3},{3,2},{4,5},{5,4},{6,7},{7,6},{8,9},{9,8},{10,11... | collective-permute-start | bytes 6291464 | tf_op jit(solution)/shard_map/ppermute | solution.py:15
  73.4 30.0 %collective-permute-start.4 = (bf16[2,128,256]{2,1,0:T(8,128)(2,1)S(1)}, bf16[2,128,256]{2,1,0:T(8,128)(2,1)S(1)}, u32[]{:S(2)}, u32[]{:S(2)}) collective-permute-start(bf16[2,128,256]{2,1,0:T(8,128)(2,1)S(1)} %pad_maximum_fusion.6.refs_0_), channel_id=1, source_target_pairs={{0,1},{1,0},{2,3},{3,2},{4,5},{5,4},{6,7},{7,6},{8,9},{9,8},{10,11... | collective-permute-start | bytes 393224 | tf_op jit(solution)/shard_map/ppermute | solution.py:15
  74.0 29.5 %collective-permute-start.5 = (bf16[2,128,256]{2,1,0:T(8,128)(2,1)S(1)}, bf16[2,128,256]{2,1,0:T(8,128)(2,1)S(1)}, u32[]{:S(2)}, u32[]{:S(2)}) collective-permute-start(bf16[2,128,256]{2,1,0:T(8,128)(2,1)S(1)} %collective-permute-done.1.refs_1_), channel_id=1, source_target_pairs={{0,1},{1,0},{2,3},{3,2},{4,5},{5,4},{6,7},{7,6},{8,9},{9,8},{10,11... | collective-permute-start | bytes 393224 | tf_op jit(solution)/shard_map/ppermute | solution.py:15
  77.1 26.4 %collective-permute-start.6 = (bf16[2,128,256]{2,1,0:T(8,128)(2,1)S(1)}, bf16[2,128,256]{2,1,0:T(8,128)(2,1)S(1)}, u32[]{:S(2)}, u32[]{:S(2)}) collective-permute-start(bf16[2,128,256]{2,1,0:T(8,128)(2,1)S(1)} %collective-permute-done.2.refs_2_), channel_id=1, source_target_pairs={{0,1},{1,0},{2,3},{3,2},{4,5},{5,4},{6,7},{7,6},{8,9},{9,8},{10,11... | collective-permute-start | bytes 393224 | tf_op jit(solution)/shard_map/ppermute | solution.py:15
  80.2 23.3 %collective-permute-start.7 = (bf16[2,128,256]{2,1,0:T(8,128)(2,1)S(1)}, bf16[2,128,256]{2,1,0:T(8,128)(2,1)S(1)}, u32[]{:S(2)}, u32[]{:S(2)}) collective-permute-start(bf16[2,128,256]{2,1,0:T(8,128)(2,1)S(1)} %collective-permute-done.3.refs_3_), channel_id=1, source_target_pairs={{0,1},{1,0},{2,3},{3,2},{4,5},{5,4},{6,7},{7,6},{8,9},{9,8},{10,11... | collective-permute-start | bytes 393224 | tf_op jit(solution)/shard_map/ppermute | solution.py:15
  113.5 26.0 %collective-permute-start.12 = (bf16[4,4,2,128,128]{4,3,2,1,0:T(8,128)(2,1)}, bf16[4,4,2,128,128]{4,3,2,1,0:T(8,128)(2,1)}, u32[]{:S(2)}, u32[]{:S(2)}) collective-permute-start(bf16[4,4,2,128,128]{4,3,2,1,0:T(8,128)(2,1)} %get-tuple-element.39), channel_id=1, source_target_pairs={{0,6},{1,97},{2,0},{3,99},{4,2},{5,101},{6,4},{7,103},{8,14},{9,10... | collective-permute-start | bytes 3145736 | tf_op jit(solution)/shard_map/ppermute | solution.py:15
  116.3 23.3 %collective-permute-start.11 = (bf16[4,4,2,128,128]{4,3,2,1,0:T(8,128)(2,1)}, bf16[4,4,2,128,128]{4,3,2,1,0:T(8,128)(2,1)}, u32[]{:S(2)}, u32[]{:S(2)}) collective-permute-start(bf16[4,4,2,128,128]{4,3,2,1,0:T(8,128)(2,1)} %get-tuple-element.38), channel_id=1, source_target_pairs={{0,4},{1,65},{2,6},{3,67},{4,0},{5,69},{6,2},{7,71},{8,12},{9,73},... | collective-permute-start | bytes 3145736 | tf_op jit(solution)/shard_map/ppermute | solution.py:15
  116.6 26.4 %collective-permute-start.10 = (bf16[4,4,2,128,128]{4,3,2,1,0:T(8,128)(2,1)}, bf16[4,4,2,128,128]{4,3,2,1,0:T(8,128)(2,1)}, u32[]{:S(2)}, u32[]{:S(2)}) collective-permute-start(bf16[4,4,2,128,128]{4,3,2,1,0:T(8,128)(2,1)} %get-tuple-element.37), channel_id=1, source_target_pairs={{0,2},{1,33},{2,4},{3,35},{4,6},{5,37},{6,0},{7,39},{8,10},{9,41},... | collective-permute-start | bytes 3145736 | tf_op jit(solution)/shard_map/ppermute | solution.py:15
  119.9 14.4 %collective-permute-start.9 = (bf16[16,128,128]{2,1,0:T(8,128)(2,1)S(1)}, bf16[16,128,128]{2,1,0:T(8,128)(2,1)S(1)}, u32[]{:S(2)}, u32[]{:S(2)}) collective-permute-start(bf16[16,128,128]{2,1,0:T(8,128)(2,1)S(1)} %bitcast.199), channel_id=1, source_target_pairs={{0,16},{1,17},{2,18},{3,19},{4,20},{5,21},{6,22},{7,23},{8,24},{9,... | collective-permute-start | bytes 1572872 | tf_op jit(solution)/shard_map/ppermute | solution.py:15
  146.2 22.4 %all-to-all-start.1 = ((bf16[32,128,128]{2,1,0:T(8,128)(2,1)}), bf16[32,128,128]{2,1,0:T(8,128)(2,1)S(1)}, u32[]{:S(2)}, u32[]{:S(2)}) async-start(bf16[32,128,128]{2,1,0:T(8,128)(2,1)} %bitcast.46), calls=%async_computation.1 | async-start | bytes 2097152 | tf_op jit(solution)/shard_map/all_to_all | solution.py:332
  208.3 23.3 %collective-permute-start.23 = (bf16[32,128,128]{2,1,0:T(8,128)(2,1)S(1)}, bf16[32,128,128]{2,1,0:T(8,128)(2,1)S(1)}, u32[]{:S(2)}, u32[]{:S(2)}) collective-permute-start(bf16[32,128,128]{2,1,0:T(8,128)(2,1)S(1)} %bitcast.197), channel_id=1, source_target_pairs={{0,32},{1,33},{2,34},{3,35},{4,36},{5,37},{6,38},{7,39},{8,40},{9,... | collective-permute-start | bytes 3145736 | tf_op jit(solution)/shard_map/ppermute | solution.py:15
  236.8 38.4 %all-to-all-start.2 = ((bf16[64,128,128]{2,1,0:T(8,128)(2,1)}), bf16[64,128,128]{2,1,0:T(8,128)(2,1)}, u32[]{:S(2)}, u32[]{:S(2)}) async-start(bf16[64,128,128]{2,1,0:T(8,128)(2,1)} %bitcast.201), calls=%async_computation.2 | async-start | bytes 4194304 | tf_op jit(solution)/shard_map/all_to_all | solution.py:332
  279.3 14.7 %collective-permute-start.32 = (bf16[2,128,256]{2,1,0:T(8,128)(2,1)S(1)}, bf16[2,128,256]{2,1,0:T(8,128)(2,1)S(1)}, u32[]{:S(2)}, u32[]{:S(2)}) collective-permute-start(bf16[2,128,256]{2,1,0:T(8,128)(2,1)S(1)} %pad_maximum_fusion.7), channel_id=1, source_target_pairs={{4,0},{17,1},{6,2},{19,3},{0,4},{21,5},{2,6},{23,7},{12,8},{25,9},... | collective-permute-start | bytes 393224 | tf_op jit(solution)/shard_map/ppermute | solution.py:15
  298.1 21.9 %collective-permute-start.37 = (bf16[8,128,256]{2,1,0:T(8,128)(2,1)S(1)}, bf16[8,128,256]{2,1,0:T(8,128)(2,1)}, u32[]{:S(2)}, u32[]{:S(2)}) collective-permute-start(bf16[8,128,256]{2,1,0:T(8,128)(2,1)S(1)} %pad_maximum_fusion.3.refs_0_), channel_id=1, source_target_pairs={{0,1},{1,0},{2,3},{3,2},{4,5},{5,4},{6,7},{7,6},{8,9},{9,8},{10,11... | collective-permute-start | bytes 1572872 | tf_op jit(solution)/shard_map/ppermute | solution.py:15
  304.8 15.1 %collective-permute-start.38 = (bf16[8,128,256]{2,1,0:T(8,128)(2,1)S(1)}, bf16[8,128,256]{2,1,0:T(8,128)(2,1)}, u32[]{:S(2)}, u32[]{:S(2)}) collective-permute-start(bf16[8,128,256]{2,1,0:T(8,128)(2,1)S(1)} %collective-permute-done.34.refs_1_), channel_id=1, source_target_pairs={{0,1},{1,0},{2,3},{3,2},{4,5},{5,4},{6,7},{7,6},{8,9},{9,8},{10,11... | collective-permute-start | bytes 1572872 | tf_op jit(solution)/shard_map/ppermute | solution.py:15
  330.8 34.8 %all-to-all-start.3 = ((bf16[64,128,128]{2,1,0:T(8,128)(2,1)}), bf16[64,128,128]{2,1,0:T(8,128)(2,1)}, u32[]{:S(2)}, u32[]{:S(2)}) async-start(bf16[64,128,128]{2,1,0:T(8,128)(2,1)} %bitcast.202), calls=%async_computation.3 | async-start | bytes 4194304 | tf_op jit(solution)/shard_map/all_to_all | solution.py:368
  377.3 17.5 %collective-permute-start.49 = (bf16[24,128,128]{2,1,0:T(8,128)(2,1)S(1)}, bf16[24,128,128]{2,1,0:T(8,128)(2,1)S(1)}, u32[]{:S(2)}, u32[]{:S(2)}) collective-permute-start(bf16[24,128,128]{2,1,0:T(8,128)(2,1)S(1)} %bitcast.203), channel_id=1, source_target_pairs={{0,64},{1,65},{2,66},{3,67},{4,68},{5,69},{6,70},{7,71},{8,72},{9,... | collective-permute-start | bytes 2359304 | tf_op jit(solution)/shard_map/ppermute | solution.py:15
  396.6 17.2 %collective-permute-start.52 = (bf16[16,128,256]{2,1,0:T(8,128)(2,1)S(1)}, bf16[16,128,256]{2,1,0:T(8,128)(2,1)}, u32[]{:S(2)}, u32[]{:S(2)}) collective-permute-start(bf16[16,128,256]{2,1,0:T(8,128)(2,1)S(1)} %pad_maximum_fusion.2.refs_0_), channel_id=1, source_target_pairs={{16,0},{5,1},{18,2},{7,3},{20,4},{1,5},{22,6},{3,7},{24,8},{13,9},... | collective-permute-start | bytes 3145736 | tf_op jit(solution)/shard_map/ppermute | solution.py:15
  398.3 25.0 %collective-permute-start.53 = (bf16[16,128,256]{2,1,0:T(8,128)(2,1)S(1)}, bf16[16,128,256]{2,1,0:T(8,128)(2,1)}, u32[]{:S(2)}, u32[]{:S(2)}) collective-permute-start(bf16[16,128,256]{2,1,0:T(8,128)(2,1)S(1)} %pad_maximum_fusion.2.refs_0_), channel_id=1, source_target_pairs={{24,0},{7,1},{26,2},{1,3},{28,4},{3,5},{30,6},{5,7},{0,8},{15,9},{... | collective-permute-start | bytes 3145736 | tf_op jit(solution)/shard_map/ppermute | solution.py:15
  398.3 29.6 %collective-permute-start.50 = (bf16[40,128,128]{2,1,0:T(8,128)(2,1)}, bf16[40,128,128]{2,1,0:T(8,128)(2,1)}, u32[]{:S(2)}, u32[]{:S(2)}) collective-permute-start(bf16[40,128,128]{2,1,0:T(8,128)(2,1)} %bitcast.89), channel_id=1, source_target_pairs={{0,64},{1,65},{2,66},{3,67},{4,68},{5,69},{6,70},{7,71},{8,72},{9,... | collective-permute-start | bytes 3932168 | tf_op jit(solution)/shard_map/ppermute | solution.py:15
  399.8 36.5 %collective-permute-start.54 = (bf16[16,128,256]{2,1,0:T(8,128)(2,1)S(1)}, bf16[16,128,256]{2,1,0:T(8,128)(2,1)}, u32[]{:S(2)}, u32[]{:S(2)}) collective-permute-start(bf16[16,128,256]{2,1,0:T(8,128)(2,1)S(1)} %pad_maximum_fusion.2.refs_0_), channel_id=1, source_target_pairs={{0,1},{1,0},{2,3},{3,2},{4,5},{5,4},{6,7},{7,6},{8,9},{9,8},{10,11... | collective-permute-start | bytes 3145736 | tf_op jit(solution)/shard_map/ppermute | solution.py:15
  409.1 27.1 %collective-permute-start.55 = (bf16[16,128,256]{2,1,0:T(8,128)(2,1)}, bf16[16,128,256]{2,1,0:T(8,128)(2,1)}, u32[]{:S(2)}, u32[]{:S(2)}) collective-permute-start(bf16[16,128,256]{2,1,0:T(8,128)(2,1)} %collective-permute-done.51.refs_1_), channel_id=1, source_target_pairs={{0,1},{1,0},{2,3},{3,2},{4,5},{5,4},{6,7},{7,6},{8,9},{9,8},{10,11... | collective-permute-start | bytes 3145736 | tf_op jit(solution)/shard_map/ppermute | solution.py:15
  413.7 22.5 %collective-permute-start.56 = (bf16[16,128,256]{2,1,0:T(8,128)(2,1)}, bf16[16,128,256]{2,1,0:T(8,128)(2,1)}, u32[]{:S(2)}, u32[]{:S(2)}) collective-permute-start(bf16[16,128,256]{2,1,0:T(8,128)(2,1)} %collective-permute-done.52.refs_2_), channel_id=1, source_target_pairs={{0,1},{1,0},{2,3},{3,2},{4,5},{5,4},{6,7},{7,6},{8,9},{9,8},{10,11... | collective-permute-start | bytes 3145736 | tf_op jit(solution)/shard_map/ppermute | solution.py:15
  (62 other events, 783.9 us)

commit v6 on v5

--- a/solution.py
+++ b/solution.py
@@ -276,6 +276,7 @@
 
     core = device & 1
     root_first, root_second = pivots_of(3)
+
     def spread_root(inverse):
         root_scaled = jnp.dot(front_root, inverse, preferred_element_type=jnp.float32)
         root_scaled = root_scaled.astype(jnp.bfloat16).reshape(4, 4, 4, 2, width, width)
@@ -311,6 +312,7 @@
             chosen.append(lax.select_n((position - along(pivot)) & 3, *parts))
         return jnp.stack(chosen, panel_dim), after
 
+    root_block = spread_root(inv_root)
     sibling_scale = permute(inv_root, [(i, i ^ (devices // 2)) for i in range(devices)])
 
     carried_rows = None
@@ -344,9 +346,6 @@
             own = (raw.astype(jnp.float32) + carried_rows).astype(jnp.bfloat16)
         if tier_num < 3:
             pieces, others, _ = gather_rows(own, device, tier_num, None)
-            if tier_num == 0:
-                pieces[1], inverse = lax.optimization_barrier((pieces[1], inv_root))
-                root_block = spread_root(inverse)
         else:
             pieces, others, received = gather_rows(own, device, tier_num, to_send)
             column = assemble(received)

time: 459 us -> 399 us (0.87)
  local copies, waits for them, and re-layouts: 67.1 us -> 24.4 us
  starting transfers between devices: 137 us -> 127 us
  waiting for transfers between devices: 147 us -> 142 us
    unnamed x50 -> x48, local copies, waits for them, and re-layouts: 27 us -> 5.62 us
    dynamic_slice x2 -> x0, local copies, waits for them, and re-layouts: 15.8 us -> none  [the longest x1 15.5 us: spread_root(): here = lax.dynamic_index_in_dim(root_scaled, core, 3, keepdims=False)]
    ppermute x58, starting transfers between devices: 108 us -> 99.6 us  [permute(): return lax.ppermute(array, AXIS, pairs)]
    reshape x1 -> x0, local copies, waits for them, and re-layouts: 7.71 us -> none  [spread_root(): root_scaled.astype(jnp.bfloat16).reshape(4, 4, 4, 2, width, width)]
    ppermute x58, waiting for transfers between devices: 78.9 us -> 74.2 us  [permute(): return lax.ppermute(array, AXIS, pairs)]
  transfers between devices with their start and end apart: 62 -> 62, of which waited for: 33 -> 32; matrix products, arithmetic and copies ran while one was open for 8% -> 7% of each run, Pallas kernels for 3% -> 3%
where the time goes in v6:
time: 399 us; the launch traced here: 394 us
  waiting for transfers between devices  142 us (36%)
  starting transfers between devices  127 us (32%)
  between operations  33.1 us (8%)
  Pallas kernels  32.2 us (8%)
  local copies, waits for them, and re-layouts  24.4 us (6%)
  other arithmetic  23.8 us (6%)
  matrix products  11.9 us (3%)
    ppermute x58, starting transfers between devices, permute(): return lax.ppermute(array, AXIS, pairs)  99.6 us
    ppermute x58, waiting for transfers between devices, permute(): return lax.ppermute(array, AXIS, pairs)  74.2 us
    all_to_all x3, waiting for transfers between devices, shards(): lax.all_to_all(scaled.reshape(groups, width, width), AXIS, 0, 0, axis_ind...  43 us
    pallas_call x4, Pallas kernels, eliminate(): pl.pallas_call(body, grid_spec=pltpu.PrefetchScalarGridSpec(num_scalar_pr...  32.2 us
    all_to_all x1, waiting for transfers between devices, shards(): lax.all_to_all(grown.astype(jnp.bfloat16).reshape(groups, width, width),...  24.9 us
    all_to_all x3, starting transfers between devices, shards(): lax.all_to_all(scaled.reshape(groups, width, width), AXIS, 0, 0, axis_ind...  21.3 us
    convert_element_type x3, other arithmetic, assemble(): return total.astype(jnp.bfloat16).reshape(-1, width)  9.85 us
  transfers between devices with their start and end apart: 62, of which 32 were waited for; matrix products, arithmetic and copies ran while one was open for 7% of the time, Pallas kernels for 3%

profile of v6, /device:TPU:1, one launch (start us, length us, event | category | flops | bytes accessed | tf_op | source)
XLA Modules:
  0.0 394.2 jit_solution(13751435926603842864)
XLA Ops:
  0.7 5.4 %convolution_convert_fusion = bf16[16384,128]{1,0:T(8,128)(2,1)} fusion(bf16[16384,128]{1,0:T(8,128)(2,1)} %param.16, bf16[128,128]{1,0:T(8,128)(2,1)} %param.20), kind=kOutput, calls=%fused_computation | convolution fusion | flops 538968064 | bytes 8421376 | tf_op jit(solution)/shard_map/dot_general | solution.py:281
  11.9 5.9 %all-to-all-start = ((bf16[16,128,128]{2,1,0:T(8,128)(2,1)}), bf16[16,128,128]{2,1,0:T(8,128)(2,1)S(1)}, u32[]{:S(2)}, u32[]{:S(2)}) async-start(bf16[16,128,128]{2,1,0:T(8,128)(2,1)} %bitcast.23), calls=%async_computation | async-start | bytes 1048576 | tf_op jit(solution)/shard_map/all_to_all | solution.py:334
  22.3 5.4 %all-to-all-done = bf16[16,128,128]{2,1,0:T(8,128)(2,1)S(1)} async-done(((bf16[16,128,128]{2,1,0:T(8,128)(2,1)}), bf16[16,128,128]{2,1,0:T(8,128)(2,1)S(1)}, u32[]{:S(2)}, u32[]{:S(2)}) %all-to-all-start) | async-done | bytes 524320 | tf_op jit(solution)/shard_map/all_to_all | solution.py:334
  50.1 5.1 %stack.64.info = s32[24]{0:T(128)S(1)} concatenate(s32[1]{0:T(128)} %bitcast, s32[1]{0:T(128)} %bitcast.1, s32[1]{0:T(128)} %bitcast.4, s32[1]{0:T(128)} %bitcast.5, s32[1]{0:T(128)} %bitcast.6, s32[1]{0:T(128)} %bitcast.6, s32[1]{0:T(128)} %bitcast.7, s32[1]{0:T(128)} %bitcast.8, s32[1]{0:T(128)} %bitcast.11, s32[1]{0:T(128)} %bitcast.5, s32[1]{0:T(128)} %bitcast.12, s32[1]{0:T(128)} %bitcast.6, ...), dimensions={0} | concatenate | bytes 192 | tf_op jit(solution)/shard_map/stack | solution.py:275
  55.3 4.3 %shard_map.156 = (f32[2048,128]{1,0:T(8,128)}, bf16[2048,128]{1,0:T(8,128)(2,1)S(1)}) custom-call(s32[24]{0:T(128)S(1)} %stack.64.info, bf16[2048,128]{1,0:T(8,128)(2,1)S(1)} %copy-done.4, bf16[2048,128]{1,0:T(8,128)(2,1)S(1)} %copy-done.4, bf16[2,128,256]{2,1,0:T(8,128)(2,1)S(1)} %pad_maximum_fusion.6.refs_0_, ...), custom_call_target="tpu_custom_call" | custom-call | flops 201326592 | bytes 3145728 | tf_op jit(solution)/shard_map/pallas_call | solution.py:205
  78.0 8.5 %collective-permute-done.9 = bf16[16,128,128]{2,1,0:T(8,128)(2,1)S(1)} collective-permute-done((bf16[16,128,128]{2,1,0:T(8,128)(2,1)S(1)}, bf16[16,128,128]{2,1,0:T(8,128)(2,1)S(1)}, u32[]{:S(2)}, u32[]{:S(2)}) %collective-permute-start.9) | collective-permute-done | bytes 524320 | tf_op jit(solution)/shard_map/ppermute | solution.py:15
  98.0 5.9 %all-to-all-start.1 = ((bf16[32,128,128]{2,1,0:T(8,128)(2,1)}), bf16[32,128,128]{2,1,0:T(8,128)(2,1)S(1)}, u32[]{:S(2)}, u32[]{:S(2)}) async-start(bf16[32,128,128]{2,1,0:T(8,128)(2,1)} %bitcast.47), calls=%async_computation.1 | async-start | bytes 2097152 | tf_op jit(solution)/shard_map/all_to_all | solution.py:334
  107.7 13.4 %all-to-all-done.1 = bf16[32,128,128]{2,1,0:T(8,128)(2,1)S(1)} async-done(((bf16[32,128,128]{2,1,0:T(8,128)(2,1)}), bf16[32,128,128]{2,1,0:T(8,128)(2,1)S(1)}, u32[]{:S(2)}, u32[]{:S(2)}) %all-to-all-start.1) | async-done | bytes 1048608 | tf_op jit(solution)/shard_map/all_to_all | solution.py:334
  147.3 4.3 %shard_map.157 = (f32[4096,128]{1,0:T(8,128)}, bf16[4096,128]{1,0:T(8,128)(2,1)S(1)}) custom-call(s32[24]{0:T(128)S(1)} %stack.64.info, bf16[4096,128]{1,0:T(8,128)(2,1)S(1)} %fusion.8.column_any.column_ref, bf16[4096,128]{1,0:T(8,128)(2,1)S(1)} %fusion.8.column_any.column_ref, bf16[4,128,256]{2,1,0:T(8,128)(2,1)S(1)} %pad_maximum_fusion.4.refs_0_, ...), custom_call_target="tpu_custom_call" | custom-call | flops 402653184 | bytes 6291456 | tf_op jit(solution)/shard_map/pallas_call | solution.py:205
  171.1 13.9 %collective-permute-done.23 = bf16[32,128,128]{2,1,0:T(8,128)(2,1)S(1)} collective-permute-done((bf16[32,128,128]{2,1,0:T(8,128)(2,1)S(1)}, bf16[32,128,128]{2,1,0:T(8,128)(2,1)S(1)}, u32[]{:S(2)}, u32[]{:S(2)}) %collective-permute-start.23) | collective-permute-done | bytes 1048608 | tf_op jit(solution)/shard_map/ppermute | solution.py:15
  190.1 9.6 %all-to-all-start.2 = ((bf16[64,128,128]{2,1,0:T(8,128)(2,1)}), bf16[64,128,128]{2,1,0:T(8,128)(2,1)}, u32[]{:S(2)}, u32[]{:S(2)}) async-start(bf16[64,128,128]{2,1,0:T(8,128)(2,1)} %bitcast.204), calls=%async_computation.2 | async-start | bytes 4194304 | tf_op jit(solution)/shard_map/all_to_all | solution.py:334
  203.6 24.2 %all-to-all-done.2 = bf16[64,128,128]{2,1,0:T(8,128)(2,1)} async-done(((bf16[64,128,128]{2,1,0:T(8,128)(2,1)}), bf16[64,128,128]{2,1,0:T(8,128)(2,1)}, u32[]{:S(2)}, u32[]{:S(2)}) %all-to-all-start.2) | async-done | bytes 2097184 | tf_op jit(solution)/shard_map/all_to_all | solution.py:334
  256.6 3.9 %collective-permute-start.40 = (bf16[8,128,256]{2,1,0:T(8,128)(2,1)}, bf16[8,128,256]{2,1,0:T(8,128)(2,1)}, u32[]{:S(2)}, u32[]{:S(2)}) collective-permute-start(bf16[8,128,256]{2,1,0:T(8,128)(2,1)} %collective-permute-done.36.refs_3_), channel_id=1, source_target_pairs={{0,1},{1,0},{2,3},{3,2},{4,5},{5,4},{6,7},{7,6},{8,9},{9,8},{10,11... | collective-permute-start | bytes 1572872 | tf_op jit(solution)/shard_map/ppermute | solution.py:15
  263.9 8.7 %shard_map.158 = (f32[8192,128]{1,0:T(8,128)}, bf16[8192,128]{1,0:T(8,128)(2,1)S(1)}) custom-call(s32[24]{0:T(128)S(1)} %stack.64.info, bf16[8192,128]{1,0:T(8,128)(2,1)S(1)} %fusion.4.column_any.column_ref, bf16[8192,128]{1,0:T(8,128)(2,1)S(1)} %fusion.4.column_any.column_ref, bf16[8,128,256]{2,1,0:T(8,128)(2,1)S(1)} %pad_maximum_fusion.3.refs_0_, ...), custom_call_target="tpu_custom_call" | custom-call | flops 805306368 | bytes 12582912 | tf_op jit(solution)/shard_map/pallas_call | solution.py:205
  274.6 5.8 %all-to-all-start.3 = ((bf16[64,128,128]{2,1,0:T(8,128)(2,1)}), bf16[64,128,128]{2,1,0:T(8,128)(2,1)}, u32[]{:S(2)}, u32[]{:S(2)}) async-start(bf16[64,128,128]{2,1,0:T(8,128)(2,1)} %bitcast.205), calls=%async_computation.3 | async-start | bytes 4194304 | tf_op jit(solution)/shard_map/all_to_all | solution.py:367
  283.6 24.9 %all-to-all-done.3 = bf16[64,128,128]{2,1,0:T(8,128)(2,1)} async-done(((bf16[64,128,128]{2,1,0:T(8,128)(2,1)}), bf16[64,128,128]{2,1,0:T(8,128)(2,1)}, u32[]{:S(2)}, u32[]{:S(2)}) %all-to-all-start.3) | async-done | bytes 2097184 | tf_op jit(solution)/shard_map/all_to_all | solution.py:367
  331.8 5.8 %collective-permute-done.49 = bf16[24,128,128]{2,1,0:T(8,128)(2,1)S(1)} collective-permute-done((bf16[24,128,128]{2,1,0:T(8,128)(2,1)S(1)}, bf16[24,128,128]{2,1,0:T(8,128)(2,1)S(1)}, u32[]{:S(2)}, u32[]{:S(2)}) %collective-permute-start.49) | collective-permute-done | bytes 786464 | tf_op jit(solution)/shard_map/ppermute | solution.py:15
  343.3 4.7 %collective-permute-start.54 = (bf16[16,128,256]{2,1,0:T(8,128)(2,1)S(1)}, bf16[16,128,256]{2,1,0:T(8,128)(2,1)}, u32[]{:S(2)}, u32[]{:S(2)}) collective-permute-start(bf16[16,128,256]{2,1,0:T(8,128)(2,1)S(1)} %pad_maximum_fusion.2.refs_0_), channel_id=1, source_target_pairs={{0,1},{1,0},{2,3},{3,2},{4,5},{5,4},{6,7},{7,6},{8,9},{9,8},{10,11... | collective-permute-start | bytes 3145736 | tf_op jit(solution)/shard_map/ppermute | solution.py:15
  348.1 3.8 collective-permute-done.51.refs_1_
  351.9 4.6 %collective-permute-start.55 = (bf16[16,128,256]{2,1,0:T(8,128)(2,1)}, bf16[16,128,256]{2,1,0:T(8,128)(2,1)}, u32[]{:S(2)}, u32[]{:S(2)}) collective-permute-start(bf16[16,128,256]{2,1,0:T(8,128)(2,1)} %collective-permute-done.51.refs_1_), channel_id=1, source_target_pairs={{0,1},{1,0},{2,3},{3,2},{4,5},{5,4},{6,7},{7,6},{8,9},{9,8},{10,11... | collective-permute-start | bytes 3145736 | tf_op jit(solution)/shard_map/ppermute | solution.py:15
  358.9 7.2 %collective-permute-done.53.refs_3_ = bf16[16,128,256]{2,1,0:T(8,128)(2,1)} collective-permute-done((bf16[16,128,256]{2,1,0:T(8,128)(2,1)S(1)}, bf16[16,128,256]{2,1,0:T(8,128)(2,1)}, u32[]{:S(2)}, u32[]{:S(2)}) %collective-permute-start.53) | collective-permute-done | bytes 1048608 | tf_op jit(solution)/shard_map/ppermute | solution.py:15
  366.1 3.9 collective-permute-start.57
  373.3 5.7 %fusion.1.column_any.column_ref = bf16[16384,128]{1,0:T(8,128)(2,1)S(1)} fusion(bf16[16384,128]{1,0:T(8,128)(2,1)S(1)} %copy-done.11, f32[64,128,128]{2,1,0:T(8,128)S(1)} %maximum_convert_fusion, f32[64,128,128]{2,1,0:T(8,128)S(1)} %convert.1, pred[16384]{0:T(1024)(128)(4,1)S(1)} %bitcast.207, pred[16384]{0:T(1024)(128)(4,1)S(1)} %bitcast.208), kind=kLoop, calls=%fused_computation.5 | loop fusion | flops 12582912 | bytes 16809984 | tf_op jit(solution)/shard_map/convert_element_type | solution.py:398
  379.0 15.0 %shard_map.159 = f32[16384,128]{1,0:T(8,128)} custom-call(s32[24]{0:T(128)S(1)} %stack.64.info, bf16[16384,128]{1,0:T(8,128)(2,1)S(1)} %fusion.1.column_any.column_ref, bf16[16384,128]{1,0:T(8,128)(2,1)S(1)} %fusion.1.column_any.column_ref, bf16[16,128,256]{2,1,0:T(8,128)(2,1)S(1)} %pad_maximum_fusion.2.refs_0_, ...), custom_call_target="tpu_custom_call" | custom-call | flops 1610612736 | bytes 25165824 | tf_op jit(solution)/shard_map/pallas_call | solution.py:205
  (228 shorter events, 161.3 us)
Async XLA Ops:
  9.3 50.2 %collective-permute-start.8 = (bf16[4,4,4,128,128]{4,3,2,1,0:T(8,128)(2,1)}, bf16[4,4,4,128,128]{4,3,2,1,0:T(8,128)(2,1)}, u32[]{:S(2)}, u32[]{:S(2)}) collective-permute-start(bf16[4,4,4,128,128]{4,3,2,1,0:T(8,128)(2,1)} %dynamic-slice_bitcast_fusion), channel_id=1, source_target_pairs={{0,1},{1,0},{2,3},{3,2},{4,5},{5,4},{6,7},{7,6},{8,9},{9,8},{10,11... | collective-permute-start | bytes 6291464 | tf_op jit(solution)/shard_map/ppermute | solution.py:15
  11.9 15.7 %all-to-all-start = ((bf16[16,128,128]{2,1,0:T(8,128)(2,1)}), bf16[16,128,128]{2,1,0:T(8,128)(2,1)S(1)}, u32[]{:S(2)}, u32[]{:S(2)}) async-start(bf16[16,128,128]{2,1,0:T(8,128)(2,1)} %bitcast.23), calls=%async_computation | async-start | bytes 1048576 | tf_op jit(solution)/shard_map/all_to_all | solution.py:334
  34.2 21.1 %collective-permute-start.4 = (bf16[2,128,256]{2,1,0:T(8,128)(2,1)S(1)}, bf16[2,128,256]{2,1,0:T(8,128)(2,1)S(1)}, u32[]{:S(2)}, u32[]{:S(2)}) collective-permute-start(bf16[2,128,256]{2,1,0:T(8,128)(2,1)S(1)} %pad_maximum_fusion.6.refs_0_), channel_id=1, source_target_pairs={{0,1},{1,0},{2,3},{3,2},{4,5},{5,4},{6,7},{7,6},{8,9},{9,8},{10,11... | collective-permute-start | bytes 393224 | tf_op jit(solution)/shard_map/ppermute | solution.py:15
  36.6 18.6 %collective-permute-start.5 = (bf16[2,128,256]{2,1,0:T(8,128)(2,1)S(1)}, bf16[2,128,256]{2,1,0:T(8,128)(2,1)S(1)}, u32[]{:S(2)}, u32[]{:S(2)}) collective-permute-start(bf16[2,128,256]{2,1,0:T(8,128)(2,1)S(1)} %collective-permute-done.1.refs_1_), channel_id=1, source_target_pairs={{0,1},{1,0},{2,3},{3,2},{4,5},{5,4},{6,7},{7,6},{8,9},{9,8},{10,11... | collective-permute-start | bytes 393224 | tf_op jit(solution)/shard_map/ppermute | solution.py:15
  39.4 15.8 %collective-permute-start.6 = (bf16[2,128,256]{2,1,0:T(8,128)(2,1)S(1)}, bf16[2,128,256]{2,1,0:T(8,128)(2,1)S(1)}, u32[]{:S(2)}, u32[]{:S(2)}) collective-permute-start(bf16[2,128,256]{2,1,0:T(8,128)(2,1)S(1)} %collective-permute-done.2.refs_2_), channel_id=1, source_target_pairs={{0,1},{1,0},{2,3},{3,2},{4,5},{5,4},{6,7},{7,6},{8,9},{9,8},{10,11... | collective-permute-start | bytes 393224 | tf_op jit(solution)/shard_map/ppermute | solution.py:15
  66.3 25.2 %collective-permute-start.12 = (bf16[4,4,2,128,128]{4,3,2,1,0:T(8,128)(2,1)}, bf16[4,4,2,128,128]{4,3,2,1,0:T(8,128)(2,1)}, u32[]{:S(2)}, u32[]{:S(2)}) collective-permute-start(bf16[4,4,2,128,128]{4,3,2,1,0:T(8,128)(2,1)} %get-tuple-element.35), channel_id=1, source_target_pairs={{0,6},{1,97},{2,0},{3,99},{4,2},{5,101},{6,4},{7,103},{8,14},{9,10... | collective-permute-start | bytes 3145736 | tf_op jit(solution)/shard_map/ppermute | solution.py:15
  68.1 23.3 %collective-permute-start.11 = (bf16[4,4,2,128,128]{4,3,2,1,0:T(8,128)(2,1)}, bf16[4,4,2,128,128]{4,3,2,1,0:T(8,128)(2,1)}, u32[]{:S(2)}, u32[]{:S(2)}) collective-permute-start(bf16[4,4,2,128,128]{4,3,2,1,0:T(8,128)(2,1)} %get-tuple-element.34), channel_id=1, source_target_pairs={{0,4},{1,65},{2,6},{3,67},{4,0},{5,69},{6,2},{7,71},{8,12},{9,73},... | collective-permute-start | bytes 3145736 | tf_op jit(solution)/shard_map/ppermute | solution.py:15
  69.4 25.5 %collective-permute-start.10 = (bf16[4,4,2,128,128]{4,3,2,1,0:T(8,128)(2,1)S(1)}, bf16[4,4,2,128,128]{4,3,2,1,0:T(8,128)(2,1)}, u32[]{:S(2)}, u32[]{:S(2)}) collective-permute-start(bf16[4,4,2,128,128]{4,3,2,1,0:T(8,128)(2,1)S(1)} %get-tuple-element.33), channel_id=1, source_target_pairs={{0,2},{1,33},{2,4},{3,35},{4,6},{5,37},{6,0},{7,39},{8,10},{9,41},... | collective-permute-start | bytes 3145736 | tf_op jit(solution)/shard_map/ppermute | solution.py:15
  72.5 14.0 %collective-permute-start.9 = (bf16[16,128,128]{2,1,0:T(8,128)(2,1)S(1)}, bf16[16,128,128]{2,1,0:T(8,128)(2,1)S(1)}, u32[]{:S(2)}, u32[]{:S(2)}) collective-permute-start(bf16[16,128,128]{2,1,0:T(8,128)(2,1)S(1)} %bitcast.200), channel_id=1, source_target_pairs={{0,16},{1,17},{2,18},{3,19},{4,20},{5,21},{6,22},{7,23},{8,24},{9,... | collective-permute-start | bytes 1572872 | tf_op jit(solution)/shard_map/ppermute | solution.py:15
  98.0 23.1 %all-to-all-start.1 = ((bf16[32,128,128]{2,1,0:T(8,128)(2,1)}), bf16[32,128,128]{2,1,0:T(8,128)(2,1)S(1)}, u32[]{:S(2)}, u32[]{:S(2)}) async-start(bf16[32,128,128]{2,1,0:T(8,128)(2,1)} %bitcast.47), calls=%async_computation.1 | async-start | bytes 2097152 | tf_op jit(solution)/shard_map/all_to_all | solution.py:334
  161.3 23.6 %collective-permute-start.23 = (bf16[32,128,128]{2,1,0:T(8,128)(2,1)S(1)}, bf16[32,128,128]{2,1,0:T(8,128)(2,1)S(1)}, u32[]{:S(2)}, u32[]{:S(2)}) collective-permute-start(bf16[32,128,128]{2,1,0:T(8,128)(2,1)S(1)} %bitcast.198), channel_id=1, source_target_pairs={{0,32},{1,33},{2,34},{3,35},{4,36},{5,37},{6,38},{7,39},{8,40},{9,... | collective-permute-start | bytes 3145736 | tf_op jit(solution)/shard_map/ppermute | solution.py:15
  190.1 37.6 %all-to-all-start.2 = ((bf16[64,128,128]{2,1,0:T(8,128)(2,1)}), bf16[64,128,128]{2,1,0:T(8,128)(2,1)}, u32[]{:S(2)}, u32[]{:S(2)}) async-start(bf16[64,128,128]{2,1,0:T(8,128)(2,1)} %bitcast.204), calls=%async_computation.2 | async-start | bytes 4194304 | tf_op jit(solution)/shard_map/all_to_all | solution.py:334
  242.6 14.0 %collective-permute-start.36 = (bf16[8,128,256]{2,1,0:T(8,128)(2,1)S(1)}, bf16[8,128,256]{2,1,0:T(8,128)(2,1)}, u32[]{:S(2)}, u32[]{:S(2)}) collective-permute-start(bf16[8,128,256]{2,1,0:T(8,128)(2,1)S(1)} %pad_maximum_fusion.3.refs_0_), channel_id=1, source_target_pairs={{24,0},{7,1},{26,2},{1,3},{28,4},{3,5},{30,6},{5,7},{0,8},{15,9},{... | collective-permute-start | bytes 1572872 | tf_op jit(solution)/shard_map/ppermute | solution.py:15
  242.7 21.2 %collective-permute-start.37 = (bf16[8,128,256]{2,1,0:T(8,128)(2,1)S(1)}, bf16[8,128,256]{2,1,0:T(8,128)(2,1)}, u32[]{:S(2)}, u32[]{:S(2)}) collective-permute-start(bf16[8,128,256]{2,1,0:T(8,128)(2,1)S(1)} %pad_maximum_fusion.3.refs_0_), channel_id=1, source_target_pairs={{0,1},{1,0},{2,3},{3,2},{4,5},{5,4},{6,7},{7,6},{8,9},{9,8},{10,11... | collective-permute-start | bytes 1572872 | tf_op jit(solution)/shard_map/ppermute | solution.py:15
  248.4 15.4 %collective-permute-start.38 = (bf16[8,128,256]{2,1,0:T(8,128)(2,1)S(1)}, bf16[8,128,256]{2,1,0:T(8,128)(2,1)}, u32[]{:S(2)}, u32[]{:S(2)}) collective-permute-start(bf16[8,128,256]{2,1,0:T(8,128)(2,1)S(1)} %collective-permute-done.34.refs_1_), channel_id=1, source_target_pairs={{0,1},{1,0},{2,3},{3,2},{4,5},{5,4},{6,7},{7,6},{8,9},{9,8},{10,11... | collective-permute-start | bytes 1572872 | tf_op jit(solution)/shard_map/ppermute | solution.py:15
  274.6 33.8 %all-to-all-start.3 = ((bf16[64,128,128]{2,1,0:T(8,128)(2,1)}), bf16[64,128,128]{2,1,0:T(8,128)(2,1)}, u32[]{:S(2)}, u32[]{:S(2)}) async-start(bf16[64,128,128]{2,1,0:T(8,128)(2,1)} %bitcast.205), calls=%async_computation.3 | async-start | bytes 4194304 | tf_op jit(solution)/shard_map/all_to_all | solution.py:367
  320.0 17.5 %collective-permute-start.49 = (bf16[24,128,128]{2,1,0:T(8,128)(2,1)S(1)}, bf16[24,128,128]{2,1,0:T(8,128)(2,1)S(1)}, u32[]{:S(2)}, u32[]{:S(2)}) collective-permute-start(bf16[24,128,128]{2,1,0:T(8,128)(2,1)S(1)} %bitcast.206), channel_id=1, source_target_pairs={{0,64},{1,65},{2,66},{3,67},{4,68},{5,69},{6,70},{7,71},{8,72},{9,... | collective-permute-start | bytes 2359304 | tf_op jit(solution)/shard_map/ppermute | solution.py:15
  337.6 14.3 %collective-permute-start.51 = (bf16[16,128,256]{2,1,0:T(8,128)(2,1)S(1)}, bf16[16,128,256]{2,1,0:T(8,128)(2,1)}, u32[]{:S(2)}, u32[]{:S(2)}) collective-permute-start(bf16[16,128,256]{2,1,0:T(8,128)(2,1)S(1)} %pad_maximum_fusion.2.refs_0_), channel_id=1, source_target_pairs={{8,0},{3,1},{10,2},{5,3},{12,4},{7,5},{14,6},{1,7},{16,8},{11,9},{... | collective-permute-start | bytes 3145736 | tf_op jit(solution)/shard_map/ppermute | solution.py:15
  339.3 17.2 %collective-permute-start.52 = (bf16[16,128,256]{2,1,0:T(8,128)(2,1)S(1)}, bf16[16,128,256]{2,1,0:T(8,128)(2,1)}, u32[]{:S(2)}, u32[]{:S(2)}) collective-permute-start(bf16[16,128,256]{2,1,0:T(8,128)(2,1)S(1)} %pad_maximum_fusion.2.refs_0_), channel_id=1, source_target_pairs={{16,0},{5,1},{18,2},{7,3},{20,4},{1,5},{22,6},{3,7},{24,8},{13,9},... | collective-permute-start | bytes 3145736 | tf_op jit(solution)/shard_map/ppermute | solution.py:15
  341.1 25.0 %collective-permute-start.53 = (bf16[16,128,256]{2,1,0:T(8,128)(2,1)S(1)}, bf16[16,128,256]{2,1,0:T(8,128)(2,1)}, u32[]{:S(2)}, u32[]{:S(2)}) collective-permute-start(bf16[16,128,256]{2,1,0:T(8,128)(2,1)S(1)} %pad_maximum_fusion.2.refs_0_), channel_id=1, source_target_pairs={{24,0},{7,1},{26,2},{1,3},{28,4},{3,5},{30,6},{5,7},{0,8},{15,9},{... | collective-permute-start | bytes 3145736 | tf_op jit(solution)/shard_map/ppermute | solution.py:15
  341.1 29.6 %collective-permute-start.50 = (bf16[40,128,128]{2,1,0:T(8,128)(2,1)}, bf16[40,128,128]{2,1,0:T(8,128)(2,1)}, u32[]{:S(2)}, u32[]{:S(2)}) collective-permute-start(bf16[40,128,128]{2,1,0:T(8,128)(2,1)} %bitcast.90), channel_id=1, source_target_pairs={{0,64},{1,65},{2,66},{3,67},{4,68},{5,69},{6,70},{7,71},{8,72},{9,... | collective-permute-start | bytes 3932168 | tf_op jit(solution)/shard_map/ppermute | solution.py:15
  343.3 35.6 %collective-permute-start.54 = (bf16[16,128,256]{2,1,0:T(8,128)(2,1)S(1)}, bf16[16,128,256]{2,1,0:T(8,128)(2,1)}, u32[]{:S(2)}, u32[]{:S(2)}) collective-permute-start(bf16[16,128,256]{2,1,0:T(8,128)(2,1)S(1)} %pad_maximum_fusion.2.refs_0_), channel_id=1, source_target_pairs={{0,1},{1,0},{2,3},{3,2},{4,5},{5,4},{6,7},{7,6},{8,9},{9,8},{10,11... | collective-permute-start | bytes 3145736 | tf_op jit(solution)/shard_map/ppermute | solution.py:15
  351.9 27.1 %collective-permute-start.55 = (bf16[16,128,256]{2,1,0:T(8,128)(2,1)}, bf16[16,128,256]{2,1,0:T(8,128)(2,1)}, u32[]{:S(2)}, u32[]{:S(2)}) collective-permute-start(bf16[16,128,256]{2,1,0:T(8,128)(2,1)} %collective-permute-done.51.refs_1_), channel_id=1, source_target_pairs={{0,1},{1,0},{2,3},{3,2},{4,5},{5,4},{6,7},{7,6},{8,9},{9,8},{10,11... | collective-permute-start | bytes 3145736 | tf_op jit(solution)/shard_map/ppermute | solution.py:15
  356.5 22.5 %collective-permute-start.56 = (bf16[16,128,256]{2,1,0:T(8,128)(2,1)}, bf16[16,128,256]{2,1,0:T(8,128)(2,1)}, u32[]{:S(2)}, u32[]{:S(2)}) collective-permute-start(bf16[16,128,256]{2,1,0:T(8,128)(2,1)} %collective-permute-done.52.refs_2_), channel_id=1, source_target_pairs={{0,1},{1,0},{2,3},{3,2},{4,5},{5,4},{6,7},{7,6},{8,9},{9,8},{10,11... | collective-permute-start | bytes 3145736 | tf_op jit(solution)/shard_map/ppermute | solution.py:15
  (62 other events, 756.0 us)

commit v7 on v6

--- a/solution.py
+++ b/solution.py
@@ -95,7 +95,7 @@
         refs[: 2 * count],
         refs[2 * count :],
     )
-    first, second, role, core, *spots = [info[tier_num * 6 + i] for i in range(6)]
+    first, second, role, core, *spots = [info[i] for i in range(6)]
     place = functools.partial(place_of, tier_num, groups)
     chunk = pl.program_id(0)
     part = groups // (2 * count)
@@ -264,16 +264,6 @@
             [jnp.where(local == first, block, zero), jnp.where(local == second, block, zero)], 1
         )
 
-    info = []
-    for tier_num in range(4):
-        first, second = pivots_of(tier_num)
-        local = device % (fronts[tier_num].shape[0] // width)
-        role = jnp.where(local == first, ROLE_FIRST, jnp.where(local == second, ROLE_SECOND, ROLE_NONE))
-        axes, count = STAGES[tier_num][-1]
-        spots = [axis_position(device, axis, count) for axis in axes]
-        info += [first, second, role, device & 1, *spots]
-    info = jnp.stack(info).astype(jnp.int32)
-
     core = device & 1
     root_first, root_second = pivots_of(3)
 
@@ -349,6 +339,10 @@
         else:
             pieces, others, received = gather_rows(own, device, tier_num, to_send)
             column = assemble(received)
+        axes, count = STAGES[tier_num][-1]
+        role = jnp.where(is_first, ROLE_FIRST, jnp.where(is_second, ROLE_SECOND, ROLE_NONE))
+        spots = [axis_position(device, axis, count) for axis in axes]
+        info = jnp.stack([first, second, role, device & 1, *spots]).astype(jnp.int32)
         made = eliminate(tier_num, column, pieces, others, info, tier_num < 3)
         results.append(made[0])
         if tier_num < 3:

time: 399 us -> 397 us (level)
  transfers between devices with their start and end apart: 62 -> 62, of which waited for: 32 -> 31; matrix products, arithmetic and copies ran while one was open for 7% -> 7% of each run, Pallas kernels for 3% -> 3%
where the time goes in v7:
time: 397 us; the launch traced here: 395 us
  waiting for transfers between devices  141 us (36%)
  starting transfers between devices  125 us (31%)
  between operations  33.7 us (8%)
  Pallas kernels  32.2 us (8%)
  other arithmetic  25.2 us (6%)
  local copies, waits for them, and re-layouts  24.8 us (6%)
  matrix products  11.9 us (3%)
    ppermute x58, starting transfers between devices, permute(): return lax.ppermute(array, AXIS, pairs)  99 us
    ppermute x58, waiting for transfers between devices, permute(): return lax.ppermute(array, AXIS, pairs)  75 us
    all_to_all x3, waiting for transfers between devices, shards(): lax.all_to_all(scaled.reshape(groups, width, width), AXIS, 0, 0, axis_ind...  41.6 us
    pallas_call x4, Pallas kernels, eliminate(): pl.pallas_call(body, grid_spec=pltpu.PrefetchScalarGridSpec(num_scalar_pr...  32.2 us
    all_to_all x1, waiting for transfers between devices, shards(): lax.all_to_all(grown.astype(jnp.bfloat16).reshape(groups, width, width),...  24.9 us
    all_to_all x3, starting transfers between devices, shards(): lax.all_to_all(scaled.reshape(groups, width, width), AXIS, 0, 0, axis_ind...  20.4 us
    convert_element_type x3, other arithmetic, assemble(): return total.astype(jnp.bfloat16).reshape(-1, width)  11.4 us
  transfers between devices with their start and end apart: 62, of which 31 were waited for; matrix products, arithmetic and copies ran while one was open for 7% of the time, Pallas kernels for 3%

profile of v7, /device:TPU:1, one launch (start us, length us, event | category | flops | bytes accessed | tf_op | source)
XLA Modules:
  0.0 394.5 jit_solution(17121810287569795612)
XLA Ops:
  0.7 5.4 %convolution_convert_fusion = bf16[16384,128]{1,0:T(8,128)(2,1)} fusion(bf16[16384,128]{1,0:T(8,128)(2,1)} %param.16, bf16[128,128]{1,0:T(8,128)(2,1)} %param.20), kind=kOutput, calls=%fused_computation | convolution fusion | flops 538968064 | bytes 8421376 | tf_op jit(solution)/shard_map/dot_general | solution.py:271
  11.8 5.9 %all-to-all-start = ((bf16[16,128,128]{2,1,0:T(8,128)(2,1)}), bf16[16,128,128]{2,1,0:T(8,128)(2,1)S(1)}, u32[]{:S(2)}, u32[]{:S(2)}) async-start(bf16[16,128,128]{2,1,0:T(8,128)(2,1)} %bitcast.7), calls=%async_computation | async-start | bytes 1048576 | tf_op jit(solution)/shard_map/all_to_all | solution.py:324
  22.2 5.4 %all-to-all-done = bf16[16,128,128]{2,1,0:T(8,128)(2,1)S(1)} async-done(((bf16[16,128,128]{2,1,0:T(8,128)(2,1)}), bf16[16,128,128]{2,1,0:T(8,128)(2,1)S(1)}, u32[]{:S(2)}, u32[]{:S(2)}) %all-to-all-start) | async-done | bytes 524320 | tf_op jit(solution)/shard_map/all_to_all | solution.py:324
  47.6 4.3 %shard_map.156 = (f32[2048,128]{1,0:T(8,128)}, bf16[2048,128]{1,0:T(8,128)(2,1)S(1)}) custom-call(s32[6]{0:T(128)S(1)} %stack.69.info, bf16[2048,128]{1,0:T(8,128)(2,1)S(1)} %copy-done.4, bf16[2048,128]{1,0:T(8,128)(2,1)S(1)} %copy-done.4, bf16[2,128,256]{2,1,0:T(8,128)(2,1)S(1)} %pad_maximum_fusion.6.refs_0_, ...), custom_call_target="tpu_custom_call" | custom-call | flops 201326592 | bytes 3145728 | tf_op jit(solution)/shard_map/pallas_call | solution.py:205
  70.5 8.5 %collective-permute-done.9 = bf16[16,128,128]{2,1,0:T(8,128)(2,1)S(1)} collective-permute-done((bf16[16,128,128]{2,1,0:T(8,128)(2,1)S(1)}, bf16[16,128,128]{2,1,0:T(8,128)(2,1)S(1)}, u32[]{:S(2)}, u32[]{:S(2)}) %collective-permute-start.9) | collective-permute-done | bytes 524320 | tf_op jit(solution)/shard_map/ppermute | solution.py:15
  91.2 5.2 %all-to-all-start.1 = ((bf16[32,128,128]{2,1,0:T(8,128)(2,1)}), bf16[32,128,128]{2,1,0:T(8,128)(2,1)S(1)}, u32[]{:S(2)}, u32[]{:S(2)}) async-start(bf16[32,128,128]{2,1,0:T(8,128)(2,1)} %bitcast.39), calls=%async_computation.1 | async-start | bytes 2097152 | tf_op jit(solution)/shard_map/all_to_all | solution.py:324
  100.9 12.7 %all-to-all-done.1 = bf16[32,128,128]{2,1,0:T(8,128)(2,1)S(1)} async-done(((bf16[32,128,128]{2,1,0:T(8,128)(2,1)}), bf16[32,128,128]{2,1,0:T(8,128)(2,1)S(1)}, u32[]{:S(2)}, u32[]{:S(2)}) %all-to-all-start.1) | async-done | bytes 1048608 | tf_op jit(solution)/shard_map/all_to_all | solution.py:324
  142.5 4.3 %shard_map.157 = (f32[4096,128]{1,0:T(8,128)}, bf16[4096,128]{1,0:T(8,128)(2,1)S(1)}) custom-call(s32[6]{0:T(128)S(1)} %stack.72.info, bf16[4096,128]{1,0:T(8,128)(2,1)S(1)} %fusion.8.column_any.column_ref, bf16[4096,128]{1,0:T(8,128)(2,1)S(1)} %fusion.8.column_any.column_ref, bf16[4,128,256]{2,1,0:T(8,128)(2,1)S(1)} %pad_maximum_fusion.4.refs_0_, ...), custom_call_target="tpu_custom_call" | custom-call | flops 402653184 | bytes 6291456 | tf_op jit(solution)/shard_map/pallas_call | solution.py:205
  166.2 14.3 %collective-permute-done.23 = bf16[32,128,128]{2,1,0:T(8,128)(2,1)S(1)} collective-permute-done((bf16[32,128,128]{2,1,0:T(8,128)(2,1)S(1)}, bf16[32,128,128]{2,1,0:T(8,128)(2,1)S(1)}, u32[]{:S(2)}, u32[]{:S(2)}) %collective-permute-start.23) | collective-permute-done | bytes 1048608 | tf_op jit(solution)/shard_map/ppermute | solution.py:15
  185.7 9.4 %all-to-all-start.2 = ((bf16[64,128,128]{2,1,0:T(8,128)(2,1)}), bf16[64,128,128]{2,1,0:T(8,128)(2,1)}, u32[]{:S(2)}, u32[]{:S(2)}) async-start(bf16[64,128,128]{2,1,0:T(8,128)(2,1)} %bitcast.204), calls=%async_computation.2 | async-start | bytes 4194304 | tf_op jit(solution)/shard_map/all_to_all | solution.py:324
  199.7 23.5 %all-to-all-done.2 = bf16[64,128,128]{2,1,0:T(8,128)(2,1)} async-done(((bf16[64,128,128]{2,1,0:T(8,128)(2,1)}), bf16[64,128,128]{2,1,0:T(8,128)(2,1)}, u32[]{:S(2)}, u32[]{:S(2)}) %all-to-all-start.2) | async-done | bytes 2097184 | tf_op jit(solution)/shard_map/all_to_all | solution.py:324
  252.1 3.9 collective-permute-start.40
  261.9 8.7 %shard_map.158 = (f32[8192,128]{1,0:T(8,128)}, bf16[8192,128]{1,0:T(8,128)(2,1)S(1)}) custom-call(s32[6]{0:T(128)S(1)} %stack.78.info, bf16[8192,128]{1,0:T(8,128)(2,1)S(1)} %fusion.4.column_any.column_ref, bf16[8192,128]{1,0:T(8,128)(2,1)S(1)} %fusion.4.column_any.column_ref, bf16[8,128,256]{2,1,0:T(8,128)(2,1)S(1)} %pad_maximum_fusion.3.refs_0_, ...), custom_call_target="tpu_custom_call" | custom-call | flops 805306368 | bytes 12582912 | tf_op jit(solution)/shard_map/pallas_call | solution.py:205
  272.7 5.8 %all-to-all-start.3 = ((bf16[64,128,128]{2,1,0:T(8,128)(2,1)}), bf16[64,128,128]{2,1,0:T(8,128)(2,1)}, u32[]{:S(2)}, u32[]{:S(2)}) async-start(bf16[64,128,128]{2,1,0:T(8,128)(2,1)} %bitcast.205), calls=%async_computation.3 | async-start | bytes 4194304 | tf_op jit(solution)/shard_map/all_to_all | solution.py:361
  281.6 24.9 %all-to-all-done.3 = bf16[64,128,128]{2,1,0:T(8,128)(2,1)} async-done(((bf16[64,128,128]{2,1,0:T(8,128)(2,1)}), bf16[64,128,128]{2,1,0:T(8,128)(2,1)}, u32[]{:S(2)}, u32[]{:S(2)}) %all-to-all-start.3) | async-done | bytes 2097184 | tf_op jit(solution)/shard_map/all_to_all | solution.py:361
  308.2 3.7 collective-permute-done.42
  329.8 5.2 %collective-permute-done.49 = bf16[24,128,128]{2,1,0:T(8,128)(2,1)S(1)} collective-permute-done((bf16[24,128,128]{2,1,0:T(8,128)(2,1)S(1)}, bf16[24,128,128]{2,1,0:T(8,128)(2,1)S(1)}, u32[]{:S(2)}, u32[]{:S(2)}) %collective-permute-start.49) | collective-permute-done | bytes 786464 | tf_op jit(solution)/shard_map/ppermute | solution.py:15
  341.4 4.7 %collective-permute-start.54 = (bf16[16,128,256]{2,1,0:T(8,128)(2,1)S(1)}, bf16[16,128,256]{2,1,0:T(8,128)(2,1)}, u32[]{:S(2)}, u32[]{:S(2)}) collective-permute-start(bf16[16,128,256]{2,1,0:T(8,128)(2,1)S(1)} %pad_maximum_fusion.2.refs_0_), channel_id=1, source_target_pairs={{0,1},{1,0},{2,3},{3,2},{4,5},{5,4},{6,7},{7,6},{8,9},{9,8},{10,11... | collective-permute-start | bytes 3145736 | tf_op jit(solution)/shard_map/ppermute | solution.py:15
  346.1 3.7 collective-permute-done.51.refs_1_
  349.8 4.3 %collective-permute-start.55 = (bf16[16,128,256]{2,1,0:T(8,128)(2,1)}, bf16[16,128,256]{2,1,0:T(8,128)(2,1)}, u32[]{:S(2)}, u32[]{:S(2)}) collective-permute-start(bf16[16,128,256]{2,1,0:T(8,128)(2,1)} %collective-permute-done.51.refs_1_), channel_id=1, source_target_pairs={{0,1},{1,0},{2,3},{3,2},{4,5},{5,4},{6,7},{7,6},{8,9},{9,8},{10,11... | collective-permute-start | bytes 3145736 | tf_op jit(solution)/shard_map/ppermute | solution.py:15
  356.6 7.4 %collective-permute-done.53.refs_3_ = bf16[16,128,256]{2,1,0:T(8,128)(2,1)} collective-permute-done((bf16[16,128,256]{2,1,0:T(8,128)(2,1)S(1)}, bf16[16,128,256]{2,1,0:T(8,128)(2,1)}, u32[]{:S(2)}, u32[]{:S(2)}) %collective-permute-start.53) | collective-permute-done | bytes 1048608 | tf_op jit(solution)/shard_map/ppermute | solution.py:15
  364.0 3.7 collective-permute-start.57
  373.6 5.7 %fusion.1.column_any.column_ref = bf16[16384,128]{1,0:T(8,128)(2,1)S(1)} fusion(bf16[16384,128]{1,0:T(8,128)(2,1)S(1)} %copy-done.11, f32[64,128,128]{2,1,0:T(8,128)S(1)} %maximum_convert_fusion, f32[64,128,128]{2,1,0:T(8,128)S(1)} %convert.1, pred[16384]{0:T(1024)(128)(4,1)S(1)} %bitcast.207, pred[16384]{0:T(1024)(128)(4,1)S(1)} %bitcast.208), kind=kLoop, calls=%fused_computation.5 | loop fusion | flops 12582912 | bytes 16809984 | tf_op jit(solution)/shard_map/convert_element_type | solution.py:392
  379.4 15.0 %shard_map.159 = f32[16384,128]{1,0:T(8,128)} custom-call(s32[6]{0:T(128)S(1)} %stack.82.info, bf16[16384,128]{1,0:T(8,128)(2,1)S(1)} %fusion.1.column_any.column_ref, bf16[16384,128]{1,0:T(8,128)(2,1)S(1)} %fusion.1.column_any.column_ref, bf16[16,128,256]{2,1,0:T(8,128)(2,1)S(1)} %pad_maximum_fusion.2.refs_0_, ...), custom_call_target="tpu_custom_call" | custom-call | flops 1610612736 | bytes 25165824 | tf_op jit(solution)/shard_map/pallas_call | solution.py:205
  (229 shorter events, 165.2 us)
Async XLA Ops:
  9.3 42.6 %collective-permute-start.8 = (bf16[4,4,4,128,128]{4,3,2,1,0:T(8,128)(2,1)}, bf16[4,4,4,128,128]{4,3,2,1,0:T(8,128)(2,1)}, u32[]{:S(2)}, u32[]{:S(2)}) collective-permute-start(bf16[4,4,4,128,128]{4,3,2,1,0:T(8,128)(2,1)} %dynamic-slice_bitcast_fusion), channel_id=1, source_target_pairs={{0,1},{1,0},{2,3},{3,2},{4,5},{5,4},{6,7},{7,6},{8,9},{9,8},{10,11... | collective-permute-start | bytes 6291464 | tf_op jit(solution)/shard_map/ppermute | solution.py:15
  11.8 15.8 %all-to-all-start = ((bf16[16,128,128]{2,1,0:T(8,128)(2,1)}), bf16[16,128,128]{2,1,0:T(8,128)(2,1)S(1)}, u32[]{:S(2)}, u32[]{:S(2)}) async-start(bf16[16,128,128]{2,1,0:T(8,128)(2,1)} %bitcast.7), calls=%async_computation | async-start | bytes 1048576 | tf_op jit(solution)/shard_map/all_to_all | solution.py:324
  33.5 14.2 %collective-permute-start.4 = (bf16[2,128,256]{2,1,0:T(8,128)(2,1)S(1)}, bf16[2,128,256]{2,1,0:T(8,128)(2,1)S(1)}, u32[]{:S(2)}, u32[]{:S(2)}) collective-permute-start(bf16[2,128,256]{2,1,0:T(8,128)(2,1)S(1)} %pad_maximum_fusion.6.refs_0_), channel_id=1, source_target_pairs={{0,1},{1,0},{2,3},{3,2},{4,5},{5,4},{6,7},{7,6},{8,9},{9,8},{10,11... | collective-permute-start | bytes 393224 | tf_op jit(solution)/shard_map/ppermute | solution.py:15
  58.7 26.0 %collective-permute-start.12 = (bf16[4,4,2,128,128]{4,3,2,1,0:T(8,128)(2,1)}, bf16[4,4,2,128,128]{4,3,2,1,0:T(8,128)(2,1)}, u32[]{:S(2)}, u32[]{:S(2)}) collective-permute-start(bf16[4,4,2,128,128]{4,3,2,1,0:T(8,128)(2,1)} %get-tuple-element.35), channel_id=1, source_target_pairs={{0,6},{1,97},{2,0},{3,99},{4,2},{5,101},{6,4},{7,103},{8,14},{9,10... | collective-permute-start | bytes 3145736 | tf_op jit(solution)/shard_map/ppermute | solution.py:15
  61.4 23.3 %collective-permute-start.11 = (bf16[4,4,2,128,128]{4,3,2,1,0:T(8,128)(2,1)}, bf16[4,4,2,128,128]{4,3,2,1,0:T(8,128)(2,1)}, u32[]{:S(2)}, u32[]{:S(2)}) collective-permute-start(bf16[4,4,2,128,128]{4,3,2,1,0:T(8,128)(2,1)} %get-tuple-element.34), channel_id=1, source_target_pairs={{0,4},{1,65},{2,6},{3,67},{4,0},{5,69},{6,2},{7,71},{8,12},{9,73},... | collective-permute-start | bytes 3145736 | tf_op jit(solution)/shard_map/ppermute | solution.py:15
  61.8 26.4 %collective-permute-start.10 = (bf16[4,4,2,128,128]{4,3,2,1,0:T(8,128)(2,1)}, bf16[4,4,2,128,128]{4,3,2,1,0:T(8,128)(2,1)}, u32[]{:S(2)}, u32[]{:S(2)}) collective-permute-start(bf16[4,4,2,128,128]{4,3,2,1,0:T(8,128)(2,1)} %get-tuple-element.33), channel_id=1, source_target_pairs={{0,2},{1,33},{2,4},{3,35},{4,6},{5,37},{6,0},{7,39},{8,10},{9,41},... | collective-permute-start | bytes 3145736 | tf_op jit(solution)/shard_map/ppermute | solution.py:15
  91.2 22.4 %all-to-all-start.1 = ((bf16[32,128,128]{2,1,0:T(8,128)(2,1)}), bf16[32,128,128]{2,1,0:T(8,128)(2,1)S(1)}, u32[]{:S(2)}, u32[]{:S(2)}) async-start(bf16[32,128,128]{2,1,0:T(8,128)(2,1)} %bitcast.39), calls=%async_computation.1 | async-start | bytes 2097152 | tf_op jit(solution)/shard_map/all_to_all | solution.py:324
  122.0 15.5 %collective-permute-start.19 = (bf16[4,128,256]{2,1,0:T(8,128)(2,1)S(1)}, bf16[4,128,256]{2,1,0:T(8,128)(2,1)S(1)}, u32[]{:S(2)}, u32[]{:S(2)}) collective-permute-start(bf16[4,128,256]{2,1,0:T(8,128)(2,1)S(1)} %pad_maximum_fusion.4.refs_0_), channel_id=1, source_target_pairs={{0,1},{1,0},{2,3},{3,2},{4,5},{5,4},{6,7},{7,6},{8,9},{9,8},{10,11... | collective-permute-start | bytes 786440 | tf_op jit(solution)/shard_map/ppermute | solution.py:15
  156.7 23.8 %collective-permute-start.23 = (bf16[32,128,128]{2,1,0:T(8,128)(2,1)S(1)}, bf16[32,128,128]{2,1,0:T(8,128)(2,1)S(1)}, u32[]{:S(2)}, u32[]{:S(2)}) collective-permute-start(bf16[32,128,128]{2,1,0:T(8,128)(2,1)S(1)} %bitcast.198), channel_id=1, source_target_pairs={{0,32},{1,33},{2,34},{3,35},{4,36},{5,37},{6,38},{7,39},{8,40},{9,... | collective-permute-start | bytes 3145736 | tf_op jit(solution)/shard_map/ppermute | solution.py:15
  185.7 37.5 %all-to-all-start.2 = ((bf16[64,128,128]{2,1,0:T(8,128)(2,1)}), bf16[64,128,128]{2,1,0:T(8,128)(2,1)}, u32[]{:S(2)}, u32[]{:S(2)}) async-start(bf16[64,128,128]{2,1,0:T(8,128)(2,1)} %bitcast.204), calls=%async_computation.2 | async-start | bytes 4194304 | tf_op jit(solution)/shard_map/all_to_all | solution.py:324
  238.1 23.8 %collective-permute-start.37 = (bf16[8,128,256]{2,1,0:T(8,128)(2,1)S(1)}, bf16[8,128,256]{2,1,0:T(8,128)(2,1)}, u32[]{:S(2)}, u32[]{:S(2)}) collective-permute-start(bf16[8,128,256]{2,1,0:T(8,128)(2,1)S(1)} %pad_maximum_fusion.3.refs_0_), channel_id=1, source_target_pairs={{0,1},{1,0},{2,3},{3,2},{4,5},{5,4},{6,7},{7,6},{8,9},{9,8},{10,11... | collective-permute-start | bytes 1572872 | tf_op jit(solution)/shard_map/ppermute | solution.py:15
  243.9 18.0 %collective-permute-start.38 = (bf16[8,128,256]{2,1,0:T(8,128)(2,1)S(1)}, bf16[8,128,256]{2,1,0:T(8,128)(2,1)}, u32[]{:S(2)}, u32[]{:S(2)}) collective-permute-start(bf16[8,128,256]{2,1,0:T(8,128)(2,1)S(1)} %collective-permute-done.34.refs_1_), channel_id=1, source_target_pairs={{0,1},{1,0},{2,3},{3,2},{4,5},{5,4},{6,7},{7,6},{8,9},{9,8},{10,11... | collective-permute-start | bytes 1572872 | tf_op jit(solution)/shard_map/ppermute | solution.py:15
  247.3 14.6 %collective-permute-start.39 = (bf16[8,128,256]{2,1,0:T(8,128)(2,1)}, bf16[8,128,256]{2,1,0:T(8,128)(2,1)}, u32[]{:S(2)}, u32[]{:S(2)}) collective-permute-start(bf16[8,128,256]{2,1,0:T(8,128)(2,1)} %collective-permute-done.35.refs_2_), channel_id=1, source_target_pairs={{0,1},{1,0},{2,3},{3,2},{4,5},{5,4},{6,7},{7,6},{8,9},{9,8},{10,11... | collective-permute-start | bytes 1572872 | tf_op jit(solution)/shard_map/ppermute | solution.py:15
  256.0 14.6 %collective-permute-start.41 = (bf16[128,128]{1,0:T(8,128)(2,1)S(1)}, bf16[128,128]{1,0:T(8,128)(2,1)S(1)}, u32[]{:S(2)}, u32[]{:S(2)}) collective-permute-start(bf16[128,128]{1,0:T(8,128)(2,1)S(1)} %copy-done.15), channel_id=1, source_target_pairs={{0,64},{1,65},{2,66},{3,67},{4,68},{5,69},{6,70},{7,71},{8,72},{9,... | collective-permute-start | bytes 98312 | tf_op jit(solution)/shard_map/ppermute | solution.py:15
  272.7 33.8 %all-to-all-start.3 = ((bf16[64,128,128]{2,1,0:T(8,128)(2,1)}), bf16[64,128,128]{2,1,0:T(8,128)(2,1)}, u32[]{:S(2)}, u32[]{:S(2)}) async-start(bf16[64,128,128]{2,1,0:T(8,128)(2,1)} %bitcast.205), calls=%async_computation.3 | async-start | bytes 4194304 | tf_op jit(solution)/shard_map/all_to_all | solution.py:361
  317.7 17.4 %collective-permute-start.49 = (bf16[24,128,128]{2,1,0:T(8,128)(2,1)S(1)}, bf16[24,128,128]{2,1,0:T(8,128)(2,1)S(1)}, u32[]{:S(2)}, u32[]{:S(2)}) collective-permute-start(bf16[24,128,128]{2,1,0:T(8,128)(2,1)S(1)} %bitcast.206), channel_id=1, source_target_pairs={{0,64},{1,65},{2,66},{3,67},{4,68},{5,69},{6,70},{7,71},{8,72},{9,... | collective-permute-start | bytes 2359304 | tf_op jit(solution)/shard_map/ppermute | solution.py:15
  335.0 14.7 %collective-permute-start.51 = (bf16[16,128,256]{2,1,0:T(8,128)(2,1)S(1)}, bf16[16,128,256]{2,1,0:T(8,128)(2,1)}, u32[]{:S(2)}, u32[]{:S(2)}) collective-permute-start(bf16[16,128,256]{2,1,0:T(8,128)(2,1)S(1)} %pad_maximum_fusion.2.refs_0_), channel_id=1, source_target_pairs={{8,0},{3,1},{10,2},{5,3},{12,4},{7,5},{14,6},{1,7},{16,8},{11,9},{... | collective-permute-start | bytes 3145736 | tf_op jit(solution)/shard_map/ppermute | solution.py:15
  337.2 16.9 %collective-permute-start.52 = (bf16[16,128,256]{2,1,0:T(8,128)(2,1)S(1)}, bf16[16,128,256]{2,1,0:T(8,128)(2,1)}, u32[]{:S(2)}, u32[]{:S(2)}) collective-permute-start(bf16[16,128,256]{2,1,0:T(8,128)(2,1)S(1)} %pad_maximum_fusion.2.refs_0_), channel_id=1, source_target_pairs={{16,0},{5,1},{18,2},{7,3},{20,4},{1,5},{22,6},{3,7},{24,8},{13,9},... | collective-permute-start | bytes 3145736 | tf_op jit(solution)/shard_map/ppermute | solution.py:15
  339.0 25.0 %collective-permute-start.53 = (bf16[16,128,256]{2,1,0:T(8,128)(2,1)S(1)}, bf16[16,128,256]{2,1,0:T(8,128)(2,1)}, u32[]{:S(2)}, u32[]{:S(2)}) collective-permute-start(bf16[16,128,256]{2,1,0:T(8,128)(2,1)S(1)} %pad_maximum_fusion.2.refs_0_), channel_id=1, source_target_pairs={{24,0},{7,1},{26,2},{1,3},{28,4},{3,5},{30,6},{5,7},{0,8},{15,9},{... | collective-permute-start | bytes 3145736 | tf_op jit(solution)/shard_map/ppermute | solution.py:15
  339.0 32.0 %collective-permute-start.50 = (bf16[40,128,128]{2,1,0:T(8,128)(2,1)}, bf16[40,128,128]{2,1,0:T(8,128)(2,1)}, u32[]{:S(2)}, u32[]{:S(2)}) collective-permute-start(bf16[40,128,128]{2,1,0:T(8,128)(2,1)} %bitcast.90), channel_id=1, source_target_pairs={{0,64},{1,65},{2,66},{3,67},{4,68},{5,69},{6,70},{7,71},{8,72},{9,... | collective-permute-start | bytes 3932168 | tf_op jit(solution)/shard_map/ppermute | solution.py:15
  341.4 37.9 %collective-permute-start.54 = (bf16[16,128,256]{2,1,0:T(8,128)(2,1)S(1)}, bf16[16,128,256]{2,1,0:T(8,128)(2,1)}, u32[]{:S(2)}, u32[]{:S(2)}) collective-permute-start(bf16[16,128,256]{2,1,0:T(8,128)(2,1)S(1)} %pad_maximum_fusion.2.refs_0_), channel_id=1, source_target_pairs={{0,1},{1,0},{2,3},{3,2},{4,5},{5,4},{6,7},{7,6},{8,9},{9,8},{10,11... | collective-permute-start | bytes 3145736 | tf_op jit(solution)/shard_map/ppermute | solution.py:15
  349.8 29.6 %collective-permute-start.55 = (bf16[16,128,256]{2,1,0:T(8,128)(2,1)}, bf16[16,128,256]{2,1,0:T(8,128)(2,1)}, u32[]{:S(2)}, u32[]{:S(2)}) collective-permute-start(bf16[16,128,256]{2,1,0:T(8,128)(2,1)} %collective-permute-done.51.refs_1_), channel_id=1, source_target_pairs={{0,1},{1,0},{2,3},{3,2},{4,5},{5,4},{6,7},{7,6},{8,9},{9,8},{10,11... | collective-permute-start | bytes 3145736 | tf_op jit(solution)/shard_map/ppermute | solution.py:15
  354.1 25.2 %collective-permute-start.56 = (bf16[16,128,256]{2,1,0:T(8,128)(2,1)}, bf16[16,128,256]{2,1,0:T(8,128)(2,1)}, u32[]{:S(2)}, u32[]{:S(2)}) collective-permute-start(bf16[16,128,256]{2,1,0:T(8,128)(2,1)} %collective-permute-done.52.refs_2_), channel_id=1, source_target_pairs={{0,1},{1,0},{2,3},{3,2},{4,5},{5,4},{6,7},{7,6},{8,9},{9,8},{10,11... | collective-permute-start | bytes 3145736 | tf_op jit(solution)/shard_map/ppermute | solution.py:15
  364.0 15.4 %collective-permute-start.57 = (bf16[16,128,256]{2,1,0:T(8,128)(2,1)}, bf16[16,128,256]{2,1,0:T(8,128)(2,1)}, u32[]{:S(2)}, u32[]{:S(2)}) collective-permute-start(bf16[16,128,256]{2,1,0:T(8,128)(2,1)} %collective-permute-done.53.refs_3_), channel_id=1, source_target_pairs={{0,1},{1,0},{2,3},{3,2},{4,5},{5,4},{6,7},{7,6},{8,9},{9,8},{10,11... | collective-permute-start | bytes 3145736 | tf_op jit(solution)/shard_map/ppermute | solution.py:15
  (61 other events, 718.4 us)
